TPU v7x, 512 devices: a whole 4x8x8 slice. The times are simulated.
512 devices in a mesh: gx: 32 (over y, z_lo, core), gy: 16 (over z_hi, x).
Axes of the slice: x: 4, y: 8, z: 8 (z_hi: 4, z_lo: 2; z = z_hi * 2 + z_lo), core: 2. Of those that a mesh axis runs over, the one named last changes fastest.
Arguments:
- strain: float32 [5, 128, 256, 128], P(None, 'gx', 'gy'), may hold values from 0.0025 to 1
- coords: float32 [3, 128, 256, 128], P(None, 'gx', 'gy'), may hold values from -2 to 2560
- displacement: float32 [3, 128, 256, 128], P(None, 'gx', 'gy'), may hold values from -6 to 6
- stiffness: float32 [1, 128, 256, 128], P(None, 'gx', 'gy'), may hold values from 1 to 60
- neighbours: int32 [9, 128, 256], P(None, 'gx', 'gy'), may hold values from -1 to 32767, as said below
- corners: int32 [4, 128, 256, 128], P(None, 'gx', 'gy'), may hold values from 0 to 1151
Outputs:
- damage: float32 [5, 128, 256, 128], P(None, 'gx', 'gy')
- nodal_force: float32 [3, 128, 256, 128], P(None, 'gx', 'gy')
Inputs may be any that keep to these rules, and one draw needn't show every extreme that they name: `neighbours`: slot 0 names the tile itself; slot k of 1 to 8 names the tile at the k-th of the row and column offsets (-1,-1), (-1,0), (-1,1), (0,-1), (0,1), (1,-1), (1,0), (1,1), or holds -1: always where that tile lies outside the grid, and for some links inside it.
All inputs are finite; a program needn't handle non-finite values.
Results may differ from a plain program's by a relative error of at most 0.0008.
Values may be sent and summed in bfloat16 or wider, within the bound.
No kernel may reach another device: no remote copies, remote signals or barrier semaphores. Data moves between devices by JAX's collectives and lax.ppermute only.
A program may use at most 64 MiB of HBM per device.

v0:
```python
import jax
import jax.numpy as jnp
from jax import lax
from jax.sharding import PartitionSpec as P

RADIUS_INV_SQ = 0.01
STRAIN_SCALE = 0.05
SLOT_ROWS = (0, -1, -1, -1, 0, 0, 1, 1, 1)
SLOT_COLS = (0, -1, 0, 1, -1, 1, -1, 0, 1)


def extended(value, sides, width):
    for axis, dim in sides:
        peers, length = (lax.axis_size(axis), value.shape[dim])
        up = [(i, (i + 1) % peers) for i in range(peers - 1)]
        down = [(j, i) for i, j in up]
        last = lax.slice_in_dim(value, length - width, length, axis=dim)
        leading = lax.slice_in_dim(value, 0, width, axis=dim)
        before = lax.ppermute(last, axis, up)
        after = lax.ppermute(leading, axis, down)
        value = jnp.concatenate([before, value, after], axis=dim)
    return value


def pair_weights(own_xyz, other_xyz, live_mask):
    dist_sq = (own_xyz[0][:, :, None, :] - other_xyz[0][:, :, :, None]) ** 2
    dist_sq = dist_sq + (own_xyz[1][:, :, None, :] - other_xyz[1][:, :, :, None]) ** 2
    dist_sq = dist_sq + (own_xyz[2][:, :, None, :] - other_xyz[2][:, :, :, None]) ** 2
    bell_curve = jnp.maximum(1.0 - dist_sq * RADIUS_INV_SQ, 0.0)
    return jnp.where(live_mask[:, :, None, None], bell_curve * bell_curve, 0.0).astype(jnp.bfloat16)


def make_source(strain_low):
    ones_layer = jnp.ones((1,) + strain_low.shape[1:], jnp.bfloat16)
    return jnp.concatenate([strain_low, ones_layer], axis=0)


def damage_block(source, coords_src, lists_region, margin, row_start, col_start):
    row_count = lists_region.shape[1]
    col_count = lists_region.shape[2]
    channels = source.shape[0]
    points = source.shape[3]
    base_row = row_start + margin
    base_col = col_start + margin
    own_xyz = coords_src[:, base_row : base_row + row_count, base_col : base_col + col_count]
    running = jnp.zeros((channels, row_count, col_count, points), jnp.float32)
    for slot_index in range(lists_region.shape[0]):
        low_row = base_row + SLOT_ROWS[slot_index]
        low_col = base_col + SLOT_COLS[slot_index]
        other_xyz = coords_src[:, low_row : low_row + row_count, low_col : low_col + col_count]
        values = source[:, low_row : low_row + row_count, low_col : low_col + col_count]
        weights = pair_weights(own_xyz, other_xyz, lists_region[slot_index] >= 0)
        running = running + jnp.einsum(
            "lrcq,rcqp->lrcp", values, weights, preferred_element_type=jnp.float32
        )
    weight_sum = running[channels - 1 :]
    averaged = running[: channels - 1] / jnp.where(weight_sum > 0, weight_sum, 1.0)
    return averaged / (averaged + STRAIN_SCALE)


def all_damage(extra, ext_source, ext_coords, ext_margin, lists_all):
    return damage_block(ext_source, ext_coords, lists_all, ext_margin, -extra, -extra)


def shell_forces(damage, stiff_region, codes, disp_pad, start, inside):
    row_count = damage.shape[1]
    col_count = damage.shape[2]
    points = damage.shape[3]
    strength = jnp.where(inside[:, :, None], (1.0 - jnp.mean(damage, axis=0)) * stiff_region, 0.0)
    offset = codes // points
    slot_of = codes % points
    node_iota = jnp.arange(points, dtype=jnp.int32)
    one_hot = [(slot_of[corner][..., None] == node_iota).astype(jnp.float32) for corner in range(4)]

    def window(offset_code):
        low_row = start + offset_code // 3 - 1
        low_col = start + offset_code % 3 - 1
        return (low_row, low_col)

    corner_disp = []
    for corner in range(4):
        picked = jnp.zeros((3, row_count, col_count, points), jnp.float32)
        for offset_code in range(9):
            low_row, low_col = window(offset_code)
            shifted = disp_pad[:, low_row : low_row + row_count, low_col : low_col + col_count]
            taken = jnp.einsum(
                "rcps,xrcs->xrcp", one_hot[corner], shifted, precision=lax.Precision.HIGHEST
            )
            picked = picked + jnp.where((offset[corner] == offset_code)[None], taken, 0.0)
        corner_disp.append(picked)
    springs = [
        strength[None] * (corner_disp[(corner + 1) % 4] - corner_disp[corner])
        for corner in range(4)
    ]
    forces = jnp.zeros(disp_pad.shape, jnp.float32)
    for corner in range(4):
        amount = springs[corner] - springs[(corner + 3) % 4]
        for offset_code in range(9):
            low_row, low_col = window(offset_code)
            masked = jnp.where((offset[corner] == offset_code)[None], amount, 0.0)
            placed = jnp.einsum(
                "rcps,xrcp->xrcs", one_hot[corner], masked, precision=lax.Precision.HIGHEST
            )
            forces = forces.at[:, low_row : low_row + row_count, low_col : low_col + col_count].add(
                placed
            )
    return forces


def local(strain, coords, displacement, stiffness, neighbours, corners):
    tiles_x = strain.shape[1]
    tiles_y = strain.shape[2]
    strain_low = strain.astype(jnp.bfloat16)
    coords_ext, disp_ext = (
        extended(coords, (("gx", 1), ("gy", 2)), 1),
        extended(displacement, (("gx", 1), ("gy", 2)), 1),
    )
    strain_ext = extended(strain_low, (("gx", 1), ("gy", 2)), 1)
    damage = all_damage(0, make_source(strain_ext), coords_ext, 1, neighbours)
    inside = jnp.ones((tiles_x, tiles_y), jnp.bool_)
    nodal_sum = shell_forces(damage, stiffness[0], corners, disp_ext, 1, inside)
    side_rims = jnp.concatenate(
        [nodal_sum[:, 0:1], nodal_sum[:, tiles_x + 1 : tiles_x + 2]], axis=1
    )
    arrived = extended(side_rims.astype(jnp.bfloat16), (("gx", 1),), 1).astype(side_rims.dtype)
    nodal_sum = nodal_sum.at[:, 1].add(arrived[:, 0]).at[:, tiles_x].add(arrived[:, 3])
    interior = nodal_sum[:, 1 : tiles_x + 1]
    side_rims = jnp.concatenate(
        [interior[:, :, 0:1], interior[:, :, tiles_y + 1 : tiles_y + 2]], axis=2
    )
    arrived = extended(side_rims, (("gy", 2),), 1)
    interior = interior.at[:, :, 1].add(arrived[:, :, 0]).at[:, :, tiles_y].add(arrived[:, :, 3])
    forces = interior[:, :, 1 : tiles_y + 1]
    local_peak = jnp.max((1.0 - jnp.mean(damage, axis=0)) * stiffness[0])
    top = lax.pmax(local_peak, ("gx", "gy"))
    return (damage, forces / top)


def solution(mesh):
    in_specs = (
        P(None, "gx", "gy", None),
        P(None, "gx", "gy", None),
        P(None, "gx", "gy", None),
        P(None, "gx", "gy", None),
        P(None, "gx", "gy"),
        P(None, "gx", "gy", None),
    )
    out_specs = (P(None, "gx", "gy", None), P(None, "gx", "gy", None))
    return jax.shard_map(local, mesh=mesh, in_specs=in_specs, out_specs=out_specs, check_vma=False)
```

profile of v0, /device:TPU:6, one launch (start us, length us, event | category | flops | bytes accessed | tf_op | source)
XLA Modules:
  0.0 486.5 jit_solution(11767508189314714054)
XLA Ops:
  7.1 5.8 %collective-permute-start = (bf16[5,1,16,128]{3,0,2,1:T(8,128)(2,1)S(1)}, bf16[5,1,16,128]{3,0,2,1:T(8,128)(2,1)S(1)}, u32[]{:S(2)}, u32[]{:S(2)}) collective-permute-start(bf16[5,1,16,128]{3,0,2,1:T(8,128)(2,1)S(1)} %get-tuple-element.558), channel_id=1, source_target_pairs={{0,16},{16,32},{32,48},{48,64},{64,80},{80,96},{96,112},{112,128},... | collective-permute-start | bytes 61448 | tf_op jit(solution)/shard_map/ppermute | solution.py:19
  13.0 3.6 collective-permute-start.8
  23.6 6.1 %collective-permute-start.2 = (bf16[5,6,1,128]{3,0,2,1:T(8,128)(2,1)S(1)}, bf16[5,6,1,128]{3,0,2,1:T(8,128)(2,1)S(1)}, u32[]{:S(2)}, u32[]{:S(2)}) collective-permute-start(bf16[5,6,1,128]{3,0,2,1:T(8,128)(2,1)S(1)} %get-tuple-element.494), channel_id=1, source_target_pairs={{0,1},{1,2},{2,3},{3,4},{4,5},{5,6},{6,7},{7,8},{8,9},{9,10},{10,1... | collective-permute-start | bytes 23048 | tf_op jit(solution)/shard_map/ppermute | solution.py:19
  31.8 6.9 %collective-permute-start.6 = (f32[3,6,1,128]{3,2,1,0:T(1,128)S(1)}, f32[3,6,1,128]{3,2,1,0:T(1,128)S(1)}, u32[]{:S(2)}, u32[]{:S(2)}) collective-permute-start(f32[3,6,1,128]{3,2,1,0:T(1,128)S(1)} %get-tuple-element.514), channel_id=1, source_target_pairs={{0,1},{1,2},{2,3},{3,4},{4,5},{5,6},{6,7},{7,8},{8,9},{9,10},{10,1... | collective-permute-start | bytes 27656 | tf_op jit(solution)/shard_map/ppermute | solution.py:19
  40.8 4.0 fusion.235
  44.8 4.0 fusion.268
  48.8 4.0 fusion.171
  52.8 4.0 fusion.204
  56.8 6.9 %collective-permute-start.10 = (f32[3,6,1,128]{3,0,2,1:T(4,128)S(1)}, f32[3,6,1,128]{3,0,2,1:T(4,128)S(1)}, u32[]{:S(2)}, u32[]{:S(2)}) collective-permute-start(f32[3,6,1,128]{3,0,2,1:T(4,128)S(1)} %get-tuple-element.492), channel_id=1, source_target_pairs={{0,1},{1,2},{2,3},{3,4},{4,5},{5,6},{6,7},{7,8},{8,9},{9,10},{10,1... | collective-permute-start | bytes 27656 | tf_op jit(solution)/shard_map/ppermute | solution.py:19
  63.9 6.5 %fusion.151 = f32[4,16,128,6]{2,3,1,0:T(8,128)S(1)} fusion(f32[4,16,128]{2,1,0:T(8,128)S(1)} %get-tuple-element.564, f32[4,16,128]{2,1,0:T(8,128)S(1)} %get-tuple-element.565, f32[4,16,128]{2,1,0:T(8,128)S(1)} %get-tuple-element.563, f32[4,16,128]{2,1,0:T(8,128)S(1)} %get-tuple-element.577, f32[4,16,128]{2,1,0:T(8,128)S(1)} %get-tuple-element.578, ...), kind=kOutput, calls=%fused_computation.164 | convolution fusion | flops 27262976 | bytes 524800 | tf_op jit(solution)/shard_map/lrcq,rcqp->lrcp/dot_general | solution.py:53
  70.4 6.5 %fusion.145 = f32[4,16,128,6]{2,3,1,0:T(8,128)S(1)} fusion(f32[4,16,128]{2,1,0:T(8,128)S(1)} %get-tuple-element.499, f32[4,16,128]{2,1,0:T(8,128)S(1)} %get-tuple-element.498, f32[4,16,128]{2,1,0:T(8,128)S(1)} %get-tuple-element.497, f32[4,16,128]{2,1,0:T(8,128)S(1)} %get-tuple-element.577, f32[4,16,128]{2,1,0:T(8,128)S(1)} %get-tuple-element.578, ...), kind=kOutput, calls=%fused_computation.158 | convolution fusion | flops 27262976 | bytes 524800 | tf_op jit(solution)/shard_map/lrcq,rcqp->lrcp/dot_general | solution.py:53
  76.9 6.5 %fusion.167 = f32[4,16,128,6]{2,3,1,0:T(8,128)S(1)} fusion(f32[4,16,128,6]{2,3,1,0:T(8,128)S(1)} %fusion.145, f32[4,16,128]{2,1,0:T(8,128)S(1)} %get-tuple-element.577, f32[4,16,128]{2,1,0:T(8,128)S(1)} %get-tuple-element.578, f32[4,16,128]{2,1,0:T(8,128)S(1)} %get-tuple-element.576, pred[4,16]{1,0:T(4,128)(4,1)S(1)} %get-tuple-element.595, ...), kind=kOutput, calls=%fused_computation.180 | convolution fusion | flops 27312128 | bytes 786944 | tf_op jit(solution)/shard_map/lrcq,rcqp->lrcp/dot_general | solution.py:53
  83.4 6.5 %fusion.152 = f32[4,16,128,6]{2,3,1,0:T(8,128)S(1)} fusion(f32[4,16,128]{2,1,0:T(8,128)S(1)} %get-tuple-element.512, f32[4,16,128]{2,1,0:T(8,128)S(1)} %get-tuple-element.513, f32[4,16,128]{2,1,0:T(8,128)S(1)} %get-tuple-element.511, f32[4,16,128]{2,1,0:T(8,128)S(1)} %get-tuple-element.577, f32[4,16,128]{2,1,0:T(8,128)S(1)} %get-tuple-element.578, ...), kind=kOutput, calls=%fused_computation.165 | convolution fusion | flops 27262976 | bytes 524800 | tf_op jit(solution)/shard_map/lrcq,rcqp->lrcp/dot_general | solution.py:53
  89.8 6.5 %fusion.166 = f32[4,16,128,6]{2,3,1,0:T(8,128)S(1)} fusion(f32[4,16,128,6]{2,3,1,0:T(8,128)S(1)} %fusion.167, f32[4,16,128]{2,1,0:T(8,128)S(1)} %get-tuple-element.561, f32[4,16,128]{2,1,0:T(8,128)S(1)} %get-tuple-element.562, f32[4,16,128]{2,1,0:T(8,128)S(1)} %get-tuple-element.560, f32[4,16,128]{2,1,0:T(8,128)S(1)} %get-tuple-element.577, ...), kind=kOutput, calls=%fused_computation.179 | convolution fusion | flops 27312128 | bytes 786944 | tf_op jit(solution)/shard_map/lrcq,rcqp->lrcp/dot_general | solution.py:53
  96.3 6.5 %fusion.165 = f32[4,16,128,6]{2,3,1,0:T(8,128)S(1)} fusion(f32[4,16,128,6]{2,3,1,0:T(8,128)S(1)} %fusion.166, f32[4,16,128]{2,1,0:T(8,128)S(1)} %get-tuple-element.508, f32[4,16,128]{2,1,0:T(8,128)S(1)} %get-tuple-element.507, f32[4,16,128]{2,1,0:T(8,128)S(1)} %get-tuple-element.506, f32[4,16,128]{2,1,0:T(8,128)S(1)} %get-tuple-element.577, ...), kind=kOutput, calls=%fused_computation.178 | convolution fusion | flops 27312128 | bytes 786944 | tf_op jit(solution)/shard_map/lrcq,rcqp->lrcp/dot_general | solution.py:53
  102.8 6.5 %fusion.164 = f32[4,16,128,6]{2,3,1,0:T(8,128)S(1)} fusion(f32[4,16,128,6]{2,3,1,0:T(8,128)S(1)} %fusion.165, f32[4,16,128]{2,1,0:T(8,128)S(1)} %get-tuple-element.502, f32[4,16,128]{2,1,0:T(8,128)S(1)} %get-tuple-element.501, f32[4,16,128]{2,1,0:T(8,128)S(1)} %get-tuple-element.500, f32[4,16,128]{2,1,0:T(8,128)S(1)} %get-tuple-element.577, ...), kind=kOutput, calls=%fused_computation.177 | convolution fusion | flops 27312128 | bytes 786944 | tf_op jit(solution)/shard_map/lrcq,rcqp->lrcp/dot_general | solution.py:53
  109.2 6.5 %fusion.163 = f32[4,16,128,6]{2,3,1,0:T(8,128)S(1)} fusion(f32[4,16,128,6]{2,3,1,0:T(8,128)S(1)} %fusion.164, f32[4,16,128]{2,1,0:T(8,128)S(1)} %get-tuple-element.510, f32[4,16,128]{2,1,0:T(8,128)S(1)} %get-tuple-element.509, f32[4,16,128]{2,1,0:T(8,128)S(1)} %get-tuple-element.505, f32[4,16,128]{2,1,0:T(8,128)S(1)} %get-tuple-element.577, ...), kind=kOutput, calls=%fused_computation.176 | convolution fusion | flops 27312128 | bytes 786944 | tf_op jit(solution)/shard_map/lrcq,rcqp->lrcp/dot_general | solution.py:53
  115.7 7.0 %fusion.170 = f32[6,4,16,128]{3,0,2,1:T(8,128)S(1)} fusion(f32[4,16,128,6]{2,3,1,0:T(8,128)S(1)} %fusion.152, f32[4,16,128,6]{2,3,1,0:T(8,128)S(1)} %fusion.151, f32[4,16,128,6]{2,3,1,0:T(8,128)S(1)} %fusion.163, f32[4,16,128]{2,1,0:T(8,128)S(1)} %get-tuple-element.503, f32[4,16,128]{2,1,0:T(8,128)S(1)} %get-tuple-element.504, ...), kind=kOutput, calls=%fused_computation.183 | convolution fusion | flops 27410432 | bytes 1311232 | tf_op jit(solution)/shard_map/lrcq,rcqp->lrcp/dot_general | solution.py:53
  122.8 3.4 fusion.357
  126.4 3.4 fusion.355
  129.9 3.4 fusion.349
  133.4 3.4 fusion.348
  136.9 3.4 fusion.347
  140.3 4.2 fusion.306
  144.6 3.4 fusion.372
  148.0 3.4 fusion.370
  151.5 3.4 fusion.364
  155.0 3.4 fusion.363
  158.5 3.4 fusion.362
  161.9 4.2 fusion.303
  166.2 3.4 fusion.327
  169.7 3.4 fusion.325
  173.2 3.4 fusion.319
  176.6 3.4 fusion.318
  180.1 3.4 fusion.317
  183.5 4.4 fusion.312
  188.0 3.4 fusion.342
  191.5 3.4 fusion.340
  195.0 3.4 fusion.334
  198.5 3.4 fusion.333
  201.9 3.4 fusion.332
  205.4 4.2 fusion.309
  209.6 3.4 fusion.353
  213.0 4.0 fusion.305
  217.1 3.4 fusion.368
  220.5 4.0 fusion.302
  224.6 3.4 fusion.323
  228.0 4.0 fusion.311
  232.1 3.4 fusion.338
  235.5 4.0 fusion.541
  239.5 3.1 fusion.209
  242.7 4.3 fusion.212
  247.0 4.8 fusion.216
  269.5 3.0 fusion.178
  272.5 4.3 fusion.181
  276.7 4.8 fusion.185
  281.5 3.0 fusion.188
  302.3 4.3 fusion.278
  306.5 5.0 %fusion.282 = f32[3,6,18,128]{3,0,2,1:T(4,128)S(1)} fusion(f32[3,6,18,128]{3,0,2,1:T(4,128)S(1)} %fusion.278, s32[]{:T(128)} %bitcast.92, s32[]{:T(128)} %bitcast.93, s32[4,16,128]{2,1,0:T(8,128)S(1)} %get-tuple-element.552, f32[3,4,16,128]{3,0,2,1:T(4,128)S(1)} %get-tuple-element.487, pred[4,16,128]{2,1,0:T(8,128)(4,1)S(1)} %get-tuple-element.543, ...), kind=kOutput, calls=%fused_computation.295 | convolution fusion | flops 38871040 | bytes 434185 | tf_op jit(solution)/shard_map/rcps,xrcp->xrcs/dot_general | solution.py:101
  332.3 4.3 fusion.245
  336.6 4.8 fusion.249
  360.5 3.0 collective-permute-start.12
  367.0 108.4 %pmax.7 = f32[]{:T(128)} all-reduce(f32[]{:T(128)} %fusion.537), channel_id=1, replica_groups=mesh['gx'=32,'gy'=16] {'gx','gy'}, use_global_device_ids=true, to_apply=%region_3.4 | all-reduce | flops 1 | bytes 8 | tf_op jit(solution)/shard_map/pmax | solution.py:135
  478.1 6.6 %collective-permute-done.15 = f32[3,4,1,128]{3,0,2,1:T(4,128)S(1)} collective-permute-done((f32[3,4,1,128]{3,0,2,1:T(4,128)S(1)}, f32[3,4,1,128]{3,0,2,1:T(4,128)S(1)}, u32[]{:S(2)}, u32[]{:S(2)}) %collective-permute-start.15) | collective-permute-done | bytes 6176 | tf_op jit(solution)/shard_map/ppermute | solution.py:20
  (133 shorter events, 101.9 us)
Async XLA Ops:
  0.6 12.3 %copy-start.1 = (f32[3,4,16,128]{3,2,1,0:T(8,128)S(1)}, f32[3,4,16,128]{3,2,1,0:T(8,128)}, u32[]{:S(2)}) copy-start(f32[3,4,16,128]{3,2,1,0:T(8,128)} %param.88) | copy-start | bytes 294916
  1.4 22.1 %collective-permute-start.4 = (f32[3,1,16,128]{3,2,1,0:T(8,128)S(1)}, f32[3,1,16,128]{3,2,1,0:T(8,128)S(1)}, u32[]{:S(2)}, u32[]{:S(2)}) collective-permute-start(f32[3,1,16,128]{3,2,1,0:T(8,128)S(1)} %get-tuple-element.580), channel_id=1, source_target_pairs={{0,16},{16,32},{32,48},{48,64},{64,80},{80,96},{96,112},{112,128},... | collective-permute-start | bytes 73736 | tf_op jit(solution)/shard_map/ppermute | solution.py:19
  3.2 13.5 %copy-start = (f32[3,4,16,128]{3,2,1,0:T(8,128)S(1)}, f32[3,4,16,128]{3,2,1,0:T(8,128)}, u32[]{:S(2)}) copy-start(f32[3,4,16,128]{3,2,1,0:T(8,128)} %param.87) | copy-start | bytes 294916
  3.2 26.6 %collective-permute-start.5 = (f32[3,1,16,128]{3,2,1,0:T(8,128)S(1)}, f32[3,1,16,128]{3,2,1,0:T(8,128)S(1)}, u32[]{:S(2)}, u32[]{:S(2)}) collective-permute-start(f32[3,1,16,128]{3,2,1,0:T(8,128)S(1)} %get-tuple-element.579), channel_id=1, source_target_pairs={{16,0},{32,16},{48,32},{64,48},{80,64},{96,80},{112,96},{128,112},... | collective-permute-start | bytes 73736 | tf_op jit(solution)/shard_map/ppermute | solution.py:20
  5.6 11.0 %copy-start.2 = (s32[4,4,16,128]{3,2,1,0:T(8,128)S(1)}, s32[4,4,16,128]{3,2,1,0:T(8,128)}, u32[]{:S(2)}) copy-start(s32[4,4,16,128]{3,2,1,0:T(8,128)} %param.91) | copy-start | bytes 393220
  5.7 13.8 %collective-permute-start.1 = (bf16[5,1,16,128]{3,0,2,1:T(8,128)(2,1)S(1)}, bf16[5,1,16,128]{3,0,2,1:T(8,128)(2,1)S(1)}, u32[]{:S(2)}, u32[]{:S(2)}) collective-permute-start(bf16[5,1,16,128]{3,0,2,1:T(8,128)(2,1)S(1)} %get-tuple-element.559), channel_id=1, source_target_pairs={{16,0},{32,16},{48,32},{64,48},{80,64},{96,80},{112,96},{128,112},... | collective-permute-start | bytes 61448 | tf_op jit(solution)/shard_map/ppermute | solution.py:20
  7.1 13.7 %collective-permute-start = (bf16[5,1,16,128]{3,0,2,1:T(8,128)(2,1)S(1)}, bf16[5,1,16,128]{3,0,2,1:T(8,128)(2,1)S(1)}, u32[]{:S(2)}, u32[]{:S(2)}) collective-permute-start(bf16[5,1,16,128]{3,0,2,1:T(8,128)(2,1)S(1)} %get-tuple-element.558), channel_id=1, source_target_pairs={{0,16},{16,32},{32,48},{48,64},{64,80},{80,96},{96,112},{112,128},... | collective-permute-start | bytes 61448 | tf_op jit(solution)/shard_map/ppermute | solution.py:19
  13.0 18.8 %collective-permute-start.8 = (f32[3,1,16,128]{3,0,2,1:T(4,128)S(1)}, f32[3,1,16,128]{3,0,2,1:T(4,128)S(1)}, u32[]{:S(2)}, u32[]{:S(2)}) collective-permute-start(f32[3,1,16,128]{3,0,2,1:T(4,128)S(1)} %copy.32), channel_id=1, source_target_pairs={{0,16},{16,32},{32,48},{48,64},{64,80},{80,96},{96,112},{112,128},... | collective-permute-start | bytes 73736 | tf_op jit(solution)/shard_map/ppermute | solution.py:19
  16.8 0.7 copy-start.4
  16.9 1.2 copy-start.5
  19.5 19.3 %collective-permute-start.9 = (f32[3,1,16,128]{3,0,2,1:T(4,128)S(1)}, f32[3,1,16,128]{3,0,2,1:T(4,128)S(1)}, u32[]{:S(2)}, u32[]{:S(2)}) collective-permute-start(f32[3,1,16,128]{3,0,2,1:T(4,128)S(1)} %copy.33), channel_id=1, source_target_pairs={{16,0},{32,16},{48,32},{64,48},{80,64},{96,80},{112,96},{128,112},... | collective-permute-start | bytes 73736 | tf_op jit(solution)/shard_map/ppermute | solution.py:20
  20.8 36.0 %collective-permute-start.3 = (bf16[5,6,1,128]{3,0,2,1:T(8,128)(2,1)S(1)}, bf16[5,6,1,128]{3,0,2,1:T(8,128)(2,1)S(1)}, u32[]{:S(2)}, u32[]{:S(2)}) collective-permute-start(bf16[5,6,1,128]{3,0,2,1:T(8,128)(2,1)S(1)} %get-tuple-element.495), channel_id=1, source_target_pairs={{1,0},{2,1},{3,2},{4,3},{5,4},{6,5},{7,6},{8,7},{9,8},{10,9},{11,1... | collective-permute-start | bytes 23048 | tf_op jit(solution)/shard_map/ppermute | solution.py:20
  23.6 40.2 %collective-permute-start.2 = (bf16[5,6,1,128]{3,0,2,1:T(8,128)(2,1)S(1)}, bf16[5,6,1,128]{3,0,2,1:T(8,128)(2,1)S(1)}, u32[]{:S(2)}, u32[]{:S(2)}) collective-permute-start(bf16[5,6,1,128]{3,0,2,1:T(8,128)(2,1)S(1)} %get-tuple-element.494), channel_id=1, source_target_pairs={{0,1},{1,2},{2,3},{3,4},{4,5},{5,6},{6,7},{7,8},{8,9},{9,10},{10,1... | collective-permute-start | bytes 23048 | tf_op jit(solution)/shard_map/ppermute | solution.py:19
  29.8 53.5 %collective-permute-start.7 = (f32[3,6,1,128]{3,2,1,0:T(1,128)S(1)}, f32[3,6,1,128]{3,2,1,0:T(1,128)S(1)}, u32[]{:S(2)}, u32[]{:S(2)}) collective-permute-start(f32[3,6,1,128]{3,2,1,0:T(1,128)S(1)} %get-tuple-element.515), channel_id=1, source_target_pairs={{1,0},{2,1},{3,2},{4,3},{5,4},{6,5},{7,6},{8,7},{9,8},{10,9},{11,1... | collective-permute-start | bytes 27656 | tf_op jit(solution)/shard_map/ppermute | solution.py:20
  31.8 38.6 %collective-permute-start.6 = (f32[3,6,1,128]{3,2,1,0:T(1,128)S(1)}, f32[3,6,1,128]{3,2,1,0:T(1,128)S(1)}, u32[]{:S(2)}, u32[]{:S(2)}) collective-permute-start(f32[3,6,1,128]{3,2,1,0:T(1,128)S(1)} %get-tuple-element.514), channel_id=1, source_target_pairs={{0,1},{1,2},{2,3},{3,4},{4,5},{5,6},{6,7},{7,8},{8,9},{9,10},{10,1... | collective-permute-start | bytes 27656 | tf_op jit(solution)/shard_map/ppermute | solution.py:19
  38.9 83.8 %collective-permute-start.11 = (f32[3,6,1,128]{3,0,2,1:T(4,128)S(1)}, f32[3,6,1,128]{3,0,2,1:T(4,128)S(1)}, u32[]{:S(2)}, u32[]{:S(2)}) collective-permute-start(f32[3,6,1,128]{3,0,2,1:T(4,128)S(1)} %get-tuple-element.493), channel_id=1, source_target_pairs={{1,0},{2,1},{3,2},{4,3},{5,4},{6,5},{7,6},{8,7},{9,8},{10,9},{11,1... | collective-permute-start | bytes 27656 | tf_op jit(solution)/shard_map/ppermute | solution.py:20
  56.8 69.5 %collective-permute-start.10 = (f32[3,6,1,128]{3,0,2,1:T(4,128)S(1)}, f32[3,6,1,128]{3,0,2,1:T(4,128)S(1)}, u32[]{:S(2)}, u32[]{:S(2)}) collective-permute-start(f32[3,6,1,128]{3,0,2,1:T(4,128)S(1)} %get-tuple-element.492), channel_id=1, source_target_pairs={{0,1},{1,2},{2,3},{3,4},{4,5},{5,6},{6,7},{7,8},{8,9},{9,10},{10,1... | collective-permute-start | bytes 27656 | tf_op jit(solution)/shard_map/ppermute | solution.py:19
  140.3 4.2 copy-start.3
  359.2 4.3 collective-permute-start.13
  360.5 3.9 collective-permute-start.12
  364.4 113.6 %collective-permute-start.14 = (f32[3,4,1,128]{3,0,2,1:T(4,128)S(1)}, f32[3,4,1,128]{3,0,2,1:T(4,128)S(1)}, u32[]{:S(2)}, u32[]{:S(2)}) collective-permute-start(f32[3,4,1,128]{3,0,2,1:T(4,128)S(1)} %get-tuple-element.491), channel_id=1, source_target_pairs={{0,1},{1,2},{2,3},{3,4},{4,5},{5,6},{6,7},{7,8},{8,9},{9,10},{10,1... | collective-permute-start | bytes 18440 | tf_op jit(solution)/shard_map/ppermute | solution.py:19
  476.1 8.6 %collective-permute-start.15 = (f32[3,4,1,128]{3,0,2,1:T(4,128)S(1)}, f32[3,4,1,128]{3,0,2,1:T(4,128)S(1)}, u32[]{:S(2)}, u32[]{:S(2)}) collective-permute-start(f32[3,4,1,128]{3,0,2,1:T(4,128)S(1)} %get-tuple-element.490), channel_id=1, source_target_pairs={{1,0},{2,1},{3,2},{4,3},{5,4},{6,5},{7,6},{8,7},{9,8},{10,9},{11,1... | collective-permute-start | bytes 18440 | tf_op jit(solution)/shard_map/ppermute | solution.py:20
where the time goes:
time: 494 us; the launch traced here: 486 us
  matrix products  309 us (63%)
  blocking collectives  108 us (22%)
  starting transfers between devices  50 us (10%)
  waiting for transfers between devices  7.45 us (2%)
  local copies, waits for them, and re-layouts  5.24 us (1%)
    dot_general x36, matrix products, shell_forces(): jnp.einsum('rcps,xrcs->xrcp', one_hot[corner], shifted, precision=lax.Pre...  131 us
    dot_general x36, matrix products, shell_forces(): jnp.einsum('rcps,xrcp->xrcs', one_hot[corner], masked, precision=lax.Prec...  119 us
    pmax x1, blocking collectives, local(): top = lax.pmax(local_peak, ('gx', 'gy'))  108 us
    dot_general x9, matrix products, damage_block(): jnp.einsum('lrcq,rcqp->lrcp', values, weights, preferred_element_type=jnp...  58.7 us
    ppermute x8, starting transfers between devices, extended(): before = lax.ppermute(last, axis, up)  36.1 us
    ppermute x8, starting transfers between devices, extended(): after = lax.ppermute(leading, axis, down)  13.9 us
  transfers between devices with their start and end apart: 16, of which 2 were waited for; matrix products, arithmetic and copies ran while one was open for 17% of the time, Pallas kernels for 0%

commit v1 on v0

v1 whole, which is shorter than its diff:
```python
import jax
import jax.numpy as jnp
from jax import lax
from jax.experimental import pallas as pl
from jax.experimental.pallas import tpu as pltpu
from jax.sharding import PartitionSpec as P

PTS = 128
LAYERS = 5
ROWS = 4
COLS = 16
EXT_ROWS = ROWS + 2
EXT_COLS = COLS + 2
STRAIN_SCALE = 0.05
INV_RADIUS = 0.1
SPREAD_LIMIT = 128.0
SLOT_OF = {(0, 0): 0, (-1, -1): 1, (-1, 0): 2, (-1, 1): 3, (0, -1): 4, (0, 1): 5, (1, -1): 6, (1, 0): 7, (1, 1): 8}
PIECES = 32
SLAB = 8 * PIECES
RAW = 24
DISP_COLS = 24
FIELDS = 11
PAIRS = [(r + dr, r) for r in range(ROWS) for dr in range(3)]


def split3(value):
    hi = value.astype(jnp.bfloat16).astype(jnp.float32)
    rest = value - hi
    mid = rest.astype(jnp.bfloat16).astype(jnp.float32)
    return hi, mid, rest - mid


def body(
    strain, coords, disp, stiff, links, corners, before, after, left, right,
    damage, inner, rim_top, rim_bot, rim_left, rim_right, peak,
    sv, su, vt, block, weights, src, totals, strength, edisp, amounts, forces,
):
    f32, bf16 = jnp.float32, jnp.bfloat16
    gx, gy = lax.axis_index("gx"), lax.axis_index("gy")
    has_top, has_bot = gx > 0, gx < lax.axis_size("gx") - 1
    has_left, has_right = gy > 0, gy < lax.axis_size("gy") - 1

    row8 = lax.broadcasted_iota(jnp.int32, (8, PTS), 0)
    v_const = jnp.where((row8 >= 2) & (row8 <= 4), 1.0, 0.0).astype(f32)
    u_const = jnp.where(row8 >= 5, 1.0, 0.0).astype(f32)
    s_const = jnp.where(row8 == LAYERS, 1.0, 0.0).astype(f32)
    zero8 = jnp.zeros((8, PTS), f32)
    for c in range(EXT_COLS):
        for r in range(EXT_ROWS):
            sv[pl.ds(c * SLAB + r * PIECES + 16, 8), :] = v_const
            sv[pl.ds(c * SLAB + r * PIECES + 24, 8), :] = zero8
            src[pl.ds((c * EXT_ROWS + r) * 8, 8), :] = s_const
        for k in range(EXT_ROWS * PIECES, SLAB, 8):
            sv[pl.ds(c * SLAB + k, 8), :] = zero8
    for t in range(ROWS * COLS):
        su[pl.ds(t * PIECES + 16, 8), :] = u_const
        su[pl.ds(t * PIECES + 24, 8), :] = zero8
    block[...] = jnp.zeros(block.shape, bf16)
    forces[...] = jnp.zeros(forces.shape, f32)

    centre = [0.5 * (jnp.min(coords[x]) + jnp.max(coords[x])) for x in range(3)]

    def place(xyz, first, stride, count, own_first):
        a = [(xyz[x] - centre[x]) * INV_RADIUS for x in range(3)]
        norm = a[0] * a[0] + a[1] * a[1] + a[2] * a[2]
        for x in range(3):
            hi, mid, lo = split3(a[x])
            for k, v in zip((0, 3, 6, 9, 12, 15), (hi, hi, mid, mid, hi, lo)):
                sv[pl.ds(first + k + x, count, stride=stride), :] = v
            sv[pl.ds(first + RAW + x, count, stride=stride), :] = xyz[x]
            if own_first is not None:
                for k, v in zip((0, 3, 6, 9, 12, 15), (hi, mid, hi, mid, lo, hi)):
                    su[pl.ds(own_first + k + x, count, stride=ROWS * PIECES), :] = 2.0 * v
        for k, v in enumerate(split3(-norm)):
            sv[pl.ds(first + 21 + k, count, stride=stride), :] = v
        if own_first is not None:
            for k, v in enumerate(split3(1.0 - norm)):
                su[pl.ds(own_first + 18 + k, count, stride=ROWS * PIECES), :] = v
        return norm

    far = jnp.zeros((8, PTS), f32)
    for r in range(ROWS):
        norm = place([coords[x, r] for x in range(3)], SLAB + (r + 1) * PIECES, SLAB, COLS, r * PIECES)
        far = jnp.maximum(far, jnp.maximum(norm[0:8], norm[8:16]))
    for halo, r, there in ((before, 0, has_top), (after, EXT_ROWS - 1, has_bot)):
        norm = place([halo[x] for x in range(3)], SLAB + r * PIECES, SLAB, COLS, None)
        norm = jnp.where(there, norm, 0.0)
        far = jnp.maximum(far, jnp.maximum(norm[0:8], norm[8:16]))
    rows6 = lax.broadcasted_iota(jnp.int32, (EXT_ROWS, PTS), 0)
    inside6 = ((rows6 > 0) | has_top) & ((rows6 < EXT_ROWS - 1) | has_bot)
    side = jnp.zeros((EXT_ROWS, PTS), f32)
    for halo, c, there in ((left, 0, has_left), (right, EXT_COLS - 1, has_right)):
        norm = place([halo[x] for x in range(3)], c * SLAB, PIECES, EXT_ROWS, None)
        side = jnp.maximum(side, jnp.where(inside6 & there, norm, 0.0))
    spread = jnp.maximum(jnp.max(far), jnp.max(side))
    near = spread <= SPREAD_LIMIT

    for l in range(LAYERS):
        for r in range(EXT_ROWS):
            row = before[3 + l] if r == 0 else after[3 + l] if r == EXT_ROWS - 1 else strain[l, r - 1]
            src[pl.ds((EXT_ROWS + r) * 8 + l, COLS, stride=EXT_ROWS * 8), :] = row
        src[pl.ds(l, EXT_ROWS, stride=8), :] = left[3 + l]
        src[pl.ds((EXT_COLS - 1) * EXT_ROWS * 8 + l, EXT_ROWS, stride=8), :] = right[3 + l]
    for x in range(3):
        for r in range(EXT_ROWS):
            row = before[8 + x] if r == 0 else after[8 + x] if r == EXT_ROWS - 1 else disp[x, r - 1]
            edisp[pl.ds((x * EXT_ROWS + r) * DISP_COLS + 1, COLS), :] = row
        edisp[pl.ds(x * EXT_ROWS * DISP_COLS, EXT_ROWS, stride=DISP_COLS), :] = left[8 + x]
        edisp[pl.ds(x * EXT_ROWS * DISP_COLS + COLS + 1, EXT_ROWS, stride=DISP_COLS), :] = right[8 + x]

    def live(dr, dc, r, c):
        return jnp.where(links[SLOT_OF[(dr, dc)], r, c] >= 0, 1.0, 0.0).astype(f32)

    @pl.when(near)
    def _():
        def turn(c, carry):
            slab = sv[pl.ds(pl.multiple_of(c * SLAB, SLAB), SLAB), :]
            vt[pl.ds(pl.multiple_of(c * PTS, PTS), PTS), :] = slab.T.astype(bf16)
            return carry

        lax.fori_loop(0, EXT_COLS, turn, 0, unroll=6)

        def column(c, carry):
            for j, (ext, r) in enumerate(PAIRS):
                own = su[pl.ds(pl.multiple_of((c * ROWS + r) * PIECES, PIECES), PIECES), :]
                block[pl.ds(ext * PIECES, PIECES), pl.ds(j * PTS, PTS)] = own.astype(bf16)
            sums = [zero8 for _ in range(ROWS)]
            near_cols = vt[pl.ds(pl.multiple_of(c * PTS, PTS), 3 * PTS), :]
            for j in range(0, len(PAIRS), 2):
                bell = jnp.dot(near_cols, block[:, j * PTS : (j + 2) * PTS], preferred_element_type=f32)
                bell = jnp.maximum(bell, 0.0)
                weights[:, j * PTS : (j + 2) * PTS] = (bell * bell).astype(bf16)
            for j in range(0, len(PAIRS), 2):
                halves = []
                for ext, r in PAIRS[j : j + 2]:
                    parts = []
                    for dc in range(3):
                        at = pl.multiple_of(((c + dc) * EXT_ROWS + ext) * 8, 8)
                        parts.append(src[pl.ds(at, 8), :] * live(ext - r - 1, dc - 1, r, c))
                    halves.append(jnp.concatenate(parts, axis=1))
                values = jnp.concatenate(halves, axis=0).astype(bf16)
                out = jnp.dot(values, weights[:, j * PTS : (j + 2) * PTS], preferred_element_type=f32)
                for h in range(2):
                    r = PAIRS[j + h][1]
                    sums[r] = sums[r] + out[8 * h : 8 * h + 8, h * PTS : (h + 1) * PTS]
            for r in range(ROWS):
                totals[pl.ds(r * COLS + c, 8, stride=ROWS * COLS), :] = sums[r]
            return carry

        lax.fori_loop(0, COLS, column, 0, unroll=2)

    @pl.when(jnp.logical_not(near))
    def _():
        def tile(t, carry):
            r, c = t // COLS, t % COLS
            own = sv[pl.ds(pl.multiple_of((c + 1) * SLAB + (r + 1) * PIECES + RAW, 8), 8), :]
            total = zero8
            for (dr, dc), slot in SLOT_OF.items():
                at = pl.multiple_of((c + 1 + dc) * SLAB + (r + 1 + dr) * PIECES + RAW, 8)
                other = sv[pl.ds(at, 8), :]
                turned = jnp.concatenate([other] + [zero8] * 15, axis=0).T
                dist = jnp.zeros((PTS, PTS), f32)
                for x in range(3):
                    dist = dist + (own[x : x + 1, :] - turned[:, x : x + 1]) ** 2
                bell = jnp.maximum(1.0 - dist * 0.01, 0.0)
                pair = (bell * bell).astype(bf16)
                at = pl.multiple_of(((c + 1 + dc) * EXT_ROWS + r + 1 + dr) * 8, 8)
                values = src[pl.ds(at, 8), :] * jnp.where(links[slot, r, c] >= 0, 1.0, 0.0)
                total = total + jnp.dot(values.astype(bf16), pair, preferred_element_type=f32)
            totals[pl.ds(t, 8, stride=ROWS * COLS), :] = total
            return carry

        lax.fori_loop(0, ROWS * COLS, tile, 0)

    top = jnp.zeros((COLS, PTS), f32)
    for r in range(ROWS):
        weight_sum = totals[pl.ds(LAYERS * ROWS * COLS + r * COLS, COLS), :]
        mean = jnp.zeros((COLS, PTS), f32)
        for l in range(LAYERS):
            averaged = totals[pl.ds(l * ROWS * COLS + r * COLS, COLS), :] / weight_sum
            value = averaged / (averaged + STRAIN_SCALE)
            damage[l, r] = value
            mean = mean + value
        power = (1.0 - mean / LAYERS) * stiff[0, r]
        strength[r] = power
        top = jnp.maximum(top, power) if r else power
    peak[...] = jnp.full(peak.shape, jnp.max(top), f32)

    def gather(r, carry):
        for g in range(COLS // 8):
            power = strength[r, 8 * g : 8 * g + 8, :]
            codes = [corners[k, r, 8 * g : 8 * g + 8, :] for k in range(4)]
            offset = [code >> 7 for code in codes]
            slot = [code & (PTS - 1) for code in codes]
            at = [
                pl.ds(pl.multiple_of(((r * COLS + 8 * g) * 4 + k) * 8, 8) + i, 8, stride=32)
                for k in range(4) for i in range(8)
            ]
            for k in range(4):
                amounts[at[8 * k + 3], :] = offset[k].astype(f32)
                amounts[at[8 * k + 7], :] = slot[k].astype(f32)
            for x in range(3):
                picked = []
                base = (x * EXT_ROWS + r) * DISP_COLS + 8 * g
                table = [edisp[pl.ds(base + (o // 3) * DISP_COLS + o % 3, 8), :] for o in range(9)]
                for k in range(4):
                    found = jnp.take_along_axis(table[0], slot[k], axis=1)
                    for o in range(1, 9):
                        found = jnp.where(offset[k] == o, jnp.take_along_axis(table[o], slot[k], axis=1), found)
                    picked.append(found)
                springs = [power * (picked[(k + 1) % 4] - picked[k]) for k in range(4)]
                for k in range(4):
                    amount = springs[k] - springs[(k + 3) % 4]
                    hi = amount.astype(bf16).astype(f32)
                    amounts[at[8 * k + x], :] = hi
                    amounts[at[8 * k + 4 + x], :] = amount - hi
        return carry

    lax.fori_loop(0, ROWS, gather, 0, unroll=2)

    nodes = lax.broadcasted_iota(jnp.int32, (PTS, PTS), 0).astype(f32)

    def scatter(t, carry):
        r, c = t // COLS, t % COLS
        picks, rows = [], []
        for k in range(4):
            own = amounts[pl.ds(pl.multiple_of((t * 4 + k) * 8, 8), 8), :]
            offset, slot = own[3:4, :], own[7:8, :]
            rows.append(jnp.concatenate([jnp.where(offset == float(o), own, 0.0) for o in range(10)], axis=0))
            picks.append(jnp.where(slot == nodes, 1.0, 0.0).astype(bf16))
        left_side = jnp.concatenate(rows, axis=1).astype(bf16)
        right_side = jnp.concatenate(picks, axis=1)
        out = lax.dot_general(left_side, right_side, (((1,), (1,)), ((), ())), preferred_element_type=f32)
        for o in range(9):
            at = pl.ds(pl.multiple_of(((r + o // 3) * EXT_COLS + c + o % 3) * 8, 8), 8)
            forces[at, :] = forces[at, :] + out[8 * o : 8 * o + 8]
        return carry

    lax.fori_loop(0, ROWS * COLS, scatter, 0, unroll=8)

    def node_sum(x, first, count, stride):
        return (
            forces[pl.ds(first * 8 + x, count, stride=8 * stride), :]
            + forces[pl.ds(first * 8 + 4 + x, count, stride=8 * stride), :]
        )

    for x in range(3):
        for r in range(ROWS):
            inner[x, r] = node_sum(x, (r + 1) * EXT_COLS + 1, COLS, 1)
        rim_top[x] = node_sum(x, 0, EXT_COLS, 1).astype(bf16)
        rim_bot[x] = node_sum(x, (EXT_ROWS - 1) * EXT_COLS, EXT_COLS, 1).astype(bf16)
        rim_left[x] = node_sum(x, EXT_COLS, ROWS, EXT_COLS)
        rim_right[x] = node_sum(x, 2 * EXT_COLS - 1, ROWS, EXT_COLS)


def block_step(strain, coords, disp, stiff, links, corners, before, after, left, right, peers):
    f32 = jnp.float32
    vmem = pl.BlockSpec(memory_space=pltpu.VMEM)
    specs = [vmem] * 10
    specs[4] = pl.BlockSpec(memory_space=pltpu.SMEM)
    outs = (
        jax.ShapeDtypeStruct((LAYERS, ROWS, COLS, PTS), f32),
        jax.ShapeDtypeStruct((3, ROWS, COLS, PTS), f32),
        jax.ShapeDtypeStruct((3, EXT_COLS, PTS), jnp.bfloat16),
        jax.ShapeDtypeStruct((3, EXT_COLS, PTS), jnp.bfloat16),
        jax.ShapeDtypeStruct((3, ROWS, PTS), f32),
        jax.ShapeDtypeStruct((3, ROWS, PTS), f32),
        jax.ShapeDtypeStruct((peers, PTS), f32),
    )
    scratch = [
        pltpu.VMEM((EXT_COLS * SLAB, PTS), f32),
        pltpu.VMEM((COLS * ROWS * PIECES, PTS), f32),
        pltpu.VMEM((EXT_COLS * PTS, SLAB), jnp.bfloat16),
        pltpu.VMEM((SLAB, len(PAIRS) * PTS), jnp.bfloat16),
        pltpu.VMEM((3 * PTS, len(PAIRS) * PTS), jnp.bfloat16),
        pltpu.VMEM((EXT_COLS * EXT_ROWS * 8, PTS), f32),
        pltpu.VMEM((8 * ROWS * COLS, PTS), f32),
        pltpu.VMEM((ROWS, COLS, PTS), f32),
        pltpu.VMEM((3 * EXT_ROWS * DISP_COLS, PTS), f32),
        pltpu.VMEM((ROWS * COLS * 32, PTS), f32),
        pltpu.VMEM((EXT_ROWS * EXT_COLS * 8, PTS), f32),
    ]
    return pl.pallas_call(
        body,
        out_shape=outs,
        in_specs=specs,
        out_specs=(vmem,) * 7,
        scratch_shapes=scratch,
        compiler_params=pltpu.CompilerParams(vmem_limit_bytes=40 * 1024 * 1024),
        name="block_step",
    )(strain, coords, disp, stiff, links, corners, before, after, left, right)


def exchange(last, first, axis):
    peers = lax.axis_size(axis)
    up = [(i, i + 1) for i in range(peers - 1)]
    return lax.ppermute(last, axis, up), lax.ppermute(first, axis, [(j, i) for i, j in up])


def local(strain, coords, displacement, stiffness, neighbours, corners):
    peers_x, peers_y = lax.axis_size("gx"), lax.axis_size("gy")
    own = (coords, strain, displacement)

    def row(r):
        return jnp.concatenate([v[:, r] for v in own], axis=0)

    def column(c):
        mid = jnp.concatenate([v[:, :, c] for v in own], axis=0)
        return jnp.concatenate([before[:, None, c], mid, after[:, None, c]], axis=1)

    before, after = exchange(row(ROWS - 1), row(0), "gx")
    left, right = exchange(column(COLS - 1), column(0), "gy")
    damage, inner, rim_top, rim_bot, rim_left, rim_right, peak = block_step(
        strain, coords, displacement, stiffness, neighbours, corners, before, after, left, right, peers_x
    )
    from_above, from_below = exchange(rim_bot, rim_top, "gx")
    peaks = lax.all_to_all(peak, "gx", 0, 0, tiled=True)
    from_above, from_below = from_above.astype(jnp.float32), from_below.astype(jnp.float32)

    def side(rim, c):
        return rim.at[:, 0].add(from_above[:, c]).at[:, ROWS - 1].add(from_below[:, c])

    from_left, from_right = exchange(side(rim_right, EXT_COLS - 1), side(rim_left, 0), "gy")
    peak = jnp.broadcast_to(jnp.max(peaks, axis=0, keepdims=True), (peers_y, PTS))
    top = jnp.max(lax.all_to_all(peak, "gy", 0, 0, tiled=True))
    inner = inner.at[:, 0].add(from_above[:, 1:-1]).at[:, ROWS - 1].add(from_below[:, 1:-1])
    inner = inner.at[:, :, 0].add(from_left).at[:, :, COLS - 1].add(from_right)
    return damage, inner / top


def solution(mesh):
    spec = P(None, "gx", "gy", None)
    in_specs = (spec, spec, spec, spec, P(None, "gx", "gy"), spec)
    return jax.shard_map(local, mesh=mesh, in_specs=in_specs, out_specs=(spec, spec), check_vma=False)
```

time: 494 us -> 93.4 us (0.19)
  the two profiles are of different devices: /device:TPU:6 before, /device:TPU:40 now
where the time goes in v1:
time: 93.4 us; the launch traced here: 92.8 us
  starting transfers between devices  50.2 us (54%)
  Pallas kernels  18.8 us (20%)
  waiting for transfers between devices  18 us (19%)
  local copies, waits for them, and re-layouts  3.35 us (4%)
  other arithmetic  1.44 us (2%)
  between operations  0.94 us (1%)
    pallas_call x1, Pallas kernels, block_step(): pl.pallas_call(body, out_shape=outs, in_specs=specs, out_specs=(vmem,) *...  18.8 us
    all_to_all x1, starting transfers between devices, local(): top = jnp.max(lax.all_to_all(peak, 'gy', 0, 0, tiled=True))  18.7 us
    ppermute x4, starting transfers between devices, exchange(): lax.ppermute(first, axis, [(j, i) for i, j in up])  11.3 us
    ppermute x4, starting transfers between devices, exchange(): lax.ppermute(last, axis, up)  10.9 us
    all_to_all x1, waiting for transfers between devices, local(): top = jnp.max(lax.all_to_all(peak, 'gy', 0, 0, tiled=True))  9.86 us
    all_to_all x1, starting transfers between devices, local(): peaks = lax.all_to_all(peak, 'gx', 0, 0, tiled=True)  9.36 us
    ppermute x4, waiting for transfers between devices, exchange(): lax.ppermute(first, axis, [(j, i) for i, j in up])  7.76 us
  transfers between devices with their start and end apart: 10, of which 5 were waited for; matrix products, arithmetic and copies ran while one was open for 1% of the time, Pallas kernels for 0%

profile of v1, /device:TPU:40, one launch (start us, length us, event | category | flops | bytes accessed | tf_op | source)
XLA Modules:
  0.0 92.8 jit_solution(12259885538475740875)
XLA Ops:
  0.6 0.0 copy-start.1
  0.6 0.8 slice_bitcast_fusion
  1.5 0.0 copy-done.1
  1.5 0.8 slice_bitcast_fusion.4
  2.3 0.0 copy-start
  2.3 2.1 %collective-permute-start = (f32[11,16,128]{2,1,0:T(8,128)S(1)}, f32[11,16,128]{2,1,0:T(8,128)S(1)}, u32[]{:S(2)}, u32[]{:S(2)}) collective-permute-start(f32[11,16,128]{2,1,0:T(8,128)S(1)} %pad_maximum_fusion), channel_id=1, source_target_pairs={{0,16},{16,32},{32,48},{48,64},{64,80},{80,96},{96,112},{112,128},... | collective-permute-start | bytes 270344 | tf_op jit(solution)/shard_map/ppermute | solution.py:297
  4.4 0.0 copy-start.2
  4.4 4.7 %collective-permute-start.1 = (f32[11,16,128]{2,1,0:T(8,128)S(1)}, f32[11,16,128]{2,1,0:T(8,128)S(1)}, u32[]{:S(2)}, u32[]{:S(2)}) collective-permute-start(f32[11,16,128]{2,1,0:T(8,128)S(1)} %pad_maximum_fusion.1), channel_id=1, source_target_pairs={{16,0},{32,16},{48,32},{64,48},{80,64},{96,80},{112,96},{128,112},... | collective-permute-start | bytes 270344 | tf_op jit(solution)/shard_map/ppermute | solution.py:297
  9.1 0.0 copy-done
  9.1 0.0 copy-done.2
  9.1 0.0 copy-start.3
  9.2 0.0 collective-permute-done.before
  9.2 2.0 %collective-permute-done.1.after = f32[11,16,128]{2,1,0:T(8,128)S(1)} collective-permute-done((f32[11,16,128]{2,1,0:T(8,128)S(1)}, f32[11,16,128]{2,1,0:T(8,128)S(1)}, u32[]{:S(2)}, u32[]{:S(2)}) %collective-permute-start.1) | collective-permute-done | bytes 90144 | tf_op jit(solution)/shard_map/ppermute | solution.py:297
  11.2 3.4 %collective-permute-start.2 = (f32[11,6,128]{2,1,0:T(8,128)S(1)}, f32[11,6,128]{2,1,0:T(8,128)S(1)}, u32[]{:S(2)}, u32[]{:S(2)}) collective-permute-start(f32[11,6,128]{2,1,0:T(8,128)S(1)} %pad_maximum_fusion.2), channel_id=1, source_target_pairs={{0,1},{1,2},{2,3},{3,4},{4,5},{5,6},{6,7},{7,8},{8,9},{9,10},{10,1... | collective-permute-start | bytes 101384 | tf_op jit(solution)/shard_map/ppermute | solution.py:297
  14.6 0.0 copy-start.4
  14.6 0.0 copy-start.5
  14.7 1.3 %collective-permute-start.3 = (f32[11,6,128]{2,1,0:T(8,128)S(1)}, f32[11,6,128]{2,1,0:T(8,128)S(1)}, u32[]{:S(2)}, u32[]{:S(2)}) collective-permute-start(f32[11,6,128]{2,1,0:T(8,128)S(1)} %pad_maximum_fusion.3), channel_id=1, source_target_pairs={{1,0},{2,1},{3,2},{4,3},{5,4},{6,5},{7,6},{8,7},{9,8},{10,9},{11,1... | collective-permute-start | bytes 101384 | tf_op jit(solution)/shard_map/ppermute | solution.py:297
  16.0 0.3 collective-permute-done.2.left
  16.3 4.5 %collective-permute-done.3.right = f32[11,6,128]{2,1,0:T(8,128)S(1)} collective-permute-done((f32[11,6,128]{2,1,0:T(8,128)S(1)}, f32[11,6,128]{2,1,0:T(8,128)S(1)}, u32[]{:S(2)}, u32[]{:S(2)}) %collective-permute-start.3) | collective-permute-done | bytes 33824 | tf_op jit(solution)/shard_map/ppermute | solution.py:297
  20.8 0.0 copy-done.3
  20.8 0.0 copy-done.4
  20.8 0.0 copy-done.5
  20.8 18.8 %block_step.1 = (f32[5,4,16,128]{3,2,1,0:T(8,128)}, f32[3,4,16,128]{3,2,1,0:T(8,128)S(1)}, bf16[3,18,128]{2,1,0:T(8,128)(2,1)S(1)}, bf16[3,18,128]{2,1,0:T(8,128...) custom-call(f32[5,4,16,128]{3,2,1,0:T(8,128)S(1)} %copy-done, ...), custom_call_target="tpu_custom_call" | custom-call | tf_op jit(solution)/shard_map/block_step/pallas_call | solution.py:283
  39.6 2.0 %collective-permute-start.4 = (bf16[3,18,128]{2,1,0:T(8,128)(2,1)S(1)}, bf16[3,18,128]{2,1,0:T(8,128)(2,1)S(1)}, u32[]{:S(2)}, u32[]{:S(2)}) collective-permute-start(bf16[3,18,128]{2,1,0:T(8,128)(2,1)S(1)} %get-tuple-element.107), channel_id=1, source_target_pairs={{0,16},{16,32},{32,48},{48,64},{64,80},{80,96},{96,112},{112,128},... | collective-permute-start | bytes 41480 | tf_op jit(solution)/shard_map/ppermute | solution.py:297
  41.7 9.4 %all-to-all-start = ((f32[32,1,128]{2,1,0:T(1,128)}), f32[32,1,128]{2,1,0:T(1,128)S(1)}, u32[]{:S(2)}, u32[]{:S(2)}) async-start(f32[32,1,128]{2,1,0:T(1,128)} %bitcast.17), calls=%async_computation | async-start | bytes 32768 | tf_op jit(solution)/shard_map/all_to_all | solution.py:317
  51.0 4.0 %collective-permute-start.5 = (bf16[3,18,128]{2,1,0:T(8,128)(2,1)S(1)}, bf16[3,18,128]{2,1,0:T(8,128)(2,1)S(1)}, u32[]{:S(2)}, u32[]{:S(2)}) collective-permute-start(bf16[3,18,128]{2,1,0:T(8,128)(2,1)S(1)} %get-tuple-element.108), channel_id=1, source_target_pairs={{16,0},{32,16},{48,32},{64,48},{80,64},{96,80},{112,96},{128,112},... | collective-permute-start | bytes 41480 | tf_op jit(solution)/shard_map/ppermute | solution.py:297
  55.1 0.0 collective-permute-done.4
  55.2 1.3 %collective-permute-done.5 = bf16[3,18,128]{2,1,0:T(8,128)(2,1)S(1)} collective-permute-done((bf16[3,18,128]{2,1,0:T(8,128)(2,1)S(1)}, bf16[3,18,128]{2,1,0:T(8,128)(2,1)S(1)}, u32[]{:S(2)}, u32[]{:S(2)}) %collective-permute-start.5) | collective-permute-done | bytes 13856 | tf_op jit(solution)/shard_map/ppermute | solution.py:297
  56.5 3.4 %collective-permute-start.6 = (f32[3,4,128]{2,1,0:T(4,128)S(1)}, f32[3,4,128]{2,1,0:T(4,128)S(1)}, u32[]{:S(2)}, u32[]{:S(2)}) collective-permute-start(f32[3,4,128]{2,1,0:T(4,128)S(1)} %scatter-add.31), channel_id=1, source_target_pairs={{0,1},{1,2},{2,3},{3,4},{4,5},{5,6},{6,7},{7,8},{8,9},{9,10},{10,1... | collective-permute-start | bytes 18440 | tf_op jit(solution)/shard_map/ppermute | solution.py:297
  60.1 1.3 %collective-permute-start.7 = (f32[3,4,128]{2,1,0:T(4,128)S(1)}, f32[3,4,128]{2,1,0:T(4,128)S(1)}, u32[]{:S(2)}, u32[]{:S(2)}) collective-permute-start(f32[3,4,128]{2,1,0:T(4,128)S(1)} %scatter-add.36), channel_id=1, source_target_pairs={{1,0},{2,1},{3,2},{4,3},{5,4},{6,5},{7,6},{8,7},{9,8},{10,9},{11,1... | collective-permute-start | bytes 18440 | tf_op jit(solution)/shard_map/ppermute | solution.py:297
  61.4 0.1 scatter-add.29
  61.5 0.0 collective-permute-done.6
  61.6 0.0 all-to-all-done
  61.6 0.1 reduce_max.18
  61.6 0.6 broadcast_in_dim.2
  62.2 18.7 %all-to-all-start.1 = ((f32[16,1,128]{2,1,0:T(1,128)}), f32[16,1,128]{2,1,0:T(1,128)S(1)}, u32[]{:S(2)}, u32[]{:S(2)}) async-start(f32[16,1,128]{2,1,0:T(1,128)} %broadcast_in_dim.2), calls=%async_computation.1 | async-start | bytes 16384 | tf_op jit(solution)/shard_map/all_to_all | solution.py:325
  81.0 0.0 collective-permute-done.7
  81.0 9.9 %all-to-all-done.1 = f32[16,1,128]{2,1,0:T(1,128)S(1)} async-done(((f32[16,1,128]{2,1,0:T(1,128)}), f32[16,1,128]{2,1,0:T(1,128)S(1)}, u32[]{:S(2)}, u32[]{:S(2)}) %all-to-all-start.1) | async-done | bytes 8224 | tf_op jit(solution)/shard_map/all_to_all | solution.py:325
  90.9 0.6 reduce_max.19
  91.5 0.7 broadcast_divide_fusion
  92.1 0.6 copy.79
  (24 shorter events, 0.4 us)
Async XLA Ops:
  0.6 0.9 copy-start.1
  2.3 6.8 %copy-start = (f32[5,4,16,128]{3,2,1,0:T(8,128)S(1)}, f32[5,4,16,128]{3,2,1,0:T(8,128)}, u32[]{:S(2)}) copy-start(f32[5,4,16,128]{3,2,1,0:T(8,128)} %strain.1) | copy-start | bytes 491524
  2.3 6.9 %collective-permute-start = (f32[11,16,128]{2,1,0:T(8,128)S(1)}, f32[11,16,128]{2,1,0:T(8,128)S(1)}, u32[]{:S(2)}, u32[]{:S(2)}) collective-permute-start(f32[11,16,128]{2,1,0:T(8,128)S(1)} %pad_maximum_fusion), channel_id=1, source_target_pairs={{0,16},{16,32},{32,48},{48,64},{64,80},{80,96},{96,112},{112,128},... | collective-permute-start | bytes 270344 | tf_op jit(solution)/shard_map/ppermute | solution.py:297
  4.4 4.8 %copy-start.2 = (f32[3,4,16,128]{3,2,1,0:T(8,128)S(1)}, f32[3,4,16,128]{3,2,1,0:T(8,128)}, u32[]{:S(2)}) copy-start(f32[3,4,16,128]{3,2,1,0:T(8,128)} %disp.1) | copy-start | bytes 294916
  4.4 6.8 %collective-permute-start.1 = (f32[11,16,128]{2,1,0:T(8,128)S(1)}, f32[11,16,128]{2,1,0:T(8,128)S(1)}, u32[]{:S(2)}, u32[]{:S(2)}) collective-permute-start(f32[11,16,128]{2,1,0:T(8,128)S(1)} %pad_maximum_fusion.1), channel_id=1, source_target_pairs={{16,0},{32,16},{48,32},{64,48},{80,64},{96,80},{112,96},{128,112},... | collective-permute-start | bytes 270344 | tf_op jit(solution)/shard_map/ppermute | solution.py:297
  9.1 11.6 %copy-start.3 = (s32[4,4,16,128]{3,2,1,0:T(8,128)S(1)}, s32[4,4,16,128]{3,2,1,0:T(8,128)}, u32[]{:S(2)}) copy-start(s32[4,4,16,128]{3,2,1,0:T(8,128)} %corners.1) | copy-start | bytes 393220
  11.2 5.1 %collective-permute-start.2 = (f32[11,6,128]{2,1,0:T(8,128)S(1)}, f32[11,6,128]{2,1,0:T(8,128)S(1)}, u32[]{:S(2)}, u32[]{:S(2)}) collective-permute-start(f32[11,6,128]{2,1,0:T(8,128)S(1)} %pad_maximum_fusion.2), channel_id=1, source_target_pairs={{0,1},{1,2},{2,3},{3,4},{4,5},{5,6},{6,7},{7,8},{8,9},{9,10},{10,1... | collective-permute-start | bytes 101384 | tf_op jit(solution)/shard_map/ppermute | solution.py:297
  14.6 6.2 %copy-start.4 = (f32[1,4,16,128]{3,2,1,0:T(8,128)S(1)}, f32[1,4,16,128]{3,2,1,0:T(8,128)}, u32[]{:S(2)}) copy-start(f32[1,4,16,128]{3,2,1,0:T(8,128)} %stiff.1) | copy-start | bytes 98308
  14.6 6.1 %copy-start.5 = (s32[9,4,16]{2,1,0:T(4,128)S(1)}, s32[9,4,16]{2,1,0:T(4,128)}, u32[]{:S(2)}) copy-start(s32[9,4,16]{2,1,0:T(4,128)} %links.1) | copy-start | bytes 6916
  14.7 6.1 %collective-permute-start.3 = (f32[11,6,128]{2,1,0:T(8,128)S(1)}, f32[11,6,128]{2,1,0:T(8,128)S(1)}, u32[]{:S(2)}, u32[]{:S(2)}) collective-permute-start(f32[11,6,128]{2,1,0:T(8,128)S(1)} %pad_maximum_fusion.3), channel_id=1, source_target_pairs={{1,0},{2,1},{3,2},{4,3},{5,4},{6,5},{7,6},{8,7},{9,8},{10,9},{11,1... | collective-permute-start | bytes 101384 | tf_op jit(solution)/shard_map/ppermute | solution.py:297
  39.6 15.4 %collective-permute-start.4 = (bf16[3,18,128]{2,1,0:T(8,128)(2,1)S(1)}, bf16[3,18,128]{2,1,0:T(8,128)(2,1)S(1)}, u32[]{:S(2)}, u32[]{:S(2)}) collective-permute-start(bf16[3,18,128]{2,1,0:T(8,128)(2,1)S(1)} %get-tuple-element.107), channel_id=1, source_target_pairs={{0,16},{16,32},{32,48},{48,64},{64,80},{80,96},{96,112},{112,128},... | collective-permute-start | bytes 41480 | tf_op jit(solution)/shard_map/ppermute | solution.py:297
  41.7 19.9 %all-to-all-start = ((f32[32,1,128]{2,1,0:T(1,128)}), f32[32,1,128]{2,1,0:T(1,128)S(1)}, u32[]{:S(2)}, u32[]{:S(2)}) async-start(f32[32,1,128]{2,1,0:T(1,128)} %bitcast.17), calls=%async_computation | async-start | bytes 32768 | tf_op jit(solution)/shard_map/all_to_all | solution.py:317
  51.0 5.5 %collective-permute-start.5 = (bf16[3,18,128]{2,1,0:T(8,128)(2,1)S(1)}, bf16[3,18,128]{2,1,0:T(8,128)(2,1)S(1)}, u32[]{:S(2)}, u32[]{:S(2)}) collective-permute-start(bf16[3,18,128]{2,1,0:T(8,128)(2,1)S(1)} %get-tuple-element.108), channel_id=1, source_target_pairs={{16,0},{32,16},{48,32},{64,48},{80,64},{96,80},{112,96},{128,112},... | collective-permute-start | bytes 41480 | tf_op jit(solution)/shard_map/ppermute | solution.py:297
  56.5 5.0 %collective-permute-start.6 = (f32[3,4,128]{2,1,0:T(4,128)S(1)}, f32[3,4,128]{2,1,0:T(4,128)S(1)}, u32[]{:S(2)}, u32[]{:S(2)}) collective-permute-start(f32[3,4,128]{2,1,0:T(4,128)S(1)} %scatter-add.31), channel_id=1, source_target_pairs={{0,1},{1,2},{2,3},{3,4},{4,5},{5,6},{6,7},{7,8},{8,9},{9,10},{10,1... | collective-permute-start | bytes 18440 | tf_op jit(solution)/shard_map/ppermute | solution.py:297
  60.1 20.9 %collective-permute-start.7 = (f32[3,4,128]{2,1,0:T(4,128)S(1)}, f32[3,4,128]{2,1,0:T(4,128)S(1)}, u32[]{:S(2)}, u32[]{:S(2)}) collective-permute-start(f32[3,4,128]{2,1,0:T(4,128)S(1)} %scatter-add.36), channel_id=1, source_target_pairs={{1,0},{2,1},{3,2},{4,3},{5,4},{6,5},{7,6},{8,7},{9,8},{10,9},{11,1... | collective-permute-start | bytes 18440 | tf_op jit(solution)/shard_map/ppermute | solution.py:297
  62.2 28.6 %all-to-all-start.1 = ((f32[16,1,128]{2,1,0:T(1,128)}), f32[16,1,128]{2,1,0:T(1,128)S(1)}, u32[]{:S(2)}, u32[]{:S(2)}) async-start(f32[16,1,128]{2,1,0:T(1,128)} %broadcast_in_dim.2), calls=%async_computation.1 | async-start | bytes 16384 | tf_op jit(solution)/shard_map/all_to_all | solution.py:325

commit v2 on v1

v2 whole, which is shorter than its diff:
```python
import jax
import jax.numpy as jnp
from jax import lax
from jax.experimental import pallas as pl
from jax.experimental.pallas import tpu as pltpu
from jax.sharding import PartitionSpec as P

PTS = 128
LAYERS = 5
ROWS = 4
COLS = 16
EXT_ROWS = ROWS + 2
LAST = ROWS + 1
EXT_COLS = COLS + 2
STRAIN_SCALE = 0.05
INV_RADIUS = 0.1
SPREAD_LIMIT = 128.0
SLOT_OF = {(0, 0): 0, (-1, -1): 1, (-1, 0): 2, (-1, 1): 3, (0, -1): 4, (0, 1): 5, (1, -1): 6, (1, 0): 7, (1, 1): 8}
PIECES = 32
RAW = 24
TILES = ROWS * COLS
DISP_COLS = 24
INSIDE = [(o, r) for r in range(ROWS) for o in range(ROWS) if abs(o - r) <= 1]
V_ROWS = (0, 3, 6, 9, 12, 15)
MIB = 1024 * 1024


def split3(value):
    hi = value.astype(jnp.bfloat16).astype(jnp.float32)
    rest = value - hi
    mid = rest.astype(jnp.bfloat16).astype(jnp.float32)
    return hi, mid, rest - mid


def scaled(xyz, centre):
    a = [(xyz[x] - centre[x]) * INV_RADIUS for x in range(3)]
    return a, a[0] * a[0] + a[1] * a[1] + a[2] * a[2]


def centre_of(coords):
    return [0.5 * (jnp.min(coords[x]) + jnp.max(coords[x])) for x in range(3)]


def put_other(sv, a, norm, at):
    for x in range(3):
        hi, mid, lo = split3(a[x])
        for k, v in zip(V_ROWS, (hi, hi, mid, mid, hi, lo)):
            sv[at(k + x), :] = v
    for k, v in enumerate(split3(-norm)):
        sv[at(21 + k), :] = v


def put_own(su, a, norm, xyz, at):
    for x in range(3):
        hi, mid, lo = split3(a[x])
        for k, v in zip(V_ROWS, (hi, mid, hi, mid, lo, hi)):
            su[at(k + x), :] = 2.0 * v
        su[at(RAW + x), :] = xyz[x]
    for k, v in enumerate(split3(1.0 - norm)):
        su[at(18 + k), :] = v


def constant_rows():
    row8 = lax.broadcasted_iota(jnp.int32, (8, PTS), 0)
    other = jnp.where((row8 >= 2) & (row8 <= 4), 1.0, 0.0)
    own = jnp.where(row8 >= 5, 1.0, 0.0)
    ones = jnp.where(row8 == LAYERS, 1.0, 0.0)
    return other.astype(jnp.float32), own.astype(jnp.float32), ones.astype(jnp.float32)


def rows_at(index, size, count=None):
    return pl.ds(pl.multiple_of(index * size, size), size if count is None else count)


def bell_weights(other, own):
    bell = jnp.maximum(jnp.dot(other, own, preferred_element_type=jnp.float32), 0.0)
    return (bell * bell).astype(jnp.bfloat16)


def direct_total(own, other, values):
    turned = jnp.concatenate([other] + [jnp.zeros((8, PTS), jnp.float32)] * 15, axis=0).T
    dist = jnp.zeros((PTS, PTS), jnp.float32)
    for x in range(3):
        dist = dist + (own[x : x + 1, :] - turned[:, x : x + 1]) ** 2
    bell = jnp.maximum(1.0 - dist * 0.01, 0.0)
    pair = (bell * bell).astype(jnp.bfloat16)
    return jnp.dot(values.astype(jnp.bfloat16), pair, preferred_element_type=jnp.float32)


def is_live(links, dr, dc, r, c):
    return jnp.where(links[SLOT_OF[(dr, dc)], r, c] >= 0, 1.0, 0.0).astype(jnp.float32)


def facing(first, second, axis):
    even = lax.axis_index(axis) % 2 == 0
    return (lambda i: jnp.where(even, second[i], first[i])), (lambda i: jnp.where(even, first[i], second[i]))


def inside_body(strain, coords, links, totals, sv, su, vt, block, weights, src):
    f32, bf16 = jnp.float32, jnp.bfloat16
    other_const, own_const, ones = constant_rows()
    zero8 = jnp.zeros((8, PTS), f32)
    for c in range(EXT_COLS):
        edge = c in (0, EXT_COLS - 1)
        for r in range(ROWS):
            src[pl.ds((c * ROWS + r) * 8, 8), :] = zero8 if edge else ones
            if not edge:
                sv[pl.ds(((c - 1) * ROWS + r) * PIECES + 16, 8), :] = other_const
                sv[pl.ds(((c - 1) * ROWS + r) * PIECES + 24, 8), :] = zero8
    for t in range(TILES):
        su[pl.ds(t * PIECES + 16, 8), :] = own_const
        su[pl.ds(t * PIECES + 24, 8), :] = zero8
    for c in (0, EXT_COLS - 1):
        vt[pl.ds(c * PTS, PTS), :] = jnp.zeros((PTS, PTS), bf16)
    block[...] = jnp.zeros(block.shape, bf16)

    centre = centre_of(coords)
    far = jnp.zeros((COLS, PTS), f32)
    step = ROWS * PIECES
    for r in range(ROWS):
        xyz = [coords[x, r] for x in range(3)]
        a, norm = scaled(xyz, centre)
        far = jnp.maximum(far, norm)
        put_other(sv, a, norm, lambda k: pl.ds(r * PIECES + k, COLS, stride=step))
        put_own(su, a, norm, xyz, lambda k: pl.ds(r * PIECES + k, COLS, stride=step))
        for l in range(LAYERS):
            src[pl.ds((ROWS + r) * 8 + l, COLS, stride=ROWS * 8), :] = strain[l, r]
    near = jnp.max(far) <= SPREAD_LIMIT

    @pl.when(near)
    def _():
        def turn(c, carry):
            vt[rows_at(c + 1, PTS), :] = sv[rows_at(c, step), :].T.astype(bf16)
            return carry

        lax.fori_loop(0, COLS, turn, 0, unroll=8)

        def column(c, carry):
            for j, (o, r) in enumerate(INSIDE):
                own = su[rows_at(c * ROWS + r, PIECES), :]
                block[pl.ds(o * PIECES, PIECES), pl.ds(j * PTS, PTS)] = own.astype(bf16)
            others = vt[rows_at(c, PTS, 3 * PTS), :]
            for j in range(0, len(INSIDE), 2):
                weights[:, j * PTS : (j + 2) * PTS] = bell_weights(others, block[:, j * PTS : (j + 2) * PTS])
            sums = [zero8 for _ in range(ROWS)]
            for j in range(0, len(INSIDE), 2):
                halves = []
                for o, r in INSIDE[j : j + 2]:
                    parts = [src[rows_at((c + dc) * ROWS + o, 8), :] * is_live(links, o - r, dc - 1, r, c) for dc in range(3)]
                    halves.append(jnp.concatenate(parts, axis=1))
                values = jnp.concatenate(halves, axis=0).astype(bf16)
                out = jnp.dot(values, weights[:, j * PTS : (j + 2) * PTS], preferred_element_type=f32)
                for h in range(2):
                    r = INSIDE[j + h][1]
                    sums[r] = sums[r] + out[8 * h : 8 * h + 8, h * PTS : (h + 1) * PTS]
            for r in range(ROWS):
                totals[pl.ds(r * COLS + c, 8, stride=TILES), :] = sums[r]
            return carry

        lax.fori_loop(0, COLS, column, 0, unroll=2)

    @pl.when(jnp.logical_not(near))
    def _():
        def tile(t, carry):
            r, c = t // COLS, t % COLS
            own = su[pl.ds(pl.multiple_of((c * ROWS + r) * PIECES + RAW, 8), 8), :]
            total = zero8
            for (dr, dc), slot in SLOT_OF.items():
                within = (r + dr >= 0) & (r + dr < ROWS) & (c + dc >= 0) & (c + dc < COLS) & (links[slot, r, c] >= 0)
                o = jnp.minimum(jnp.maximum(r + dr, 0), ROWS - 1)
                oc = jnp.minimum(jnp.maximum(c + dc, 0), COLS - 1)
                other = su[pl.ds(pl.multiple_of((oc * ROWS + o) * PIECES + RAW, 8), 8), :]
                values = src[rows_at((oc + 1) * ROWS + o, 8), :] * jnp.where(within, 1.0, 0.0)
                total = total + direct_total(own, other, values)
            totals[pl.ds(t, 8, stride=TILES), :] = total
            return carry

        lax.fori_loop(0, TILES, tile, 0)


def rim_body(
    coords, stiff, links, inside, x_first, x_second, y_first, y_second,
    damage, strength, peak,
    sv, sides, su, vt, vt_sides, block, block_sides, weights, src, raw, totals,
):
    before, after = facing(x_first, x_second, "gx")
    left, right = facing(y_first, y_second, "gy")
    f32, bf16 = jnp.float32, jnp.bfloat16
    gx, gy = lax.axis_index("gx"), lax.axis_index("gy")
    has_top, has_bot = gx > 0, gx < lax.axis_size("gx") - 1
    has_left, has_right = gy > 0, gy < lax.axis_size("gy") - 1
    other_const, own_const, ones = constant_rows()
    zero8 = jnp.zeros((8, PTS), f32)
    totals[...] = inside[...]
    for c in range(EXT_COLS):
        for h in range(2):
            sv[pl.ds(c * PTS + h * PIECES + 16, 8), :] = other_const
            sv[pl.ds(c * PTS + h * PIECES + 24, 8), :] = zero8
            src[pl.ds(((h * LAST) * EXT_COLS + c) * 8, 8), :] = ones
        sv[pl.ds(c * PTS + 64, 64), :] = jnp.zeros((64, PTS), f32)
    for r in range(ROWS):
        for h in range(2):
            sides[pl.ds((h * ROWS + r) * PIECES + 16, 8), :] = other_const
            sides[pl.ds((h * ROWS + r) * PIECES + 24, 8), :] = zero8
            src[pl.ds(((r + 1) * EXT_COLS + h * (EXT_COLS - 1)) * 8, 8), :] = ones
    for t in range(TILES):
        su[pl.ds(t * PIECES + 16, 8), :] = own_const
        su[pl.ds(t * PIECES + 24, 8), :] = zero8
    block[...] = jnp.zeros(block.shape, bf16)
    block_sides[...] = jnp.zeros(block_sides.shape, bf16)

    centre = centre_of(coords)
    far = jnp.zeros((COLS, PTS), f32)
    for r in range(ROWS):
        xyz = [coords[x, r] for x in range(3)]
        a, norm = scaled(xyz, centre)
        far = jnp.maximum(far, norm)
        put_own(su, a, norm, xyz, lambda k: pl.ds(r * PIECES + k, COLS, stride=ROWS * PIECES))
    for h, halo, there in ((0, before, has_top), (1, after, has_bot)):
        xyz = [halo(x) for x in range(3)]
        a, norm = scaled(xyz, centre)
        far = jnp.maximum(far, jnp.where(there, norm, 0.0))
        put_other(sv, a, norm, lambda k: pl.ds(PTS + h * PIECES + k, COLS, stride=PTS))
        first = (h * LAST * EXT_COLS + 1) * 8
        for x in range(3):
            raw[pl.ds(first + x, COLS, stride=8), :] = xyz[x]
        for l in range(LAYERS):
            src[pl.ds(first + l, COLS, stride=8), :] = halo(3 + l)
    rows6 = lax.broadcasted_iota(jnp.int32, (EXT_ROWS, PTS), 0)
    there6 = ((rows6 > 0) | has_top) & ((rows6 < LAST) | has_bot)
    side = jnp.zeros((EXT_ROWS, PTS), f32)
    for h, halo, there in ((0, left, has_left), (1, right, has_right)):
        xyz = [halo(x) for x in range(3)]
        a, norm = scaled(xyz, centre)
        side = jnp.maximum(side, jnp.where(there6 & there, norm, 0.0))
        mid = [v[1:LAST] for v in a]
        put_other(sides, mid, norm[1:LAST], lambda k: pl.ds(h * ROWS * PIECES + k, ROWS, stride=PIECES))
        col = h * (EXT_COLS - 1)
        for e in range(2):
            one = slice(e * LAST, e * LAST + 1)
            put_other(sv, [v[one] for v in a], norm[one], lambda k: pl.ds(col * PTS + e * PIECES + k, 1))
        for x in range(3):
            raw[pl.ds(col * 8 + x, EXT_ROWS, stride=EXT_COLS * 8), :] = xyz[x]
        for l in range(LAYERS):
            src[pl.ds(col * 8 + l, EXT_ROWS, stride=EXT_COLS * 8), :] = halo(3 + l)
    near = jnp.maximum(jnp.max(far), jnp.max(side)) <= SPREAD_LIMIT

    def add(r, c, value):
        at = pl.ds(r * COLS + c, 8, stride=TILES)
        totals[at, :] = totals[at, :] + value

    @pl.when(near)
    def _():
        def turn(c, carry):
            vt[rows_at(c, PTS), :] = sv[rows_at(c, PTS), :].T.astype(bf16)
            return carry

        lax.fori_loop(0, EXT_COLS, turn, 0, unroll=9)
        vt_sides[...] = sides[...].T.astype(bf16)
        for h in range(2):
            for j, (o, r) in enumerate(INSIDE):
                own = su[pl.ds((h * (COLS - 1) * ROWS + r) * PIECES, PIECES), :].astype(bf16)
                block_sides[pl.ds((h * ROWS + o) * PIECES, PIECES), pl.ds((h * len(INSIDE) + j) * PTS, PTS)] = own
        for j in range(0, 2 * len(INSIDE), 2):
            weights[pl.ds(3 * PTS * COLS + (j // 2) * PTS, PTS), :] = bell_weights(
                vt_sides[...], block_sides[:, j * PTS : (j + 2) * PTS]
            )

        def weigh(c, carry):
            for h in range(2):
                own = su[rows_at(c * ROWS + h * (ROWS - 1), PIECES), :].astype(bf16)
                block[rows_at(2 * c + h, PIECES), pl.ds(h * PTS, PTS)] = own
            here = block[rows_at(c, 2 * PIECES), :]
            own = jnp.concatenate([here, jnp.zeros((64, 2 * PTS), bf16)], axis=0)
            weights[rows_at(c, 3 * PTS), :] = bell_weights(vt[rows_at(c, PTS, 3 * PTS), :], own)
            return carry

        lax.fori_loop(0, COLS, weigh, 0, unroll=4)

        def total(c, carry):
            halves = []
            for h in range(2):
                parts = [
                    src[rows_at(h * LAST * EXT_COLS + c + dc, 8), :] * is_live(links, 2 * h - 1, dc - 1, h * (ROWS - 1), c)
                    for dc in range(3)
                ]
                halves.append(jnp.concatenate(parts, axis=1))
            values = jnp.concatenate(halves, axis=0).astype(bf16)
            out = jnp.dot(values, weights[rows_at(c, 3 * PTS), :], preferred_element_type=f32)
            for h in range(2):
                add(h * (ROWS - 1), c, out[8 * h : 8 * h + 8, h * PTS : (h + 1) * PTS])
            return carry

        lax.fori_loop(0, COLS, total, 0, unroll=4)
        sums = [[zero8 for _ in range(ROWS)] for _ in range(2)]
        for j in range(0, 2 * len(INSIDE), 2):
            halves, owners = [], []
            for i in (j, j + 1):
                h, (o, r) = i // len(INSIDE), INSIDE[i % len(INSIDE)]
                held = src[pl.ds(((o + 1) * EXT_COLS + h * (EXT_COLS - 1)) * 8, 8), :]
                halves.append(held * is_live(links, o - r, 2 * h - 1, r, h * (COLS - 1)))
                owners.append((h, r))
            values = jnp.concatenate(halves, axis=0).astype(bf16)
            pair = weights[pl.ds(3 * PTS * COLS + (j // 2) * PTS, PTS), :]
            out = jnp.dot(values, pair, preferred_element_type=f32)
            for i, (h, r) in enumerate(owners):
                sums[h][r] = sums[h][r] + out[8 * i : 8 * i + 8, i * PTS : (i + 1) * PTS]
        for h in range(2):
            for r in range(ROWS):
                add(r, h * (COLS - 1), sums[h][r])

    @pl.when(jnp.logical_not(near))
    def _():
        def tile(t, carry):
            r, c = t // COLS, t % COLS
            own = su[pl.ds(pl.multiple_of((c * ROWS + r) * PIECES + RAW, 8), 8), :]
            for (dr, dc), slot in SLOT_OF.items():
                o, oc = r + dr, c + dc
                within = (o >= 0) & (o < ROWS) & (oc >= 0) & (oc < COLS)

                @pl.when(jnp.logical_not(within) & (links[slot, r, c] >= 0))
                def _():
                    at = rows_at((o + 1) * EXT_COLS + oc + 1, 8)
                    add(r, c, direct_total(own, raw[at, :], src[at, :]))

            return carry

        lax.fori_loop(0, TILES, tile, 0)

    for r in range(ROWS):
        weight_sum = totals[pl.ds(LAYERS * TILES + r * COLS, COLS), :]
        mean = jnp.zeros((COLS, PTS), f32)
        for l in range(LAYERS):
            averaged = totals[pl.ds(l * TILES + r * COLS, COLS), :] / weight_sum
            value = averaged / (averaged + STRAIN_SCALE)
            damage[l, r] = value
            mean = mean + value
        power = (1.0 - mean / LAYERS) * stiff[0, r]
        strength[r] = power
        top = jnp.maximum(top, power) if r else power
    peak[...] = jnp.full(peak.shape, jnp.max(top), f32)


def force_body(
    disp, strength, corners, x_first, x_second, y_first, y_second,
    inner, rim_first, rim_second, rim_left, rim_right,
    edisp, amounts, forces,
):
    f32, bf16 = jnp.float32, jnp.bfloat16
    before, after = facing(x_first, x_second, "gx")
    left, right = facing(y_first, y_second, "gy")
    even = lax.axis_index("gx") % 2 == 0
    forces[...] = jnp.zeros(forces.shape, f32)
    for x in range(3):
        for r in range(EXT_ROWS):
            row = before(8 + x) if r == 0 else after(8 + x) if r == LAST else disp[x, r - 1]
            edisp[pl.ds((x * EXT_ROWS + r) * DISP_COLS + 1, COLS), :] = row
        edisp[pl.ds(x * EXT_ROWS * DISP_COLS, EXT_ROWS, stride=DISP_COLS), :] = left(8 + x)
        edisp[pl.ds(x * EXT_ROWS * DISP_COLS + COLS + 1, EXT_ROWS, stride=DISP_COLS), :] = right(8 + x)

    def gather(r, carry):
        for g in range(COLS // 8):
            power = strength[r, 8 * g : 8 * g + 8, :]
            codes = [corners[k, r, 8 * g : 8 * g + 8, :] for k in range(4)]
            offset = [code >> 7 for code in codes]
            slot = [code & (PTS - 1) for code in codes]
            at = [
                pl.ds(pl.multiple_of(((r * COLS + 8 * g) * 4 + k) * 8, 8) + i, 8, stride=32)
                for k in range(4) for i in range(8)
            ]
            for k in range(4):
                amounts[at[8 * k + 3], :] = offset[k].astype(f32)
                amounts[at[8 * k + 7], :] = slot[k].astype(f32)
            for x in range(3):
                picked = []
                base = (x * EXT_ROWS + r) * DISP_COLS + 8 * g
                table = [edisp[pl.ds(base + (o // 3) * DISP_COLS + o % 3, 8), :] for o in range(9)]
                for k in range(4):
                    found = jnp.take_along_axis(table[0], slot[k], axis=1)
                    for o in range(1, 9):
                        found = jnp.where(offset[k] == o, jnp.take_along_axis(table[o], slot[k], axis=1), found)
                    picked.append(found)
                springs = [power * (picked[(k + 1) % 4] - picked[k]) for k in range(4)]
                for k in range(4):
                    amount = springs[k] - springs[(k + 3) % 4]
                    hi = amount.astype(bf16).astype(f32)
                    amounts[at[8 * k + x], :] = hi
                    amounts[at[8 * k + 4 + x], :] = amount - hi
        return carry

    lax.fori_loop(0, ROWS, gather, 0, unroll=2)

    nodes = lax.broadcasted_iota(jnp.int32, (PTS, PTS), 0).astype(f32)

    def scatter(t, carry):
        r, c = t // COLS, t % COLS
        picks, rows = [], []
        for k in range(4):
            own = amounts[pl.ds(pl.multiple_of((t * 4 + k) * 8, 8), 8), :]
            offset, slot = own[3:4, :], own[7:8, :]
            rows.append(jnp.concatenate([jnp.where(offset == float(o), own, 0.0) for o in range(10)], axis=0))
            picks.append(jnp.where(slot == nodes, 1.0, 0.0).astype(bf16))
        left_side = jnp.concatenate(rows, axis=1).astype(bf16)
        right_side = jnp.concatenate(picks, axis=1)
        out = lax.dot_general(left_side, right_side, (((1,), (1,)), ((), ())), preferred_element_type=f32)
        for o in range(9):
            at = pl.ds(pl.multiple_of(((r + o // 3) * EXT_COLS + c + o % 3) * 8, 8), 8)
            forces[at, :] = forces[at, :] + out[8 * o : 8 * o + 8]
        return carry

    lax.fori_loop(0, ROWS * COLS, scatter, 0, unroll=8)

    def node_sum(x, first, count, stride):
        return (
            forces[pl.ds(first * 8 + x, count, stride=8 * stride), :]
            + forces[pl.ds(first * 8 + 4 + x, count, stride=8 * stride), :]
        )

    for x in range(3):
        for r in range(ROWS):
            inner[x, r] = node_sum(x, (r + 1) * EXT_COLS + 1, COLS, 1)
        top = node_sum(x, 0, EXT_COLS, 1)
        bottom = node_sum(x, LAST * EXT_COLS, EXT_COLS, 1)
        rim_first[x] = jnp.where(even, bottom, top)
        rim_second[x] = jnp.where(even, top, bottom)
        rim_left[x] = node_sum(x, EXT_COLS, ROWS, EXT_COLS)
        rim_right[x] = node_sum(x, 2 * EXT_COLS - 1, ROWS, EXT_COLS)


def finish_body(inner, x_first, x_second, y_first, y_second, peaks, out):
    before, after = facing(x_first, x_second, "gx")
    left, right = facing(y_first, y_second, "gy")
    top = jnp.max(peaks[...])
    cols = lax.broadcasted_iota(jnp.int32, (COLS, PTS), 0)
    for x in range(3):
        west, east = left(x), right(x)
        for r in range(ROWS):
            value = inner[x, r]
            if r == 0:
                value = value + before(x)[1 : COLS + 1]
            if r == ROWS - 1:
                value = value + after(x)[1 : COLS + 1]
            value = value + jnp.where(cols == 0, west[r : r + 1], 0.0) + jnp.where(cols == COLS - 1, east[r : r + 1], 0.0)
            out[x, r] = value / top


def kernels(peers):
    f32, bf16 = jnp.float32, jnp.bfloat16
    vmem = pl.BlockSpec(memory_space=pltpu.VMEM)
    smem = pl.BlockSpec(memory_space=pltpu.SMEM)

    def call(body, name, ins, outs, scratch, flops):
        return pl.pallas_call(
            body,
            out_shape=tuple(jax.ShapeDtypeStruct(*o) for o in outs),
            in_specs=[smem if i == "links" else vmem for i in ins],
            out_specs=(vmem,) * len(outs),
            scratch_shapes=[pltpu.VMEM(*v) for v in scratch],
            compiler_params=pltpu.CompilerParams(vmem_limit_bytes=40 * MIB),
            cost_estimate=pl.CostEstimate(flops=flops, bytes_accessed=MIB, transcendentals=0),
            name=name,
        )

    inside = call(
        inside_body,
        "inside_links",
        ("strain", "coords", "links"),
        [((8 * TILES, PTS), f32)],
        [
            ((TILES * PIECES, PTS), f32),
            ((TILES * PIECES, PTS), f32),
            ((EXT_COLS * PTS, PTS), bf16),
            ((PTS, len(INSIDE) * PTS), bf16),
            ((3 * PTS, len(INSIDE) * PTS), bf16),
            ((EXT_COLS * ROWS * 8, PTS), f32),
        ],
        8 * 10**9,
    )
    rim = call(
        rim_body,
        "rim_links",
        ("coords", "stiff", "links", "inside", "x_first", "x_second", "y_first", "y_second"),
        [((LAYERS, ROWS, COLS, PTS), f32), ((ROWS, COLS, PTS), f32), ((peers, PTS), f32)],
        [
            ((EXT_COLS * PTS, PTS), f32),
            ((2 * PTS, PTS), f32),
            ((TILES * PIECES, PTS), f32),
            ((EXT_COLS * PTS, PTS), bf16),
            ((PTS, 2 * PTS), bf16),
            ((COLS * 2 * PIECES, 2 * PTS), bf16),
            ((2 * PTS, 2 * len(INSIDE) * PTS), bf16),
            ((3 * PTS * COLS + len(INSIDE) * PTS, 2 * PTS), bf16),
            ((EXT_ROWS * EXT_COLS * 8, PTS), f32),
            ((EXT_ROWS * EXT_COLS * 8, PTS), f32),
            ((8 * TILES, PTS), f32),
        ],
        4 * 10**9,
    )
    force = call(
        force_body,
        "node_forces",
        ("disp", "strength", "corners", "x_first", "x_second", "y_first", "y_second"),
        [
            ((3, ROWS, COLS, PTS), f32),
            ((3, EXT_COLS, PTS), f32),
            ((3, EXT_COLS, PTS), f32),
            ((3, ROWS, PTS), f32),
            ((3, ROWS, PTS), f32),
        ],
        [
            ((3 * EXT_ROWS * DISP_COLS, PTS), f32),
            ((TILES * 32, PTS), f32),
            ((EXT_ROWS * EXT_COLS * 8, PTS), f32),
        ],
        8 * 10**9,
    )
    finish = call(
        finish_body,
        "finish",
        ("inner", "x_first", "x_second", "y_first", "y_second", "peaks"),
        [((3, ROWS, COLS, PTS), f32)],
        [],
        10**6,
    )
    return inside, rim, force, finish


def swap(first, second, axis):
    peers = lax.axis_size(axis)
    with_first = [(i, i ^ 1) for i in range(peers)]
    with_second = [(i, ((i - 1) ^ 1) + 1) for i in range(1, peers - 1)]
    return lax.ppermute(first, axis, with_first), lax.ppermute(second, axis, with_second)


def local(strain, coords, displacement, stiffness, neighbours, corners):
    peers_x, peers_y = lax.axis_size("gx"), lax.axis_size("gy")
    even_x, even_y = lax.axis_index("gx") % 2 == 0, lax.axis_index("gy") % 2 == 0
    own = (coords, strain, displacement)

    def take(value, index, dim):
        return lax.dynamic_index_in_dim(value, index, dim, keepdims=False)

    def row(r):
        return jnp.concatenate([take(v, r, 1) for v in own], axis=0)

    inside, rim, force, finish = kernels(peers_x)
    x_halos = swap(row(jnp.where(even_x, ROWS - 1, 0)), row(jnp.where(even_x, 0, ROWS - 1)), "gx")
    above = jnp.where(even_x, x_halos[1], x_halos[0])
    below = jnp.where(even_x, x_halos[0], x_halos[1])

    def column(c):
        mid = jnp.concatenate([take(v, c, 2) for v in own], axis=0)
        return jnp.concatenate([take(above, c, 1)[:, None], mid, take(below, c, 1)[:, None]], axis=1)

    y_halos = swap(column(jnp.where(even_y, COLS - 1, 0)), column(jnp.where(even_y, 0, COLS - 1)), "gy")
    totals = inside(strain, coords, neighbours)[0]
    damage, strength, peak = rim(coords, stiffness, neighbours, totals, *x_halos, *y_halos)
    peaks = lax.all_to_all(peak, "gx", 0, 0, tiled=True)
    inner, rim_first, rim_second, rim_left, rim_right = force(displacement, strength, corners, *x_halos, *y_halos)
    x_rims = swap(rim_first, rim_second, "gx")
    *x_rims, peaks = lax.optimization_barrier((*x_rims, peaks))
    peaks = jnp.broadcast_to(jnp.max(peaks, axis=0, keepdims=True), (peers_y, PTS))
    peaks = lax.all_to_all(peaks, "gy", 0, 0, tiled=True)
    above = jnp.where(even_x, x_rims[1], x_rims[0])
    below = jnp.where(even_x, x_rims[0], x_rims[1])

    def side(rim_side, c):
        return rim_side.at[:, 0].add(above[:, c]).at[:, ROWS - 1].add(below[:, c])

    west, east = side(rim_left, 0), side(rim_right, EXT_COLS - 1)
    y_rims = swap(jnp.where(even_y, east, west), jnp.where(even_y, west, east), "gy")
    return damage, finish(inner, *x_rims, *y_rims, peaks)[0]


def solution(mesh):
    spec = P(None, "gx", "gy", None)
    in_specs = (spec, spec, spec, spec, P(None, "gx", "gy"), spec)
    return jax.shard_map(local, mesh=mesh, in_specs=in_specs, out_specs=(spec, spec), check_vma=False)
```

time: 93.4 us -> 83.7 us (0.90)
  the two profiles are of different devices: /device:TPU:40 before, /device:TPU:38 now
where the time goes in v2:
time: 83.7 us; the launch traced here: 83.2 us
  starting transfers between devices  45.9 us (55%)
  Pallas kernels  23.3 us (28%)
  waiting for transfers between devices  11.2 us (13%)
  local copies, waits for them, and re-layouts  1.78 us (2%)
  between operations  0.93 us (1%)
    ppermute x4, starting transfers between devices, swap(): lax.ppermute(second, axis, with_second)  18.5 us
    all_to_all x1, starting transfers between devices, local(): peaks = lax.all_to_all(peaks, 'gy', 0, 0, tiled=True)  11 us
    pallas_call x1, Pallas kernels, local(): totals = inside(strain, coords, neighbours)[0]  10.6 us
    ppermute x4, waiting for transfers between devices, swap(): lax.ppermute(second, axis, with_second)  9.93 us
    ppermute x4, starting transfers between devices, swap(): lax.ppermute(first, axis, with_first)  8.77 us
    all_to_all x1, starting transfers between devices, local(): peaks = lax.all_to_all(peak, 'gx', 0, 0, tiled=True)  7.52 us
    pallas_call x1, Pallas kernels, local(): rim(coords, stiffness, neighbours, totals, *x_halos, *y_halos)  6.26 us
    pallas_call x1, Pallas kernels, local(): force(displacement, strength, corners, *x_halos, *y_halos)  5.64 us
  transfers between devices with their start and end apart: 10, of which 4 were waited for; matrix products, arithmetic and copies ran while one was open for 0% of the time, Pallas kernels for 20%

profile of v2, /device:TPU:38, one launch (start us, length us, event | category | flops | bytes accessed | tf_op | source)
XLA Modules:
  0.0 83.2 jit_solution(495945619626994932)
XLA Ops:
  0.6 0.0 copy-start.2
  0.6 0.0 copy-start.1
  0.7 0.9 %dynamic-slice_bitcast_fusion = (f32[5,16,128]{2,1,0:T(8,128)S(1)}, f32[5,16,128]{2,1,0:T(8,128)S(1)}) fusion(f32[5,4,16,128]{3,2,1,0:T(8,128)} %strain.1, s32[]{:T(128)S(6)} %select_n.83, s32[]{:T(128)S(6)} %select_n.82), kind=kLoop, calls=%fused_computation.6 | loop fusion | bytes 163848 | tf_op jit(solution)/shard_map/jit(dynamic_index_in_dim)/squeeze | solution.py:541
  1.5 0.0 copy-done.2
  1.5 0.0 copy-done.1
  1.6 0.0 copy-start
  1.6 2.1 %collective-permute-start = (f32[11,16,128]{2,1,0:T(8,128)S(1)}, f32[11,16,128]{2,1,0:T(8,128)S(1)}, u32[]{:S(2)}, u32[]{:S(2)}) collective-permute-start(f32[11,16,128]{2,1,0:T(8,128)S(1)} %pad_maximum_fusion), channel_id=1, source_target_pairs={{0,16},{16,0},{32,48},{48,32},{64,80},{80,64},{96,112},{112,96},{1... | collective-permute-start | bytes 270344 | tf_op jit(solution)/shard_map/ppermute | solution.py:532
  3.7 4.3 %collective-permute-start.1 = (f32[11,16,128]{2,1,0:T(8,128)S(1)}, f32[11,16,128]{2,1,0:T(8,128)S(1)}, u32[]{:S(2)}, u32[]{:S(2)}) collective-permute-start(f32[11,16,128]{2,1,0:T(8,128)S(1)} %pad_maximum_fusion.1), channel_id=1, source_target_pairs={{16,32},{32,16},{48,64},{64,48},{80,96},{96,80},{112,128},{128,112... | collective-permute-start | bytes 270344 | tf_op jit(solution)/shard_map/ppermute | solution.py:532
  8.0 0.0 copy-done
  8.1 0.0 collective-permute-done.x_first
  8.1 3.6 %collective-permute-done.1.x_second = f32[11,16,128]{2,1,0:T(8,128)S(1)} collective-permute-done((f32[11,16,128]{2,1,0:T(8,128)S(1)}, f32[11,16,128]{2,1,0:T(8,128)S(1)}, u32[]{:S(2)}, u32[]{:S(2)}) %collective-permute-start.1) | collective-permute-done | bytes 90144 | tf_op jit(solution)/shard_map/ppermute | solution.py:532
  11.7 2.7 %collective-permute-start.2 = (f32[11,6,128]{2,1,0:T(8,128)S(1)}, f32[11,6,128]{2,1,0:T(8,128)S(1)}, u32[]{:S(2)}, u32[]{:S(2)}) collective-permute-start(f32[11,6,128]{2,1,0:T(8,128)S(1)} %pad_maximum_fusion.2), channel_id=1, source_target_pairs={{0,1},{1,0},{2,3},{3,2},{4,5},{5,4},{6,7},{7,6},{8,9},{9,8},{10,11... | collective-permute-start | bytes 101384 | tf_op jit(solution)/shard_map/ppermute | solution.py:532
  14.5 0.0 copy-start.5
  14.5 0.0 copy-start.4
  14.5 6.7 %collective-permute-start.3 = (f32[11,6,128]{2,1,0:T(8,128)S(1)}, f32[11,6,128]{2,1,0:T(8,128)S(1)}, u32[]{:S(2)}, u32[]{:S(2)}) collective-permute-start(f32[11,6,128]{2,1,0:T(8,128)S(1)} %pad_maximum_fusion.3), channel_id=1, source_target_pairs={{1,2},{2,1},{3,4},{4,3},{5,6},{6,5},{7,8},{8,7},{9,10},{10,9},{11,... | collective-permute-start | bytes 101384 | tf_op jit(solution)/shard_map/ppermute | solution.py:532
  21.2 0.0 copy-done.5
  21.2 10.6 %inside_links.1.inside = f32[512,128]{1,0:T(8,128)S(1)} custom-call(f32[5,4,16,128]{3,2,1,0:T(8,128)S(1)} %copy-done, f32[3,4,16,128]{3,2,1,0:T(8,128)S(1)} %copy-done.1, s32[9,4,16]{2,1,0:T(4,128)S(1)} %copy-done.5), custom_call_target="tpu_custom_call" | custom-call | flops 8000000000 | bytes 1048576 | tf_op jit(solution)/shard_map/inside_links/pallas_call | solution.py:556
  31.9 0.0 copy-start.3
  31.9 0.0 collective-permute-done.2.y_first
  31.9 0.0 collective-permute-done.3.y_second
  31.9 0.0 copy-done.4
  31.9 6.3 %rim_links.1 = (f32[5,4,16,128]{3,2,1,0:T(8,128)}, f32[4,16,128]{2,1,0:T(8,128)S(1)}, f32[32,128]{1,0:T(8,128)}) custom-call(f32[3,4,16,128]{3,2,1,0:T(8,128)S(1)} %copy-done.1, f32[1,4,16,128]{3,2,1,0:T(8,128)S(1)} %copy-done.4, s32[9,4,16]{2,1,0:T(4,128)S(1)} %copy-done.5, f32[512,128]{1,0:T(8,128)S(1)} %inside_links.1.inside, ...), custom_call_target="tpu_custom_call" | custom-call | flops 4000000000 | bytes 1048576 | tf_op jit(solution)/shard_map/rim_links/pallas_call | solution.py:557
  38.2 7.5 %all-to-all-start = ((f32[32,1,128]{2,1,0:T(1,128)}), f32[32,1,128]{2,1,0:T(1,128)S(1)}, u32[]{:S(2)}, u32[]{:S(2)}) async-start(f32[32,1,128]{2,1,0:T(1,128)} %bitcast.13), calls=%async_computation | async-start | bytes 32768 | tf_op jit(solution)/shard_map/all_to_all | solution.py:558
  45.7 0.0 copy-done.3
  45.7 5.6 %node_forces.1 = (f32[3,4,16,128]{3,2,1,0:T(8,128)S(1)}, f32[3,18,128]{2,1,0:T(8,128)S(1)}, f32[3,18,128]{2,1,0:T(8,128)S(1)}, f32[3,4,128]{2,1,0:T(4,128)S(1)}, f32[3,4,128]{2,1,0:T(4,128)S(1)}) custom-call(f32[3,4,16,128]{3,2,1,0:T(8,128)S(1)} %copy-done.2, f32[4,16,128]{2,1,0:T(8,128)S(1)} %get-tuple-element.62.strength, s32[4,4,16,128]{3,2,1,0:T(8,128)S(1)} %copy-done.3, ...), custom_call_target="tpu_custom_call" | custom-call | flops 8000000000 | bytes 1048576 | tf_op jit(solution)/shard_map/node_forces/pallas_call | solution.py:559
  51.4 2.1 %collective-permute-start.4 = (f32[3,18,128]{2,1,0:T(8,128)S(1)}, f32[3,18,128]{2,1,0:T(8,128)S(1)}, u32[]{:S(2)}, u32[]{:S(2)}) collective-permute-start(f32[3,18,128]{2,1,0:T(8,128)S(1)} %get-tuple-element.64), channel_id=1, source_target_pairs={{0,16},{16,0},{32,48},{48,32},{64,80},{80,64},{96,112},{112,96},{1... | collective-permute-start | bytes 82952 | tf_op jit(solution)/shard_map/ppermute | solution.py:532
  53.4 3.3 %collective-permute-start.5 = (f32[3,18,128]{2,1,0:T(8,128)S(1)}, f32[3,18,128]{2,1,0:T(8,128)S(1)}, u32[]{:S(2)}, u32[]{:S(2)}) collective-permute-start(f32[3,18,128]{2,1,0:T(8,128)S(1)} %get-tuple-element.65), channel_id=1, source_target_pairs={{16,32},{32,16},{48,64},{64,48},{80,96},{96,80},{112,128},{128,112... | collective-permute-start | bytes 82952 | tf_op jit(solution)/shard_map/ppermute | solution.py:532
  56.8 0.0 collective-permute-done.4.x_first
  56.8 4.0 %collective-permute-done.5.x_second = f32[3,18,128]{2,1,0:T(8,128)S(1)} collective-permute-done((f32[3,18,128]{2,1,0:T(8,128)S(1)}, f32[3,18,128]{2,1,0:T(8,128)S(1)}, u32[]{:S(2)}, u32[]{:S(2)}) %collective-permute-start.5) | collective-permute-done | bytes 27680 | tf_op jit(solution)/shard_map/ppermute | solution.py:532
  60.8 0.0 all-to-all-done
  60.8 0.6 broadcast_in_dim.2
  61.5 11.0 %all-to-all-start.1 = ((f32[16,1,128]{2,1,0:T(1,128)}), f32[16,1,128]{2,1,0:T(1,128)S(1)}, u32[]{:S(2)}, u32[]{:S(2)}) async-start(f32[16,1,128]{2,1,0:T(1,128)} %broadcast_in_dim.2), calls=%async_computation.1 | async-start | bytes 16384 | tf_op jit(solution)/shard_map/all_to_all | solution.py:563
  72.7 4.3 %collective-permute-start.7 = (f32[3,4,128]{2,1,0:T(4,128)S(1)}, f32[3,4,128]{2,1,0:T(4,128)S(1)}, u32[]{:S(2)}, u32[]{:S(2)}) collective-permute-start(f32[3,4,128]{2,1,0:T(4,128)S(1)} %get-tuple-element.96), channel_id=1, source_target_pairs={{1,2},{2,1},{3,4},{4,3},{5,6},{6,5},{7,8},{8,7},{9,10},{10,9},{11,... | collective-permute-start | bytes 18440 | tf_op jit(solution)/shard_map/ppermute | solution.py:532
  76.9 1.9 %collective-permute-start.6 = (f32[3,4,128]{2,1,0:T(4,128)S(1)}, f32[3,4,128]{2,1,0:T(4,128)S(1)}, u32[]{:S(2)}, u32[]{:S(2)}) collective-permute-start(f32[3,4,128]{2,1,0:T(4,128)S(1)} %get-tuple-element.97), channel_id=1, source_target_pairs={{0,1},{1,0},{2,3},{3,2},{4,5},{5,4},{6,7},{7,6},{8,9},{9,8},{10,11... | collective-permute-start | bytes 18440 | tf_op jit(solution)/shard_map/ppermute | solution.py:532
  78.9 2.3 %collective-permute-done.7.y_second = f32[3,4,128]{2,1,0:T(4,128)S(1)} collective-permute-done((f32[3,4,128]{2,1,0:T(4,128)S(1)}, f32[3,4,128]{2,1,0:T(4,128)S(1)}, u32[]{:S(2)}, u32[]{:S(2)}) %collective-permute-start.7) | collective-permute-done | bytes 6176 | tf_op jit(solution)/shard_map/ppermute | solution.py:532
  81.2 1.3 %collective-permute-done.6.y_first = f32[3,4,128]{2,1,0:T(4,128)S(1)} collective-permute-done((f32[3,4,128]{2,1,0:T(4,128)S(1)}, f32[3,4,128]{2,1,0:T(4,128)S(1)}, u32[]{:S(2)}, u32[]{:S(2)}) %collective-permute-start.6) | collective-permute-done | bytes 6176 | tf_op jit(solution)/shard_map/ppermute | solution.py:532
  82.5 0.0 all-to-all-done.1
  82.5 0.8 finish.1
  (19 shorter events, 0.4 us)
Async XLA Ops:
  0.6 0.9 %copy-start.2 = (f32[3,4,16,128]{3,2,1,0:T(8,128)S(1)}, f32[3,4,16,128]{3,2,1,0:T(8,128)}, u32[]{:S(2)}) copy-start(f32[3,4,16,128]{3,2,1,0:T(8,128)} %disp.1) | copy-start | bytes 294916
  0.6 0.9 %copy-start.1 = (f32[3,4,16,128]{3,2,1,0:T(8,128)S(1)}, f32[3,4,16,128]{3,2,1,0:T(8,128)}, u32[]{:S(2)}) copy-start(f32[3,4,16,128]{3,2,1,0:T(8,128)} %coords.3) | copy-start | bytes 294916
  1.6 6.4 %copy-start = (f32[5,4,16,128]{3,2,1,0:T(8,128)S(1)}, f32[5,4,16,128]{3,2,1,0:T(8,128)}, u32[]{:S(2)}) copy-start(f32[5,4,16,128]{3,2,1,0:T(8,128)} %strain.1) | copy-start | bytes 491524
  1.6 6.5 %collective-permute-start = (f32[11,16,128]{2,1,0:T(8,128)S(1)}, f32[11,16,128]{2,1,0:T(8,128)S(1)}, u32[]{:S(2)}, u32[]{:S(2)}) collective-permute-start(f32[11,16,128]{2,1,0:T(8,128)S(1)} %pad_maximum_fusion), channel_id=1, source_target_pairs={{0,16},{16,0},{32,48},{48,32},{64,80},{80,64},{96,112},{112,96},{1... | collective-permute-start | bytes 270344 | tf_op jit(solution)/shard_map/ppermute | solution.py:532
  3.7 8.0 %collective-permute-start.1 = (f32[11,16,128]{2,1,0:T(8,128)S(1)}, f32[11,16,128]{2,1,0:T(8,128)S(1)}, u32[]{:S(2)}, u32[]{:S(2)}) collective-permute-start(f32[11,16,128]{2,1,0:T(8,128)S(1)} %pad_maximum_fusion.1), channel_id=1, source_target_pairs={{16,32},{32,16},{48,64},{64,48},{80,96},{96,80},{112,128},{128,112... | collective-permute-start | bytes 270344 | tf_op jit(solution)/shard_map/ppermute | solution.py:532
  11.7 20.2 %collective-permute-start.2 = (f32[11,6,128]{2,1,0:T(8,128)S(1)}, f32[11,6,128]{2,1,0:T(8,128)S(1)}, u32[]{:S(2)}, u32[]{:S(2)}) collective-permute-start(f32[11,6,128]{2,1,0:T(8,128)S(1)} %pad_maximum_fusion.2), channel_id=1, source_target_pairs={{0,1},{1,0},{2,3},{3,2},{4,5},{5,4},{6,7},{7,6},{8,9},{9,8},{10,11... | collective-permute-start | bytes 101384 | tf_op jit(solution)/shard_map/ppermute | solution.py:532
  14.5 6.7 %copy-start.5 = (s32[9,4,16]{2,1,0:T(4,128)S(1)}, s32[9,4,16]{2,1,0:T(4,128)}, u32[]{:S(2)}) copy-start(s32[9,4,16]{2,1,0:T(4,128)} %links.3) | copy-start | bytes 6916
  14.5 17.4 %copy-start.4 = (f32[1,4,16,128]{3,2,1,0:T(8,128)S(1)}, f32[1,4,16,128]{3,2,1,0:T(8,128)}, u32[]{:S(2)}) copy-start(f32[1,4,16,128]{3,2,1,0:T(8,128)} %stiff.1) | copy-start | bytes 98308
  14.5 17.4 %collective-permute-start.3 = (f32[11,6,128]{2,1,0:T(8,128)S(1)}, f32[11,6,128]{2,1,0:T(8,128)S(1)}, u32[]{:S(2)}, u32[]{:S(2)}) collective-permute-start(f32[11,6,128]{2,1,0:T(8,128)S(1)} %pad_maximum_fusion.3), channel_id=1, source_target_pairs={{1,2},{2,1},{3,4},{4,3},{5,6},{6,5},{7,8},{8,7},{9,10},{10,9},{11,... | collective-permute-start | bytes 101384 | tf_op jit(solution)/shard_map/ppermute | solution.py:532
  31.9 13.8 %copy-start.3 = (s32[4,4,16,128]{3,2,1,0:T(8,128)S(1)}, s32[4,4,16,128]{3,2,1,0:T(8,128)}, u32[]{:S(2)}) copy-start(s32[4,4,16,128]{3,2,1,0:T(8,128)} %corners.1) | copy-start | bytes 393220
  38.2 22.6 %all-to-all-start = ((f32[32,1,128]{2,1,0:T(1,128)}), f32[32,1,128]{2,1,0:T(1,128)S(1)}, u32[]{:S(2)}, u32[]{:S(2)}) async-start(f32[32,1,128]{2,1,0:T(1,128)} %bitcast.13), calls=%async_computation | async-start | bytes 32768 | tf_op jit(solution)/shard_map/all_to_all | solution.py:558
  51.4 5.4 %collective-permute-start.4 = (f32[3,18,128]{2,1,0:T(8,128)S(1)}, f32[3,18,128]{2,1,0:T(8,128)S(1)}, u32[]{:S(2)}, u32[]{:S(2)}) collective-permute-start(f32[3,18,128]{2,1,0:T(8,128)S(1)} %get-tuple-element.64), channel_id=1, source_target_pairs={{0,16},{16,0},{32,48},{48,32},{64,80},{80,64},{96,112},{112,96},{1... | collective-permute-start | bytes 82952 | tf_op jit(solution)/shard_map/ppermute | solution.py:532
  53.4 7.4 %collective-permute-start.5 = (f32[3,18,128]{2,1,0:T(8,128)S(1)}, f32[3,18,128]{2,1,0:T(8,128)S(1)}, u32[]{:S(2)}, u32[]{:S(2)}) collective-permute-start(f32[3,18,128]{2,1,0:T(8,128)S(1)} %get-tuple-element.65), channel_id=1, source_target_pairs={{16,32},{32,16},{48,64},{64,48},{80,96},{96,80},{112,128},{128,112... | collective-permute-start | bytes 82952 | tf_op jit(solution)/shard_map/ppermute | solution.py:532
  61.5 21.0 %all-to-all-start.1 = ((f32[16,1,128]{2,1,0:T(1,128)}), f32[16,1,128]{2,1,0:T(1,128)S(1)}, u32[]{:S(2)}, u32[]{:S(2)}) async-start(f32[16,1,128]{2,1,0:T(1,128)} %broadcast_in_dim.2), calls=%async_computation.1 | async-start | bytes 16384 | tf_op jit(solution)/shard_map/all_to_all | solution.py:563
  72.7 8.5 %collective-permute-start.7 = (f32[3,4,128]{2,1,0:T(4,128)S(1)}, f32[3,4,128]{2,1,0:T(4,128)S(1)}, u32[]{:S(2)}, u32[]{:S(2)}) collective-permute-start(f32[3,4,128]{2,1,0:T(4,128)S(1)} %get-tuple-element.96), channel_id=1, source_target_pairs={{1,2},{2,1},{3,4},{4,3},{5,6},{6,5},{7,8},{8,7},{9,10},{10,9},{11,... | collective-permute-start | bytes 18440 | tf_op jit(solution)/shard_map/ppermute | solution.py:532
  76.9 5.5 %collective-permute-start.6 = (f32[3,4,128]{2,1,0:T(4,128)S(1)}, f32[3,4,128]{2,1,0:T(4,128)S(1)}, u32[]{:S(2)}, u32[]{:S(2)}) collective-permute-start(f32[3,4,128]{2,1,0:T(4,128)S(1)} %get-tuple-element.97), channel_id=1, source_target_pairs={{0,1},{1,0},{2,3},{3,2},{4,5},{5,4},{6,7},{7,6},{8,9},{9,8},{10,11... | collective-permute-start | bytes 18440 | tf_op jit(solution)/shard_map/ppermute | solution.py:532

commit v3 on v2

--- a/solution.py
+++ b/solution.py
@@ -96,7 +96,7 @@
     return (lambda i: jnp.where(even, second[i], first[i])), (lambda i: jnp.where(even, first[i], second[i]))
 
 
-def inside_body(strain, coords, links, totals, sv, su, vt, block, weights, src):
+def split_body(strain, coords, su, vt, src, info, sv):
     f32, bf16 = jnp.float32, jnp.bfloat16
     other_const, own_const, ones = constant_rows()
     zero8 = jnp.zeros((8, PTS), f32)
@@ -112,7 +112,6 @@
         su[pl.ds(t * PIECES + 24, 8), :] = zero8
     for c in (0, EXT_COLS - 1):
         vt[pl.ds(c * PTS, PTS), :] = jnp.zeros((PTS, PTS), bf16)
-    block[...] = jnp.zeros(block.shape, bf16)
 
     centre = centre_of(coords)
     far = jnp.zeros((COLS, PTS), f32)
@@ -125,16 +124,26 @@
         put_own(su, a, norm, xyz, lambda k: pl.ds(r * PIECES + k, COLS, stride=step))
         for l in range(LAYERS):
             src[pl.ds((ROWS + r) * 8 + l, COLS, stride=ROWS * 8), :] = strain[l, r]
-    near = jnp.max(far) <= SPREAD_LIMIT
+    info[...] = jnp.zeros(info.shape, f32)
+    for x in range(3):
+        info[x : x + 1] = jnp.full((1, PTS), centre[x], f32)
+    info[3:4] = jnp.max(far, axis=0, keepdims=True)
+
+    def turn(c, carry):
+        vt[rows_at(c + 1, PTS), :] = sv[rows_at(c, step), :].T.astype(bf16)
+        return carry
+
+    lax.fori_loop(0, COLS, turn, 0, unroll=8)
+
+
+def inside_body(links, su, vt, src, info, totals, block, weights):
+    f32, bf16 = jnp.float32, jnp.bfloat16
+    zero8 = jnp.zeros((8, PTS), f32)
+    block[...] = jnp.zeros(block.shape, bf16)
+    near = jnp.max(info[3:4]) <= SPREAD_LIMIT
 
     @pl.when(near)
     def _():
-        def turn(c, carry):
-            vt[rows_at(c + 1, PTS), :] = sv[rows_at(c, step), :].T.astype(bf16)
-            return carry
-
-        lax.fori_loop(0, COLS, turn, 0, unroll=8)
-
         def column(c, carry):
             for j, (o, r) in enumerate(INSIDE):
                 own = su[rows_at(c * ROWS + r, PIECES), :]
@@ -157,7 +166,7 @@
                 totals[pl.ds(r * COLS + c, 8, stride=TILES), :] = sums[r]
             return carry
 
-        lax.fori_loop(0, COLS, column, 0, unroll=2)
+        lax.fori_loop(0, COLS, column, 0, unroll=4)
 
     @pl.when(jnp.logical_not(near))
     def _():
@@ -179,9 +188,9 @@
 
 
 def rim_body(
-    coords, stiff, links, inside, x_first, x_second, y_first, y_second,
+    stiff, links, inside, su, info, x_first, x_second, y_first, y_second,
     damage, strength, peak,
-    sv, sides, su, vt, vt_sides, block, block_sides, weights, src, raw, totals,
+    sv, sides, vt, vt_sides, block, block_sides, weights, src, raw, totals,
 ):
     before, after = facing(x_first, x_second, "gx")
     left, right = facing(y_first, y_second, "gy")
@@ -189,7 +198,7 @@
     gx, gy = lax.axis_index("gx"), lax.axis_index("gy")
     has_top, has_bot = gx > 0, gx < lax.axis_size("gx") - 1
     has_left, has_right = gy > 0, gy < lax.axis_size("gy") - 1
-    other_const, own_const, ones = constant_rows()
+    other_const, _, ones = constant_rows()
     zero8 = jnp.zeros((8, PTS), f32)
     totals[...] = inside[...]
     for c in range(EXT_COLS):
@@ -203,19 +212,11 @@
             sides[pl.ds((h * ROWS + r) * PIECES + 16, 8), :] = other_const
             sides[pl.ds((h * ROWS + r) * PIECES + 24, 8), :] = zero8
             src[pl.ds(((r + 1) * EXT_COLS + h * (EXT_COLS - 1)) * 8, 8), :] = ones
-    for t in range(TILES):
-        su[pl.ds(t * PIECES + 16, 8), :] = own_const
-        su[pl.ds(t * PIECES + 24, 8), :] = zero8
     block[...] = jnp.zeros(block.shape, bf16)
     block_sides[...] = jnp.zeros(block_sides.shape, bf16)
 
-    centre = centre_of(coords)
-    far = jnp.zeros((COLS, PTS), f32)
-    for r in range(ROWS):
-        xyz = [coords[x, r] for x in range(3)]
-        a, norm = scaled(xyz, centre)
-        far = jnp.maximum(far, norm)
-        put_own(su, a, norm, xyz, lambda k: pl.ds(r * PIECES + k, COLS, stride=ROWS * PIECES))
+    centre = [info[x : x + 1, :] for x in range(3)]
+    far = jnp.broadcast_to(info[3:4, :], (COLS, PTS))
     for h, halo, there in ((0, before, has_top), (1, after, has_bot)):
         xyz = [halo(x) for x in range(3)]
         a, norm = scaled(xyz, centre)
@@ -408,7 +409,7 @@
             forces[at, :] = forces[at, :] + out[8 * o : 8 * o + 8]
         return carry
 
-    lax.fori_loop(0, ROWS * COLS, scatter, 0, unroll=8)
+    lax.fori_loop(0, ROWS * COLS, scatter, 0, unroll=16)
 
     def node_sum(x, first, count, stride):
         return (
@@ -456,35 +457,43 @@
             in_specs=[smem if i == "links" else vmem for i in ins],
             out_specs=(vmem,) * len(outs),
             scratch_shapes=[pltpu.VMEM(*v) for v in scratch],
-            compiler_params=pltpu.CompilerParams(vmem_limit_bytes=40 * MIB),
+            compiler_params=pltpu.CompilerParams(vmem_limit_bytes=24 * MIB),
             cost_estimate=pl.CostEstimate(flops=flops, bytes_accessed=MIB, transcendentals=0),
             name=name,
         )
 
+    split = call(
+        split_body,
+        "split_block",
+        ("strain", "coords"),
+        [
+            ((TILES * PIECES, PTS), f32),
+            ((EXT_COLS * PTS, PTS), bf16),
+            ((EXT_COLS * ROWS * 8, PTS), f32),
+            ((8, PTS), f32),
+        ],
+        [((TILES * PIECES, PTS), f32)],
+        3 * 10**9,
+    )
     inside = call(
         inside_body,
         "inside_links",
-        ("strain", "coords", "links"),
+        ("links", "su", "vt", "src", "info"),
         [((8 * TILES, PTS), f32)],
         [
-            ((TILES * PIECES, PTS), f32),
-            ((TILES * PIECES, PTS), f32),
-            ((EXT_COLS * PTS, PTS), bf16),
             ((PTS, len(INSIDE) * PTS), bf16),
             ((3 * PTS, len(INSIDE) * PTS), bf16),
-            ((EXT_COLS * ROWS * 8, PTS), f32),
         ],
-        8 * 10**9,
+        6 * 10**9,
     )
     rim = call(
         rim_body,
         "rim_links",
-        ("coords", "stiff", "links", "inside", "x_first", "x_second", "y_first", "y_second"),
+        ("stiff", "links", "inside", "su", "info", "x_first", "x_second", "y_first", "y_second"),
         [((LAYERS, ROWS, COLS, PTS), f32), ((ROWS, COLS, PTS), f32), ((peers, PTS), f32)],
         [
             ((EXT_COLS * PTS, PTS), f32),
             ((2 * PTS, PTS), f32),
-            ((TILES * PIECES, PTS), f32),
             ((EXT_COLS * PTS, PTS), bf16),
             ((PTS, 2 * PTS), bf16),
             ((COLS * 2 * PIECES, 2 * PTS), bf16),
@@ -522,7 +531,7 @@
         [],
         10**6,
     )
-    return inside, rim, force, finish
+    return split, inside, rim, force, finish
 
 
 def swap(first, second, axis):
@@ -543,8 +552,10 @@
     def row(r):
         return jnp.concatenate([take(v, r, 1) for v in own], axis=0)
 
-    inside, rim, force, finish = kernels(peers_x)
+    split, inside, rim, force, finish = kernels(peers_x)
     x_halos = swap(row(jnp.where(even_x, ROWS - 1, 0)), row(jnp.where(even_x, 0, ROWS - 1)), "gx")
+    pieces = split(strain, coords)
+    *x_halos, pieces = lax.optimization_barrier((*x_halos, pieces))
     above = jnp.where(even_x, x_halos[1], x_halos[0])
     below = jnp.where(even_x, x_halos[0], x_halos[1])
 
@@ -553,8 +564,9 @@
         return jnp.concatenate([take(above, c, 1)[:, None], mid, take(below, c, 1)[:, None]], axis=1)
 
     y_halos = swap(column(jnp.where(even_y, COLS - 1, 0)), column(jnp.where(even_y, 0, COLS - 1)), "gy")
-    totals = inside(strain, coords, neighbours)[0]
-    damage, strength, peak = rim(coords, stiffness, neighbours, totals, *x_halos, *y_halos)
+    own_pieces, _, _, info = pieces
+    totals = inside(neighbours, *pieces)[0]
+    damage, strength, peak = rim(stiffness, neighbours, totals, own_pieces, info, *x_halos, *y_halos)
     peaks = lax.all_to_all(peak, "gx", 0, 0, tiled=True)
     inner, rim_first, rim_second, rim_left, rim_right = force(displacement, strength, corners, *x_halos, *y_halos)
     x_rims = swap(rim_first, rim_second, "gx")

time: 83.7 us -> 81.4 us (0.973)
  Pallas kernels: 23.3 us -> 21.2 us
  waiting for transfers between devices: 11.2 us -> 9.57 us
  starting transfers between devices: 45.9 us -> 47.3 us
    pallas_call x2 -> x3, Pallas kernels: 16.9 us -> 15.4 us  [the longest x1 8.14 us: local(): totals = inside(neighbours, *pieces)[0]]
    ppermute x4, waiting for transfers between devices: 1.3 us -> 0.04 us  [swap(): lax.ppermute(first, axis, with_first)]
    ppermute x4, starting transfers between devices: 8.77 us -> 9.61 us  [swap(): lax.ppermute(first, axis, with_first)]
  transfers between devices with their start and end apart: 10 -> 10, of which waited for: 4 -> 3; matrix products, arithmetic and copies ran while one was open for 0% -> 0% of each run, Pallas kernels for 20% -> 18%
where the time goes in v3:
time: 81.4 us; the launch traced here: 81 us
  starting transfers between devices  47.3 us (58%)
  Pallas kernels  21.2 us (26%)
  waiting for transfers between devices  9.57 us (12%)
  local copies, waits for them, and re-layouts  1.78 us (2%)
  between operations  0.95 us (1%)
    ppermute x4, starting transfers between devices, swap(): lax.ppermute(second, axis, with_second)  19.1 us
    all_to_all x1, starting transfers between devices, local(): peaks = lax.all_to_all(peaks, 'gy', 0, 0, tiled=True)  11 us
    ppermute x4, starting transfers between devices, swap(): lax.ppermute(first, axis, with_first)  9.61 us
    ppermute x4, waiting for transfers between devices, swap(): lax.ppermute(second, axis, with_second)  9.53 us
    pallas_call x1, Pallas kernels, local(): totals = inside(neighbours, *pieces)[0]  8.14 us
    all_to_all x1, starting transfers between devices, local(): peaks = lax.all_to_all(peak, 'gx', 0, 0, tiled=True)  7.51 us
    pallas_call x1, Pallas kernels, local(): rim(stiffness, neighbours, totals, own_pieces, info, *x_halos, *y_halos)  5.52 us
    pallas_call x1, Pallas kernels, local(): force(displacement, strength, corners, *x_halos, *y_halos)  5.1 us
  transfers between devices with their start and end apart: 10, of which 3 were waited for; matrix products, arithmetic and copies ran while one was open for 0% of the time, Pallas kernels for 18%

profile of v3, /device:TPU:38, one launch (start us, length us, event | category | flops | bytes accessed | tf_op | source)
XLA Modules:
  0.0 81.0 jit_solution(4540710606493321871)
XLA Ops:
  0.6 0.0 copy-start.2
  0.6 0.0 copy-start.1
  0.7 0.9 %dynamic-slice_bitcast_fusion = (f32[5,16,128]{2,1,0:T(8,128)S(1)}, f32[5,16,128]{2,1,0:T(8,128)S(1)}) fusion(f32[5,4,16,128]{3,2,1,0:T(8,128)} %strain.1, s32[]{:T(128)S(6)} %select_n.83, s32[]{:T(128)S(6)} %select_n.82), kind=kLoop, calls=%fused_computation.6 | loop fusion | bytes 163848 | tf_op jit(solution)/shard_map/jit(dynamic_index_in_dim)/squeeze | solution.py:550
  1.5 0.0 copy-done.2
  1.5 0.0 copy-done.1
  1.6 0.0 copy-start
  1.6 2.1 %collective-permute-start = (f32[11,16,128]{2,1,0:T(8,128)S(1)}, f32[11,16,128]{2,1,0:T(8,128)S(1)}, u32[]{:S(2)}, u32[]{:S(2)}) collective-permute-start(f32[11,16,128]{2,1,0:T(8,128)S(1)} %pad_maximum_fusion), channel_id=1, source_target_pairs={{0,16},{16,0},{32,48},{48,32},{64,80},{80,64},{96,112},{112,96},{1... | collective-permute-start | bytes 270344 | tf_op jit(solution)/shard_map/ppermute | solution.py:541
  3.7 4.3 %collective-permute-start.1 = (f32[11,16,128]{2,1,0:T(8,128)S(1)}, f32[11,16,128]{2,1,0:T(8,128)S(1)}, u32[]{:S(2)}, u32[]{:S(2)}) collective-permute-start(f32[11,16,128]{2,1,0:T(8,128)S(1)} %pad_maximum_fusion.1), channel_id=1, source_target_pairs={{16,32},{32,16},{48,64},{64,48},{80,96},{96,80},{112,128},{128,112... | collective-permute-start | bytes 270344 | tf_op jit(solution)/shard_map/ppermute | solution.py:541
  8.0 0.0 copy-done
  8.0 1.7 %split_block.1 = (f32[2048,128]{1,0:T(8,128)S(1)}, bf16[2304,128]{1,0:T(8,128)(2,1)S(1)}, f32[576,128]{1,0:T(8,128)S(1)}, f32[8,128]{1,0:T(8,128)S(1)}) custom-call(f32[5,4,16,128]{3,2,1,0:T(8,128)S(1)} %copy-done, f32[3,4,16,128]{3,2,1,0:T(8,128)S(1)} %copy-done.1), custom_call_target="tpu_custom_call" | custom-call | flops 3000000000 | bytes 1048576 | tf_op jit(solution)/shard_map/split_block/pallas_call | solution.py:557
  9.8 0.0 collective-permute-done.x_first
  9.8 1.9 %collective-permute-done.1.x_second = f32[11,16,128]{2,1,0:T(8,128)S(1)} collective-permute-done((f32[11,16,128]{2,1,0:T(8,128)S(1)}, f32[11,16,128]{2,1,0:T(8,128)S(1)}, u32[]{:S(2)}, u32[]{:S(2)}) %collective-permute-start.1) | collective-permute-done | bytes 90144 | tf_op jit(solution)/shard_map/ppermute | solution.py:541
  11.7 2.7 %collective-permute-start.2 = (f32[11,6,128]{2,1,0:T(8,128)S(1)}, f32[11,6,128]{2,1,0:T(8,128)S(1)}, u32[]{:S(2)}, u32[]{:S(2)}) collective-permute-start(f32[11,6,128]{2,1,0:T(8,128)S(1)} %pad_maximum_fusion.2), channel_id=1, source_target_pairs={{0,1},{1,0},{2,3},{3,2},{4,5},{5,4},{6,7},{7,6},{8,9},{9,8},{10,11... | collective-permute-start | bytes 101384 | tf_op jit(solution)/shard_map/ppermute | solution.py:541
  14.5 0.0 copy-start.5
  14.5 0.0 copy-start.4
  14.5 6.7 %collective-permute-start.3 = (f32[11,6,128]{2,1,0:T(8,128)S(1)}, f32[11,6,128]{2,1,0:T(8,128)S(1)}, u32[]{:S(2)}, u32[]{:S(2)}) collective-permute-start(f32[11,6,128]{2,1,0:T(8,128)S(1)} %pad_maximum_fusion.3), channel_id=1, source_target_pairs={{1,2},{2,1},{3,4},{4,3},{5,6},{6,5},{7,8},{8,7},{9,10},{10,9},{11,... | collective-permute-start | bytes 101384 | tf_op jit(solution)/shard_map/ppermute | solution.py:541
  21.2 0.0 copy-done.5
  21.2 8.1 %inside_links.1.inside = f32[512,128]{1,0:T(8,128)S(1)} custom-call(s32[9,4,16]{2,1,0:T(4,128)S(1)} %copy-done.5, f32[2048,128]{1,0:T(8,128)S(1)} %get-tuple-element.75.su, bf16[2304,128]{1,0:T(8,128)(2,1)S(1)} %get-tuple-element.76.vt, f32[576,128]{1,0:T(8,128)S(1)} %get-tuple-element.77.src, f32[8,128]{1,0:T(8,128)S(1)} %get-tuple-element.78.info), custom_call_target="tpu_custom_call" | custom-call | flops 6000000000 | bytes 1048576 | tf_op jit(solution)/shard_map/inside_links/pallas_call | solution.py:568
  29.4 0.0 copy-start.3
  29.4 0.0 collective-permute-done.2.y_first
  29.4 0.0 collective-permute-done.3.y_second
  29.4 0.0 copy-done.4
  29.4 5.5 %rim_links.1 = (f32[5,4,16,128]{3,2,1,0:T(8,128)}, f32[4,16,128]{2,1,0:T(8,128)S(1)}, f32[32,128]{1,0:T(8,128)}) custom-call(f32[1,4,16,128]{3,2,1,0:T(8,128)S(1)} %copy-done.4, s32[9,4,16]{2,1,0:T(4,128)S(1)} %copy-done.5, f32[512,128]{1,0:T(8,128)S(1)} %inside_links.1.inside, f32[2048,128]{1,0:T(8,128)S(1)} %get-tuple-element.75.su, ...), custom_call_target="tpu_custom_call" | custom-call | flops 4000000000 | bytes 1048576 | tf_op jit(solution)/shard_map/rim_links/pallas_call | solution.py:569
  34.9 7.5 %all-to-all-start = ((f32[32,1,128]{2,1,0:T(1,128)}), f32[32,1,128]{2,1,0:T(1,128)S(1)}, u32[]{:S(2)}, u32[]{:S(2)}) async-start(f32[32,1,128]{2,1,0:T(1,128)} %bitcast.13), calls=%async_computation | async-start | bytes 32768 | tf_op jit(solution)/shard_map/all_to_all | solution.py:570
  42.5 0.0 copy-done.3
  42.5 5.1 %node_forces.1 = (f32[3,4,16,128]{3,2,1,0:T(8,128)S(1)}, f32[3,18,128]{2,1,0:T(8,128)S(1)}, f32[3,18,128]{2,1,0:T(8,128)S(1)}, f32[3,4,128]{2,1,0:T(4,128)S(1)}, f32[3,4,128]{2,1,0:T(4,128)S(1)}) custom-call(f32[3,4,16,128]{3,2,1,0:T(8,128)S(1)} %copy-done.2, f32[4,16,128]{2,1,0:T(8,128)S(1)} %get-tuple-element.82.strength, s32[4,4,16,128]{3,2,1,0:T(8,128)S(1)} %copy-done.3, ...), custom_call_target="tpu_custom_call" | custom-call | flops 8000000000 | bytes 1048576 | tf_op jit(solution)/shard_map/node_forces/pallas_call | solution.py:571
  47.6 2.1 %collective-permute-start.4 = (f32[3,18,128]{2,1,0:T(8,128)S(1)}, f32[3,18,128]{2,1,0:T(8,128)S(1)}, u32[]{:S(2)}, u32[]{:S(2)}) collective-permute-start(f32[3,18,128]{2,1,0:T(8,128)S(1)} %get-tuple-element.84), channel_id=1, source_target_pairs={{0,16},{16,0},{32,48},{48,32},{64,80},{80,64},{96,112},{112,96},{1... | collective-permute-start | bytes 82952 | tf_op jit(solution)/shard_map/ppermute | solution.py:541
  49.7 3.3 %collective-permute-start.5 = (f32[3,18,128]{2,1,0:T(8,128)S(1)}, f32[3,18,128]{2,1,0:T(8,128)S(1)}, u32[]{:S(2)}, u32[]{:S(2)}) collective-permute-start(f32[3,18,128]{2,1,0:T(8,128)S(1)} %get-tuple-element.85), channel_id=1, source_target_pairs={{16,32},{32,16},{48,64},{64,48},{80,96},{96,80},{112,128},{128,112... | collective-permute-start | bytes 82952 | tf_op jit(solution)/shard_map/ppermute | solution.py:541
  53.0 0.0 collective-permute-done.4.x_first
  53.0 4.0 %collective-permute-done.5.x_second = f32[3,18,128]{2,1,0:T(8,128)S(1)} collective-permute-done((f32[3,18,128]{2,1,0:T(8,128)S(1)}, f32[3,18,128]{2,1,0:T(8,128)S(1)}, u32[]{:S(2)}, u32[]{:S(2)}) %collective-permute-start.5) | collective-permute-done | bytes 27680 | tf_op jit(solution)/shard_map/ppermute | solution.py:541
  57.0 0.0 all-to-all-done
  57.2 0.6 broadcast_in_dim.2
  57.8 11.0 %all-to-all-start.1 = ((f32[16,1,128]{2,1,0:T(1,128)}), f32[16,1,128]{2,1,0:T(1,128)S(1)}, u32[]{:S(2)}, u32[]{:S(2)}) async-start(f32[16,1,128]{2,1,0:T(1,128)} %broadcast_in_dim.2), calls=%async_computation.1 | async-start | bytes 16384 | tf_op jit(solution)/shard_map/all_to_all | solution.py:575
  68.9 2.8 %collective-permute-start.6 = (f32[3,4,128]{2,1,0:T(4,128)S(1)}, f32[3,4,128]{2,1,0:T(4,128)S(1)}, u32[]{:S(2)}, u32[]{:S(2)}) collective-permute-start(f32[3,4,128]{2,1,0:T(4,128)S(1)} %get-tuple-element.117), channel_id=1, source_target_pairs={{0,1},{1,0},{2,3},{3,2},{4,5},{5,4},{6,7},{7,6},{8,9},{9,8},{10,11... | collective-permute-start | bytes 18440 | tf_op jit(solution)/shard_map/ppermute | solution.py:541
  71.7 4.9 %collective-permute-start.7 = (f32[3,4,128]{2,1,0:T(4,128)S(1)}, f32[3,4,128]{2,1,0:T(4,128)S(1)}, u32[]{:S(2)}, u32[]{:S(2)}) collective-permute-start(f32[3,4,128]{2,1,0:T(4,128)S(1)} %get-tuple-element.116), channel_id=1, source_target_pairs={{1,2},{2,1},{3,4},{4,3},{5,6},{6,5},{7,8},{8,7},{9,10},{10,9},{11,... | collective-permute-start | bytes 18440 | tf_op jit(solution)/shard_map/ppermute | solution.py:541
  76.5 0.0 collective-permute-done.6.y_first
  76.6 3.6 %collective-permute-done.7.y_second = f32[3,4,128]{2,1,0:T(4,128)S(1)} collective-permute-done((f32[3,4,128]{2,1,0:T(4,128)S(1)}, f32[3,4,128]{2,1,0:T(4,128)S(1)}, u32[]{:S(2)}, u32[]{:S(2)}) %collective-permute-start.7) | collective-permute-done | bytes 6176 | tf_op jit(solution)/shard_map/ppermute | solution.py:541
  80.2 0.0 all-to-all-done.1
  80.2 0.8 finish.1
  (19 shorter events, 0.4 us)
Async XLA Ops:
  0.6 0.9 %copy-start.2 = (f32[3,4,16,128]{3,2,1,0:T(8,128)S(1)}, f32[3,4,16,128]{3,2,1,0:T(8,128)}, u32[]{:S(2)}) copy-start(f32[3,4,16,128]{3,2,1,0:T(8,128)} %disp.1) | copy-start | bytes 294916
  0.6 0.9 %copy-start.1 = (f32[3,4,16,128]{3,2,1,0:T(8,128)S(1)}, f32[3,4,16,128]{3,2,1,0:T(8,128)}, u32[]{:S(2)}) copy-start(f32[3,4,16,128]{3,2,1,0:T(8,128)} %coords.1) | copy-start | bytes 294916
  1.6 6.4 %copy-start = (f32[5,4,16,128]{3,2,1,0:T(8,128)S(1)}, f32[5,4,16,128]{3,2,1,0:T(8,128)}, u32[]{:S(2)}) copy-start(f32[5,4,16,128]{3,2,1,0:T(8,128)} %strain.1) | copy-start | bytes 491524
  1.6 8.2 %collective-permute-start = (f32[11,16,128]{2,1,0:T(8,128)S(1)}, f32[11,16,128]{2,1,0:T(8,128)S(1)}, u32[]{:S(2)}, u32[]{:S(2)}) collective-permute-start(f32[11,16,128]{2,1,0:T(8,128)S(1)} %pad_maximum_fusion), channel_id=1, source_target_pairs={{0,16},{16,0},{32,48},{48,32},{64,80},{80,64},{96,112},{112,96},{1... | collective-permute-start | bytes 270344 | tf_op jit(solution)/shard_map/ppermute | solution.py:541
  3.7 8.0 %collective-permute-start.1 = (f32[11,16,128]{2,1,0:T(8,128)S(1)}, f32[11,16,128]{2,1,0:T(8,128)S(1)}, u32[]{:S(2)}, u32[]{:S(2)}) collective-permute-start(f32[11,16,128]{2,1,0:T(8,128)S(1)} %pad_maximum_fusion.1), channel_id=1, source_target_pairs={{16,32},{32,16},{48,64},{64,48},{80,96},{96,80},{112,128},{128,112... | collective-permute-start | bytes 270344 | tf_op jit(solution)/shard_map/ppermute | solution.py:541
  11.7 17.6 %collective-permute-start.2 = (f32[11,6,128]{2,1,0:T(8,128)S(1)}, f32[11,6,128]{2,1,0:T(8,128)S(1)}, u32[]{:S(2)}, u32[]{:S(2)}) collective-permute-start(f32[11,6,128]{2,1,0:T(8,128)S(1)} %pad_maximum_fusion.2), channel_id=1, source_target_pairs={{0,1},{1,0},{2,3},{3,2},{4,5},{5,4},{6,7},{7,6},{8,9},{9,8},{10,11... | collective-permute-start | bytes 101384 | tf_op jit(solution)/shard_map/ppermute | solution.py:541
  14.5 6.7 %copy-start.5 = (s32[9,4,16]{2,1,0:T(4,128)S(1)}, s32[9,4,16]{2,1,0:T(4,128)}, u32[]{:S(2)}) copy-start(s32[9,4,16]{2,1,0:T(4,128)} %links.3) | copy-start | bytes 6916
  14.5 14.9 %copy-start.4 = (f32[1,4,16,128]{3,2,1,0:T(8,128)S(1)}, f32[1,4,16,128]{3,2,1,0:T(8,128)}, u32[]{:S(2)}) copy-start(f32[1,4,16,128]{3,2,1,0:T(8,128)} %stiff.1) | copy-start | bytes 98308
  14.5 14.9 %collective-permute-start.3 = (f32[11,6,128]{2,1,0:T(8,128)S(1)}, f32[11,6,128]{2,1,0:T(8,128)S(1)}, u32[]{:S(2)}, u32[]{:S(2)}) collective-permute-start(f32[11,6,128]{2,1,0:T(8,128)S(1)} %pad_maximum_fusion.3), channel_id=1, source_target_pairs={{1,2},{2,1},{3,4},{4,3},{5,6},{6,5},{7,8},{8,7},{9,10},{10,9},{11,... | collective-permute-start | bytes 101384 | tf_op jit(solution)/shard_map/ppermute | solution.py:541
  29.4 13.1 %copy-start.3 = (s32[4,4,16,128]{3,2,1,0:T(8,128)S(1)}, s32[4,4,16,128]{3,2,1,0:T(8,128)}, u32[]{:S(2)}) copy-start(s32[4,4,16,128]{3,2,1,0:T(8,128)} %corners.1) | copy-start | bytes 393220
  34.9 22.1 %all-to-all-start = ((f32[32,1,128]{2,1,0:T(1,128)}), f32[32,1,128]{2,1,0:T(1,128)S(1)}, u32[]{:S(2)}, u32[]{:S(2)}) async-start(f32[32,1,128]{2,1,0:T(1,128)} %bitcast.13), calls=%async_computation | async-start | bytes 32768 | tf_op jit(solution)/shard_map/all_to_all | solution.py:570
  47.6 5.4 %collective-permute-start.4 = (f32[3,18,128]{2,1,0:T(8,128)S(1)}, f32[3,18,128]{2,1,0:T(8,128)S(1)}, u32[]{:S(2)}, u32[]{:S(2)}) collective-permute-start(f32[3,18,128]{2,1,0:T(8,128)S(1)} %get-tuple-element.84), channel_id=1, source_target_pairs={{0,16},{16,0},{32,48},{48,32},{64,80},{80,64},{96,112},{112,96},{1... | collective-permute-start | bytes 82952 | tf_op jit(solution)/shard_map/ppermute | solution.py:541
  49.7 7.4 %collective-permute-start.5 = (f32[3,18,128]{2,1,0:T(8,128)S(1)}, f32[3,18,128]{2,1,0:T(8,128)S(1)}, u32[]{:S(2)}, u32[]{:S(2)}) collective-permute-start(f32[3,18,128]{2,1,0:T(8,128)S(1)} %get-tuple-element.85), channel_id=1, source_target_pairs={{16,32},{32,16},{48,64},{64,48},{80,96},{96,80},{112,128},{128,112... | collective-permute-start | bytes 82952 | tf_op jit(solution)/shard_map/ppermute | solution.py:541
  57.8 22.3 %all-to-all-start.1 = ((f32[16,1,128]{2,1,0:T(1,128)}), f32[16,1,128]{2,1,0:T(1,128)S(1)}, u32[]{:S(2)}, u32[]{:S(2)}) async-start(f32[16,1,128]{2,1,0:T(1,128)} %broadcast_in_dim.2), calls=%async_computation.1 | async-start | bytes 16384 | tf_op jit(solution)/shard_map/all_to_all | solution.py:575
  68.9 7.7 %collective-permute-start.6 = (f32[3,4,128]{2,1,0:T(4,128)S(1)}, f32[3,4,128]{2,1,0:T(4,128)S(1)}, u32[]{:S(2)}, u32[]{:S(2)}) collective-permute-start(f32[3,4,128]{2,1,0:T(4,128)S(1)} %get-tuple-element.117), channel_id=1, source_target_pairs={{0,1},{1,0},{2,3},{3,2},{4,5},{5,4},{6,7},{7,6},{8,9},{9,8},{10,11... | collective-permute-start | bytes 18440 | tf_op jit(solution)/shard_map/ppermute | solution.py:541
  71.7 8.5 %collective-permute-start.7 = (f32[3,4,128]{2,1,0:T(4,128)S(1)}, f32[3,4,128]{2,1,0:T(4,128)S(1)}, u32[]{:S(2)}, u32[]{:S(2)}) collective-permute-start(f32[3,4,128]{2,1,0:T(4,128)S(1)} %get-tuple-element.116), channel_id=1, source_target_pairs={{1,2},{2,1},{3,4},{4,3},{5,6},{6,5},{7,8},{8,7},{9,10},{10,9},{11,... | collective-permute-start | bytes 18440 | tf_op jit(solution)/shard_map/ppermute | solution.py:541

commit v4 on v3

--- a/solution.py
+++ b/solution.py
@@ -166,7 +166,7 @@
                 totals[pl.ds(r * COLS + c, 8, stride=TILES), :] = sums[r]
             return carry
 
-        lax.fori_loop(0, COLS, column, 0, unroll=4)
+        lax.fori_loop(0, COLS, column, 0, unroll=16)
 
     @pl.when(jnp.logical_not(near))
     def _():
@@ -256,7 +256,7 @@
             vt[rows_at(c, PTS), :] = sv[rows_at(c, PTS), :].T.astype(bf16)
             return carry
 
-        lax.fori_loop(0, EXT_COLS, turn, 0, unroll=9)
+        lax.fori_loop(0, EXT_COLS, turn, 0, unroll=18)
         vt_sides[...] = sides[...].T.astype(bf16)
         for h in range(2):
             for j, (o, r) in enumerate(INSIDE):
@@ -276,7 +276,7 @@
             weights[rows_at(c, 3 * PTS), :] = bell_weights(vt[rows_at(c, PTS, 3 * PTS), :], own)
             return carry
 
-        lax.fori_loop(0, COLS, weigh, 0, unroll=4)
+        lax.fori_loop(0, COLS, weigh, 0, unroll=16)
 
         def total(c, carry):
             halves = []
@@ -292,7 +292,7 @@
                 add(h * (ROWS - 1), c, out[8 * h : 8 * h + 8, h * PTS : (h + 1) * PTS])
             return carry
 
-        lax.fori_loop(0, COLS, total, 0, unroll=4)
+        lax.fori_loop(0, COLS, total, 0, unroll=16)
         sums = [[zero8 for _ in range(ROWS)] for _ in range(2)]
         for j in range(0, 2 * len(INSIDE), 2):
             halves, owners = [], []
@@ -389,7 +389,7 @@
                     amounts[at[8 * k + 4 + x], :] = amount - hi
         return carry
 
-    lax.fori_loop(0, ROWS, gather, 0, unroll=2)
+    lax.fori_loop(0, ROWS, gather, 0, unroll=4)
 
     nodes = lax.broadcasted_iota(jnp.int32, (PTS, PTS), 0).astype(f32)
 
@@ -409,7 +409,7 @@
             forces[at, :] = forces[at, :] + out[8 * o : 8 * o + 8]
         return carry
 
-    lax.fori_loop(0, ROWS * COLS, scatter, 0, unroll=16)
+    lax.fori_loop(0, ROWS * COLS, scatter, 0, unroll=32)
 
     def node_sum(x, first, count, stride):
         return (
@@ -569,8 +569,8 @@
     damage, strength, peak = rim(stiffness, neighbours, totals, own_pieces, info, *x_halos, *y_halos)
     peaks = lax.all_to_all(peak, "gx", 0, 0, tiled=True)
     inner, rim_first, rim_second, rim_left, rim_right = force(displacement, strength, corners, *x_halos, *y_halos)
+    rim_first, rim_second, peaks = lax.optimization_barrier((rim_first, rim_second, peaks))
     x_rims = swap(rim_first, rim_second, "gx")
-    *x_rims, peaks = lax.optimization_barrier((*x_rims, peaks))
     peaks = jnp.broadcast_to(jnp.max(peaks, axis=0, keepdims=True), (peers_y, PTS))
     peaks = lax.all_to_all(peaks, "gy", 0, 0, tiled=True)
     above = jnp.where(even_x, x_rims[1], x_rims[0])

time: 81.4 us -> 77.7 us (0.955)
  the two profiles are of different devices: /device:TPU:38 before, /device:TPU:14 now
where the time goes in v4:
time: 77.7 us; the launch traced here: 77.2 us
  starting transfers between devices  48.8 us (63%)
  Pallas kernels  18.8 us (24%)
  waiting for transfers between devices  6.7 us (9%)
  local copies, waits for them, and re-layouts  1.78 us (2%)
  between operations  0.95 us (1%)
    ppermute x4, starting transfers between devices, swap(): lax.ppermute(second, axis, with_second)  19.4 us
    all_to_all x1, starting transfers between devices, local(): peaks = lax.all_to_all(peaks, 'gy', 0, 0, tiled=True)  11 us
    ppermute x4, starting transfers between devices, swap(): lax.ppermute(first, axis, with_first)  9.46 us
    all_to_all x1, starting transfers between devices, local(): peaks = lax.all_to_all(peak, 'gx', 0, 0, tiled=True)  8.96 us
    pallas_call x1, Pallas kernels, local(): totals = inside(neighbours, *pieces)[0]  7.47 us
    pallas_call x1, Pallas kernels, local(): force(displacement, strength, corners, *x_halos, *y_halos)  4.71 us
    ppermute x4, waiting for transfers between devices, swap(): lax.ppermute(second, axis, with_second)  4.33 us
    pallas_call x1, Pallas kernels, local(): rim(stiffness, neighbours, totals, own_pieces, info, *x_halos, *y_halos)  4.15 us
  transfers between devices with their start and end apart: 10, of which 4 were waited for; matrix products, arithmetic and copies ran while one was open for 1% of the time, Pallas kernels for 18%

profile of v4, /device:TPU:14, one launch (start us, length us, event | category | flops | bytes accessed | tf_op | source)
XLA Modules:
  0.0 77.2 jit_solution(13216620574879984653)
XLA Ops:
  0.6 0.0 copy-start.2
  0.6 0.0 copy-start.1
  0.7 0.9 %dynamic-slice_bitcast_fusion = (f32[5,16,128]{2,1,0:T(8,128)S(1)}, f32[5,16,128]{2,1,0:T(8,128)S(1)}) fusion(f32[5,4,16,128]{3,2,1,0:T(8,128)} %strain.1, s32[]{:T(128)S(6)} %select_n.83, s32[]{:T(128)S(6)} %select_n.82), kind=kLoop, calls=%fused_computation.6 | loop fusion | bytes 163848 | tf_op jit(solution)/shard_map/jit(dynamic_index_in_dim)/squeeze | solution.py:550
  1.5 0.0 copy-done.2
  1.5 0.0 copy-done.1
  1.6 0.0 copy-start
  1.6 2.1 %collective-permute-start = (f32[11,16,128]{2,1,0:T(8,128)S(1)}, f32[11,16,128]{2,1,0:T(8,128)S(1)}, u32[]{:S(2)}, u32[]{:S(2)}) collective-permute-start(f32[11,16,128]{2,1,0:T(8,128)S(1)} %pad_maximum_fusion), channel_id=1, source_target_pairs={{0,16},{16,0},{32,48},{48,32},{64,80},{80,64},{96,112},{112,96},{1... | collective-permute-start | bytes 270344 | tf_op jit(solution)/shard_map/ppermute | solution.py:541
  3.7 4.3 %collective-permute-start.1 = (f32[11,16,128]{2,1,0:T(8,128)S(1)}, f32[11,16,128]{2,1,0:T(8,128)S(1)}, u32[]{:S(2)}, u32[]{:S(2)}) collective-permute-start(f32[11,16,128]{2,1,0:T(8,128)S(1)} %pad_maximum_fusion.1), channel_id=1, source_target_pairs={{16,32},{32,16},{48,64},{64,48},{80,96},{96,80},{112,128},{128,112... | collective-permute-start | bytes 270344 | tf_op jit(solution)/shard_map/ppermute | solution.py:541
  8.0 0.0 copy-done
  8.0 1.7 %split_block.1 = (f32[2048,128]{1,0:T(8,128)S(1)}, bf16[2304,128]{1,0:T(8,128)(2,1)S(1)}, f32[576,128]{1,0:T(8,128)S(1)}, f32[8,128]{1,0:T(8,128)S(1)}) custom-call(f32[5,4,16,128]{3,2,1,0:T(8,128)S(1)} %copy-done, f32[3,4,16,128]{3,2,1,0:T(8,128)S(1)} %copy-done.1), custom_call_target="tpu_custom_call" | custom-call | flops 3000000000 | bytes 1048576 | tf_op jit(solution)/shard_map/split_block/pallas_call | solution.py:557
  9.8 0.0 collective-permute-done.x_first
  9.8 0.7 collective-permute-done.1.x_second
  10.6 2.7 %collective-permute-start.2 = (f32[11,6,128]{2,1,0:T(8,128)S(1)}, f32[11,6,128]{2,1,0:T(8,128)S(1)}, u32[]{:S(2)}, u32[]{:S(2)}) collective-permute-start(f32[11,6,128]{2,1,0:T(8,128)S(1)} %pad_maximum_fusion.2), channel_id=1, source_target_pairs={{0,1},{1,0},{2,3},{3,2},{4,5},{5,4},{6,7},{7,6},{8,9},{9,8},{10,11... | collective-permute-start | bytes 101384 | tf_op jit(solution)/shard_map/ppermute | solution.py:541
  13.4 0.0 copy-start.5
  13.4 0.0 copy-start.4
  13.4 6.7 %collective-permute-start.3 = (f32[11,6,128]{2,1,0:T(8,128)S(1)}, f32[11,6,128]{2,1,0:T(8,128)S(1)}, u32[]{:S(2)}, u32[]{:S(2)}) collective-permute-start(f32[11,6,128]{2,1,0:T(8,128)S(1)} %pad_maximum_fusion.3), channel_id=1, source_target_pairs={{1,2},{2,1},{3,4},{4,3},{5,6},{6,5},{7,8},{8,7},{9,10},{10,9},{11,... | collective-permute-start | bytes 101384 | tf_op jit(solution)/shard_map/ppermute | solution.py:541
  20.1 0.0 copy-done.5
  20.1 7.5 %inside_links.1.inside = f32[512,128]{1,0:T(8,128)S(1)} custom-call(s32[9,4,16]{2,1,0:T(4,128)S(1)} %copy-done.5, f32[2048,128]{1,0:T(8,128)S(1)} %get-tuple-element.75.su, bf16[2304,128]{1,0:T(8,128)(2,1)S(1)} %get-tuple-element.76.vt, f32[576,128]{1,0:T(8,128)S(1)} %get-tuple-element.77.src, f32[8,128]{1,0:T(8,128)S(1)} %get-tuple-element.78.info), custom_call_target="tpu_custom_call" | custom-call | flops 6000000000 | bytes 1048576 | tf_op jit(solution)/shard_map/inside_links/pallas_call | solution.py:568
  27.6 0.0 copy-start.3
  27.6 0.0 collective-permute-done.2.y_first
  27.6 0.0 collective-permute-done.3.y_second
  27.6 0.0 copy-done.4
  27.6 4.2 %rim_links.1 = (f32[5,4,16,128]{3,2,1,0:T(8,128)}, f32[4,16,128]{2,1,0:T(8,128)S(1)}, f32[32,128]{1,0:T(8,128)}) custom-call(f32[1,4,16,128]{3,2,1,0:T(8,128)S(1)} %copy-done.4, s32[9,4,16]{2,1,0:T(4,128)S(1)} %copy-done.5, f32[512,128]{1,0:T(8,128)S(1)} %inside_links.1.inside, f32[2048,128]{1,0:T(8,128)S(1)} %get-tuple-element.75.su, ...), custom_call_target="tpu_custom_call" | custom-call | flops 4000000000 | bytes 1048576 | tf_op jit(solution)/shard_map/rim_links/pallas_call | solution.py:569
  31.8 9.0 %all-to-all-start = ((f32[32,1,128]{2,1,0:T(1,128)}), f32[32,1,128]{2,1,0:T(1,128)S(1)}, u32[]{:S(2)}, u32[]{:S(2)}) async-start(f32[32,1,128]{2,1,0:T(1,128)} %bitcast.13), calls=%async_computation | async-start | bytes 32768 | tf_op jit(solution)/shard_map/all_to_all | solution.py:570
  40.8 0.0 copy-done.3
  40.8 4.7 %node_forces.1 = (f32[3,4,16,128]{3,2,1,0:T(8,128)S(1)}, f32[3,18,128]{2,1,0:T(8,128)S(1)}, f32[3,18,128]{2,1,0:T(8,128)S(1)}, f32[3,4,128]{2,1,0:T(4,128)S(1)}, f32[3,4,128]{2,1,0:T(4,128)S(1)}) custom-call(f32[3,4,16,128]{3,2,1,0:T(8,128)S(1)} %copy-done.2, f32[4,16,128]{2,1,0:T(8,128)S(1)} %get-tuple-element.82.strength, s32[4,4,16,128]{3,2,1,0:T(8,128)S(1)} %copy-done.3, ...), custom_call_target="tpu_custom_call" | custom-call | flops 8000000000 | bytes 1048576 | tf_op jit(solution)/shard_map/node_forces/pallas_call | solution.py:571
  45.5 2.3 %all-to-all-done = f32[32,1,128]{2,1,0:T(1,128)S(1)} async-done(((f32[32,1,128]{2,1,0:T(1,128)}), f32[32,1,128]{2,1,0:T(1,128)S(1)}, u32[]{:S(2)}, u32[]{:S(2)}) %all-to-all-start) | async-done | bytes 16416 | tf_op jit(solution)/shard_map/all_to_all | solution.py:570
  47.8 1.9 %collective-permute-start.4 = (f32[3,18,128]{2,1,0:T(8,128)S(1)}, f32[3,18,128]{2,1,0:T(8,128)S(1)}, u32[]{:S(2)}, u32[]{:S(2)}) collective-permute-start(f32[3,18,128]{2,1,0:T(8,128)S(1)} %get-tuple-element.87), channel_id=1, source_target_pairs={{0,16},{16,0},{32,48},{48,32},{64,80},{80,64},{96,112},{112,96},{1... | collective-permute-start | bytes 82952 | tf_op jit(solution)/shard_map/ppermute | solution.py:541
  49.7 3.6 %collective-permute-start.5 = (f32[3,18,128]{2,1,0:T(8,128)S(1)}, f32[3,18,128]{2,1,0:T(8,128)S(1)}, u32[]{:S(2)}, u32[]{:S(2)}) collective-permute-start(f32[3,18,128]{2,1,0:T(8,128)S(1)} %get-tuple-element.88), channel_id=1, source_target_pairs={{16,32},{32,16},{48,64},{64,48},{80,96},{96,80},{112,128},{128,112... | collective-permute-start | bytes 82952 | tf_op jit(solution)/shard_map/ppermute | solution.py:541
  53.3 0.6 broadcast_in_dim.2
  53.9 11.0 %all-to-all-start.1 = ((f32[16,1,128]{2,1,0:T(1,128)}), f32[16,1,128]{2,1,0:T(1,128)S(1)}, u32[]{:S(2)}, u32[]{:S(2)}) async-start(f32[16,1,128]{2,1,0:T(1,128)} %broadcast_in_dim.2), calls=%async_computation.1 | async-start | bytes 16384 | tf_op jit(solution)/shard_map/all_to_all | solution.py:575
  64.9 0.0 collective-permute-done.4.x_first
  64.9 0.0 collective-permute-done.5.x_second
  65.1 2.8 %collective-permute-start.6 = (f32[3,4,128]{2,1,0:T(4,128)S(1)}, f32[3,4,128]{2,1,0:T(4,128)S(1)}, u32[]{:S(2)}, u32[]{:S(2)}) collective-permute-start(f32[3,4,128]{2,1,0:T(4,128)S(1)} %get-tuple-element.117), channel_id=1, source_target_pairs={{0,1},{1,0},{2,3},{3,2},{4,5},{5,4},{6,7},{7,6},{8,9},{9,8},{10,11... | collective-permute-start | bytes 18440 | tf_op jit(solution)/shard_map/ppermute | solution.py:541
  67.9 4.9 %collective-permute-start.7 = (f32[3,4,128]{2,1,0:T(4,128)S(1)}, f32[3,4,128]{2,1,0:T(4,128)S(1)}, u32[]{:S(2)}, u32[]{:S(2)}) collective-permute-start(f32[3,4,128]{2,1,0:T(4,128)S(1)} %get-tuple-element.116), channel_id=1, source_target_pairs={{1,2},{2,1},{3,4},{4,3},{5,6},{6,5},{7,8},{8,7},{9,10},{10,9},{11,... | collective-permute-start | bytes 18440 | tf_op jit(solution)/shard_map/ppermute | solution.py:541
  72.8 0.1 all-to-all-done.1
  72.8 0.0 collective-permute-done.6.y_first
  72.8 3.6 %collective-permute-done.7.y_second = f32[3,4,128]{2,1,0:T(4,128)S(1)} collective-permute-done((f32[3,4,128]{2,1,0:T(4,128)S(1)}, f32[3,4,128]{2,1,0:T(4,128)S(1)}, u32[]{:S(2)}, u32[]{:S(2)}) %collective-permute-start.7) | collective-permute-done | bytes 6176 | tf_op jit(solution)/shard_map/ppermute | solution.py:541
  76.4 0.8 %finish.1 = f32[3,4,16,128]{3,2,1,0:T(8,128)} custom-call(f32[3,4,16,128]{3,2,1,0:T(8,128)S(1)} %get-tuple-element.83.inner, f32[3,18,128]{2,1,0:T(8,128)S(1)} %collective-permute-done.4.x_first, f32[3,18,128]{2,1,0:T(8,128)S(1)} %collective-permute-done.5.x_second, f32[3,4,128]{2,1,0:T(4,128)S(1)} %collective-permute-done.6.y_first, ...), custom_call_target="tpu_custom_call" | custom-call | flops 1000000 | bytes 1048576 | tf_op jit(solution)/shard_map/finish/pallas_call | solution.py:584
  (19 shorter events, 0.4 us)
Async XLA Ops:
  0.6 0.9 %copy-start.2 = (f32[3,4,16,128]{3,2,1,0:T(8,128)S(1)}, f32[3,4,16,128]{3,2,1,0:T(8,128)}, u32[]{:S(2)}) copy-start(f32[3,4,16,128]{3,2,1,0:T(8,128)} %disp.1) | copy-start | bytes 294916
  0.6 0.9 %copy-start.1 = (f32[3,4,16,128]{3,2,1,0:T(8,128)S(1)}, f32[3,4,16,128]{3,2,1,0:T(8,128)}, u32[]{:S(2)}) copy-start(f32[3,4,16,128]{3,2,1,0:T(8,128)} %coords.1) | copy-start | bytes 294916
  1.6 6.4 %copy-start = (f32[5,4,16,128]{3,2,1,0:T(8,128)S(1)}, f32[5,4,16,128]{3,2,1,0:T(8,128)}, u32[]{:S(2)}) copy-start(f32[5,4,16,128]{3,2,1,0:T(8,128)} %strain.1) | copy-start | bytes 491524
  1.6 8.2 %collective-permute-start = (f32[11,16,128]{2,1,0:T(8,128)S(1)}, f32[11,16,128]{2,1,0:T(8,128)S(1)}, u32[]{:S(2)}, u32[]{:S(2)}) collective-permute-start(f32[11,16,128]{2,1,0:T(8,128)S(1)} %pad_maximum_fusion), channel_id=1, source_target_pairs={{0,16},{16,0},{32,48},{48,32},{64,80},{80,64},{96,112},{112,96},{1... | collective-permute-start | bytes 270344 | tf_op jit(solution)/shard_map/ppermute | solution.py:541
  3.7 6.8 %collective-permute-start.1 = (f32[11,16,128]{2,1,0:T(8,128)S(1)}, f32[11,16,128]{2,1,0:T(8,128)S(1)}, u32[]{:S(2)}, u32[]{:S(2)}) collective-permute-start(f32[11,16,128]{2,1,0:T(8,128)S(1)} %pad_maximum_fusion.1), channel_id=1, source_target_pairs={{16,32},{32,16},{48,64},{64,48},{80,96},{96,80},{112,128},{128,112... | collective-permute-start | bytes 270344 | tf_op jit(solution)/shard_map/ppermute | solution.py:541
  10.6 17.0 %collective-permute-start.2 = (f32[11,6,128]{2,1,0:T(8,128)S(1)}, f32[11,6,128]{2,1,0:T(8,128)S(1)}, u32[]{:S(2)}, u32[]{:S(2)}) collective-permute-start(f32[11,6,128]{2,1,0:T(8,128)S(1)} %pad_maximum_fusion.2), channel_id=1, source_target_pairs={{0,1},{1,0},{2,3},{3,2},{4,5},{5,4},{6,7},{7,6},{8,9},{9,8},{10,11... | collective-permute-start | bytes 101384 | tf_op jit(solution)/shard_map/ppermute | solution.py:541
  13.4 6.7 %copy-start.5 = (s32[9,4,16]{2,1,0:T(4,128)S(1)}, s32[9,4,16]{2,1,0:T(4,128)}, u32[]{:S(2)}) copy-start(s32[9,4,16]{2,1,0:T(4,128)} %links.3) | copy-start | bytes 6916
  13.4 14.2 %copy-start.4 = (f32[1,4,16,128]{3,2,1,0:T(8,128)S(1)}, f32[1,4,16,128]{3,2,1,0:T(8,128)}, u32[]{:S(2)}) copy-start(f32[1,4,16,128]{3,2,1,0:T(8,128)} %stiff.1) | copy-start | bytes 98308
  13.4 14.2 %collective-permute-start.3 = (f32[11,6,128]{2,1,0:T(8,128)S(1)}, f32[11,6,128]{2,1,0:T(8,128)S(1)}, u32[]{:S(2)}, u32[]{:S(2)}) collective-permute-start(f32[11,6,128]{2,1,0:T(8,128)S(1)} %pad_maximum_fusion.3), channel_id=1, source_target_pairs={{1,2},{2,1},{3,4},{4,3},{5,6},{6,5},{7,8},{8,7},{9,10},{10,9},{11,... | collective-permute-start | bytes 101384 | tf_op jit(solution)/shard_map/ppermute | solution.py:541
  27.6 13.2 %copy-start.3 = (s32[4,4,16,128]{3,2,1,0:T(8,128)S(1)}, s32[4,4,16,128]{3,2,1,0:T(8,128)}, u32[]{:S(2)}) copy-start(s32[4,4,16,128]{3,2,1,0:T(8,128)} %corners.1) | copy-start | bytes 393220
  31.8 16.0 %all-to-all-start = ((f32[32,1,128]{2,1,0:T(1,128)}), f32[32,1,128]{2,1,0:T(1,128)S(1)}, u32[]{:S(2)}, u32[]{:S(2)}) async-start(f32[32,1,128]{2,1,0:T(1,128)} %bitcast.13), calls=%async_computation | async-start | bytes 32768 | tf_op jit(solution)/shard_map/all_to_all | solution.py:570
  47.8 17.1 %collective-permute-start.4 = (f32[3,18,128]{2,1,0:T(8,128)S(1)}, f32[3,18,128]{2,1,0:T(8,128)S(1)}, u32[]{:S(2)}, u32[]{:S(2)}) collective-permute-start(f32[3,18,128]{2,1,0:T(8,128)S(1)} %get-tuple-element.87), channel_id=1, source_target_pairs={{0,16},{16,0},{32,48},{48,32},{64,80},{80,64},{96,112},{112,96},{1... | collective-permute-start | bytes 82952 | tf_op jit(solution)/shard_map/ppermute | solution.py:541
  49.7 15.2 %collective-permute-start.5 = (f32[3,18,128]{2,1,0:T(8,128)S(1)}, f32[3,18,128]{2,1,0:T(8,128)S(1)}, u32[]{:S(2)}, u32[]{:S(2)}) collective-permute-start(f32[3,18,128]{2,1,0:T(8,128)S(1)} %get-tuple-element.88), channel_id=1, source_target_pairs={{16,32},{32,16},{48,64},{64,48},{80,96},{96,80},{112,128},{128,112... | collective-permute-start | bytes 82952 | tf_op jit(solution)/shard_map/ppermute | solution.py:541
  53.9 19.0 %all-to-all-start.1 = ((f32[16,1,128]{2,1,0:T(1,128)}), f32[16,1,128]{2,1,0:T(1,128)S(1)}, u32[]{:S(2)}, u32[]{:S(2)}) async-start(f32[16,1,128]{2,1,0:T(1,128)} %broadcast_in_dim.2), calls=%async_computation.1 | async-start | bytes 16384 | tf_op jit(solution)/shard_map/all_to_all | solution.py:575
  65.1 7.7 %collective-permute-start.6 = (f32[3,4,128]{2,1,0:T(4,128)S(1)}, f32[3,4,128]{2,1,0:T(4,128)S(1)}, u32[]{:S(2)}, u32[]{:S(2)}) collective-permute-start(f32[3,4,128]{2,1,0:T(4,128)S(1)} %get-tuple-element.117), channel_id=1, source_target_pairs={{0,1},{1,0},{2,3},{3,2},{4,5},{5,4},{6,7},{7,6},{8,9},{9,8},{10,11... | collective-permute-start | bytes 18440 | tf_op jit(solution)/shard_map/ppermute | solution.py:541
  67.9 8.5 %collective-permute-start.7 = (f32[3,4,128]{2,1,0:T(4,128)S(1)}, f32[3,4,128]{2,1,0:T(4,128)S(1)}, u32[]{:S(2)}, u32[]{:S(2)}) collective-permute-start(f32[3,4,128]{2,1,0:T(4,128)S(1)} %get-tuple-element.116), channel_id=1, source_target_pairs={{1,2},{2,1},{3,4},{4,3},{5,6},{6,5},{7,8},{8,7},{9,10},{10,9},{11,... | collective-permute-start | bytes 18440 | tf_op jit(solution)/shard_map/ppermute | solution.py:541

commit v5 on v4

--- a/solution.py
+++ b/solution.py
@@ -569,7 +569,7 @@
     damage, strength, peak = rim(stiffness, neighbours, totals, own_pieces, info, *x_halos, *y_halos)
     peaks = lax.all_to_all(peak, "gx", 0, 0, tiled=True)
     inner, rim_first, rim_second, rim_left, rim_right = force(displacement, strength, corners, *x_halos, *y_halos)
-    rim_first, rim_second, peaks = lax.optimization_barrier((rim_first, rim_second, peaks))
+    rim_first, peaks = lax.optimization_barrier((rim_first, peaks))
     x_rims = swap(rim_first, rim_second, "gx")
     peaks = jnp.broadcast_to(jnp.max(peaks, axis=0, keepdims=True), (peers_y, PTS))
     peaks = lax.all_to_all(peaks, "gy", 0, 0, tiled=True)

time: 77.7 us -> 75.4 us (0.970)
  the two profiles are of different devices: /device:TPU:14 before, /device:TPU:6 now
where the time goes in v5:
time: 75.4 us; the launch traced here: 75 us
  starting transfers between devices  46.8 us (62%)
  Pallas kernels  18.8 us (25%)
  waiting for transfers between devices  6.44 us (9%)
  local copies, waits for them, and re-layouts  1.78 us (2%)
  between operations  0.96 us (1%)
    all_to_all x1, starting transfers between devices, local(): peaks = lax.all_to_all(peak, 'gx', 0, 0, tiled=True)  13.1 us
    ppermute x4, starting transfers between devices, swap(): lax.ppermute(second, axis, with_second)  12.9 us
    all_to_all x1, starting transfers between devices, local(): peaks = lax.all_to_all(peaks, 'gy', 0, 0, tiled=True)  11 us
    ppermute x4, starting transfers between devices, swap(): lax.ppermute(first, axis, with_first)  9.86 us
    pallas_call x1, Pallas kernels, local(): totals = inside(neighbours, *pieces)[0]  7.47 us
    pallas_call x1, Pallas kernels, local(): force(displacement, strength, corners, *x_halos, *y_halos)  4.71 us
    pallas_call x1, Pallas kernels, local(): rim(stiffness, neighbours, totals, own_pieces, info, *x_halos, *y_halos)  4.15 us
    ppermute x4, waiting for transfers between devices, swap(): lax.ppermute(second, axis, with_second)  3.59 us
  transfers between devices with their start and end apart: 10, of which 3 were waited for; matrix products, arithmetic and copies ran while one was open for 1% of the time, Pallas kernels for 19%

profile of v5, /device:TPU:6, one launch (start us, length us, event | category | flops | bytes accessed | tf_op | source)
XLA Modules:
  0.0 75.0 jit_solution(2103725351869326211)
XLA Ops:
  0.6 0.0 copy-start.2
  0.6 0.0 copy-start.1
  0.7 0.9 %dynamic-slice_bitcast_fusion = (f32[5,16,128]{2,1,0:T(8,128)S(1)}, f32[5,16,128]{2,1,0:T(8,128)S(1)}) fusion(f32[5,4,16,128]{3,2,1,0:T(8,128)} %strain.1, s32[]{:T(128)S(6)} %select_n.83, s32[]{:T(128)S(6)} %select_n.82), kind=kLoop, calls=%fused_computation.6 | loop fusion | bytes 163848 | tf_op jit(solution)/shard_map/jit(dynamic_index_in_dim)/squeeze | solution.py:550
  1.5 0.0 copy-done.2
  1.5 0.0 copy-done.1
  1.6 0.0 copy-start
  1.6 2.1 %collective-permute-start = (f32[11,16,128]{2,1,0:T(8,128)S(1)}, f32[11,16,128]{2,1,0:T(8,128)S(1)}, u32[]{:S(2)}, u32[]{:S(2)}) collective-permute-start(f32[11,16,128]{2,1,0:T(8,128)S(1)} %pad_maximum_fusion), channel_id=1, source_target_pairs={{0,16},{16,0},{32,48},{48,32},{64,80},{80,64},{96,112},{112,96},{1... | collective-permute-start | bytes 270344 | tf_op jit(solution)/shard_map/ppermute | solution.py:541
  3.7 0.7 collective-permute-start.1
  4.4 0.0 copy-done
  4.4 1.7 %split_block.1 = (f32[2048,128]{1,0:T(8,128)S(1)}, bf16[2304,128]{1,0:T(8,128)(2,1)S(1)}, f32[576,128]{1,0:T(8,128)S(1)}, f32[8,128]{1,0:T(8,128)S(1)}) custom-call(f32[5,4,16,128]{3,2,1,0:T(8,128)S(1)} %copy-done, f32[3,4,16,128]{3,2,1,0:T(8,128)S(1)} %copy-done.1), custom_call_target="tpu_custom_call" | custom-call | flops 3000000000 | bytes 1048576 | tf_op jit(solution)/shard_map/split_block/pallas_call | solution.py:557
  6.2 0.0 collective-permute-done.x_first
  6.2 0.0 collective-permute-done.1.x_second
  6.3 2.7 %collective-permute-start.2 = (f32[11,6,128]{2,1,0:T(8,128)S(1)}, f32[11,6,128]{2,1,0:T(8,128)S(1)}, u32[]{:S(2)}, u32[]{:S(2)}) collective-permute-start(f32[11,6,128]{2,1,0:T(8,128)S(1)} %pad_maximum_fusion.2), channel_id=1, source_target_pairs={{0,1},{1,0},{2,3},{3,2},{4,5},{5,4},{6,7},{7,6},{8,9},{9,8},{10,11... | collective-permute-start | bytes 101384 | tf_op jit(solution)/shard_map/ppermute | solution.py:541
  9.0 0.0 copy-start.5
  9.1 0.0 copy-start.4
  9.1 6.7 %collective-permute-start.3 = (f32[11,6,128]{2,1,0:T(8,128)S(1)}, f32[11,6,128]{2,1,0:T(8,128)S(1)}, u32[]{:S(2)}, u32[]{:S(2)}) collective-permute-start(f32[11,6,128]{2,1,0:T(8,128)S(1)} %pad_maximum_fusion.3), channel_id=1, source_target_pairs={{1,2},{2,1},{3,4},{4,3},{5,6},{6,5},{7,8},{8,7},{9,10},{10,9},{11,... | collective-permute-start | bytes 101384 | tf_op jit(solution)/shard_map/ppermute | solution.py:541
  15.8 0.0 copy-done.5
  15.8 7.5 %inside_links.1.inside = f32[512,128]{1,0:T(8,128)S(1)} custom-call(s32[9,4,16]{2,1,0:T(4,128)S(1)} %copy-done.5, f32[2048,128]{1,0:T(8,128)S(1)} %get-tuple-element.74.su, bf16[2304,128]{1,0:T(8,128)(2,1)S(1)} %get-tuple-element.75.vt, f32[576,128]{1,0:T(8,128)S(1)} %get-tuple-element.76.src, f32[8,128]{1,0:T(8,128)S(1)} %get-tuple-element.77.info), custom_call_target="tpu_custom_call" | custom-call | flops 6000000000 | bytes 1048576 | tf_op jit(solution)/shard_map/inside_links/pallas_call | solution.py:568
  23.3 0.0 copy-start.3
  23.3 0.0 collective-permute-done.2.y_first
  23.3 0.0 collective-permute-done.3.y_second
  23.3 0.0 copy-done.4
  23.3 4.1 %rim_links.1 = (f32[5,4,16,128]{3,2,1,0:T(8,128)}, f32[4,16,128]{2,1,0:T(8,128)S(1)}, f32[32,128]{1,0:T(8,128)}) custom-call(f32[1,4,16,128]{3,2,1,0:T(8,128)S(1)} %copy-done.4, s32[9,4,16]{2,1,0:T(4,128)S(1)} %copy-done.5, f32[512,128]{1,0:T(8,128)S(1)} %inside_links.1.inside, f32[2048,128]{1,0:T(8,128)S(1)} %get-tuple-element.74.su, ...), custom_call_target="tpu_custom_call" | custom-call | flops 4000000000 | bytes 1048576 | tf_op jit(solution)/shard_map/rim_links/pallas_call | solution.py:569
  27.5 13.1 %all-to-all-start = ((f32[32,1,128]{2,1,0:T(1,128)}), f32[32,1,128]{2,1,0:T(1,128)S(1)}, u32[]{:S(2)}, u32[]{:S(2)}) async-start(f32[32,1,128]{2,1,0:T(1,128)} %bitcast.13), calls=%async_computation | async-start | bytes 32768 | tf_op jit(solution)/shard_map/all_to_all | solution.py:570
  40.5 0.0 copy-done.3
  40.6 4.7 %node_forces.1 = (f32[3,4,16,128]{3,2,1,0:T(8,128)S(1)}, f32[3,18,128]{2,1,0:T(8,128)S(1)}, f32[3,18,128]{2,1,0:T(8,128)S(1)}, f32[3,4,128]{2,1,0:T(4,128)S(1)}, f32[3,4,128]{2,1,0:T(4,128)S(1)}) custom-call(f32[3,4,16,128]{3,2,1,0:T(8,128)S(1)} %copy-done.2, f32[4,16,128]{2,1,0:T(8,128)S(1)} %get-tuple-element.81.strength, s32[4,4,16,128]{3,2,1,0:T(8,128)S(1)} %copy-done.3, ...), custom_call_target="tpu_custom_call" | custom-call | flops 8000000000 | bytes 1048576 | tf_op jit(solution)/shard_map/node_forces/pallas_call | solution.py:571
  45.3 0.7 collective-permute-start.5
  45.9 2.8 %all-to-all-done = f32[32,1,128]{2,1,0:T(1,128)S(1)} async-done(((f32[32,1,128]{2,1,0:T(1,128)}), f32[32,1,128]{2,1,0:T(1,128)S(1)}, u32[]{:S(2)}, u32[]{:S(2)}) %all-to-all-start) | async-done | bytes 16416 | tf_op jit(solution)/shard_map/all_to_all | solution.py:570
  48.7 2.3 %collective-permute-start.4 = (f32[3,18,128]{2,1,0:T(8,128)S(1)}, f32[3,18,128]{2,1,0:T(8,128)S(1)}, u32[]{:S(2)}, u32[]{:S(2)}) collective-permute-start(f32[3,18,128]{2,1,0:T(8,128)S(1)} %get-tuple-element.85), channel_id=1, source_target_pairs={{0,16},{16,0},{32,48},{48,32},{64,80},{80,64},{96,112},{112,96},{1... | collective-permute-start | bytes 82952 | tf_op jit(solution)/shard_map/ppermute | solution.py:541
  51.0 0.6 broadcast_in_dim.2
  51.6 11.0 %all-to-all-start.1 = ((f32[16,1,128]{2,1,0:T(1,128)}), f32[16,1,128]{2,1,0:T(1,128)S(1)}, u32[]{:S(2)}, u32[]{:S(2)}) async-start(f32[16,1,128]{2,1,0:T(1,128)} %broadcast_in_dim.2), calls=%async_computation.1 | async-start | bytes 16384 | tf_op jit(solution)/shard_map/all_to_all | solution.py:575
  62.7 0.0 collective-permute-done.5.x_second
  62.7 0.0 collective-permute-done.4.x_first
  62.9 2.8 %collective-permute-start.6 = (f32[3,4,128]{2,1,0:T(4,128)S(1)}, f32[3,4,128]{2,1,0:T(4,128)S(1)}, u32[]{:S(2)}, u32[]{:S(2)}) collective-permute-start(f32[3,4,128]{2,1,0:T(4,128)S(1)} %get-tuple-element.115), channel_id=1, source_target_pairs={{0,1},{1,0},{2,3},{3,2},{4,5},{5,4},{6,7},{7,6},{8,9},{9,8},{10,11... | collective-permute-start | bytes 18440 | tf_op jit(solution)/shard_map/ppermute | solution.py:541
  65.7 4.9 %collective-permute-start.7 = (f32[3,4,128]{2,1,0:T(4,128)S(1)}, f32[3,4,128]{2,1,0:T(4,128)S(1)}, u32[]{:S(2)}, u32[]{:S(2)}) collective-permute-start(f32[3,4,128]{2,1,0:T(4,128)S(1)} %get-tuple-element.114), channel_id=1, source_target_pairs={{1,2},{2,1},{3,4},{4,3},{5,6},{6,5},{7,8},{8,7},{9,10},{10,9},{11,... | collective-permute-start | bytes 18440 | tf_op jit(solution)/shard_map/ppermute | solution.py:541
  70.5 0.1 all-to-all-done.1
  70.6 0.0 collective-permute-done.6.y_first
  70.6 3.6 %collective-permute-done.7.y_second = f32[3,4,128]{2,1,0:T(4,128)S(1)} collective-permute-done((f32[3,4,128]{2,1,0:T(4,128)S(1)}, f32[3,4,128]{2,1,0:T(4,128)S(1)}, u32[]{:S(2)}, u32[]{:S(2)}) %collective-permute-start.7) | collective-permute-done | bytes 6176 | tf_op jit(solution)/shard_map/ppermute | solution.py:541
  74.2 0.8 %finish.1 = f32[3,4,16,128]{3,2,1,0:T(8,128)} custom-call(f32[3,4,16,128]{3,2,1,0:T(8,128)S(1)} %get-tuple-element.82.inner, f32[3,18,128]{2,1,0:T(8,128)S(1)} %collective-permute-done.4.x_first, f32[3,18,128]{2,1,0:T(8,128)S(1)} %collective-permute-done.5.x_second, f32[3,4,128]{2,1,0:T(4,128)S(1)} %collective-permute-done.6.y_first, ...), custom_call_target="tpu_custom_call" | custom-call | flops 1000000 | bytes 1048576 | tf_op jit(solution)/shard_map/finish/pallas_call | solution.py:584
  (19 shorter events, 0.4 us)
Async XLA Ops:
  0.6 0.9 %copy-start.2 = (f32[3,4,16,128]{3,2,1,0:T(8,128)S(1)}, f32[3,4,16,128]{3,2,1,0:T(8,128)}, u32[]{:S(2)}) copy-start(f32[3,4,16,128]{3,2,1,0:T(8,128)} %disp.1) | copy-start | bytes 294916
  0.6 0.9 %copy-start.1 = (f32[3,4,16,128]{3,2,1,0:T(8,128)S(1)}, f32[3,4,16,128]{3,2,1,0:T(8,128)}, u32[]{:S(2)}) copy-start(f32[3,4,16,128]{3,2,1,0:T(8,128)} %coords.1) | copy-start | bytes 294916
  1.6 2.8 %copy-start = (f32[5,4,16,128]{3,2,1,0:T(8,128)S(1)}, f32[5,4,16,128]{3,2,1,0:T(8,128)}, u32[]{:S(2)}) copy-start(f32[5,4,16,128]{3,2,1,0:T(8,128)} %strain.1) | copy-start | bytes 491524
  1.6 4.6 %collective-permute-start = (f32[11,16,128]{2,1,0:T(8,128)S(1)}, f32[11,16,128]{2,1,0:T(8,128)S(1)}, u32[]{:S(2)}, u32[]{:S(2)}) collective-permute-start(f32[11,16,128]{2,1,0:T(8,128)S(1)} %pad_maximum_fusion), channel_id=1, source_target_pairs={{0,16},{16,0},{32,48},{48,32},{64,80},{80,64},{96,112},{112,96},{1... | collective-permute-start | bytes 270344 | tf_op jit(solution)/shard_map/ppermute | solution.py:541
  3.7 2.5 %collective-permute-start.1 = (f32[11,16,128]{2,1,0:T(8,128)S(1)}, f32[11,16,128]{2,1,0:T(8,128)S(1)}, u32[]{:S(2)}, u32[]{:S(2)}) collective-permute-start(f32[11,16,128]{2,1,0:T(8,128)S(1)} %pad_maximum_fusion.1), channel_id=1, source_target_pairs={{16,32},{32,16},{48,64},{64,48},{80,96},{96,80},{112,128},{128,112... | collective-permute-start | bytes 270344 | tf_op jit(solution)/shard_map/ppermute | solution.py:541
  6.3 17.0 %collective-permute-start.2 = (f32[11,6,128]{2,1,0:T(8,128)S(1)}, f32[11,6,128]{2,1,0:T(8,128)S(1)}, u32[]{:S(2)}, u32[]{:S(2)}) collective-permute-start(f32[11,6,128]{2,1,0:T(8,128)S(1)} %pad_maximum_fusion.2), channel_id=1, source_target_pairs={{0,1},{1,0},{2,3},{3,2},{4,5},{5,4},{6,7},{7,6},{8,9},{9,8},{10,11... | collective-permute-start | bytes 101384 | tf_op jit(solution)/shard_map/ppermute | solution.py:541
  9.0 6.7 %copy-start.5 = (s32[9,4,16]{2,1,0:T(4,128)S(1)}, s32[9,4,16]{2,1,0:T(4,128)}, u32[]{:S(2)}) copy-start(s32[9,4,16]{2,1,0:T(4,128)} %links.3) | copy-start | bytes 6916
  9.1 14.2 %copy-start.4 = (f32[1,4,16,128]{3,2,1,0:T(8,128)S(1)}, f32[1,4,16,128]{3,2,1,0:T(8,128)}, u32[]{:S(2)}) copy-start(f32[1,4,16,128]{3,2,1,0:T(8,128)} %stiff.1) | copy-start | bytes 98308
  9.1 14.2 %collective-permute-start.3 = (f32[11,6,128]{2,1,0:T(8,128)S(1)}, f32[11,6,128]{2,1,0:T(8,128)S(1)}, u32[]{:S(2)}, u32[]{:S(2)}) collective-permute-start(f32[11,6,128]{2,1,0:T(8,128)S(1)} %pad_maximum_fusion.3), channel_id=1, source_target_pairs={{1,2},{2,1},{3,4},{4,3},{5,6},{6,5},{7,8},{8,7},{9,10},{10,9},{11,... | collective-permute-start | bytes 101384 | tf_op jit(solution)/shard_map/ppermute | solution.py:541
  23.3 17.3 %copy-start.3 = (s32[4,4,16,128]{3,2,1,0:T(8,128)S(1)}, s32[4,4,16,128]{3,2,1,0:T(8,128)}, u32[]{:S(2)}) copy-start(s32[4,4,16,128]{3,2,1,0:T(8,128)} %corners.1) | copy-start | bytes 393220
  27.5 21.2 %all-to-all-start = ((f32[32,1,128]{2,1,0:T(1,128)}), f32[32,1,128]{2,1,0:T(1,128)S(1)}, u32[]{:S(2)}, u32[]{:S(2)}) async-start(f32[32,1,128]{2,1,0:T(1,128)} %bitcast.13), calls=%async_computation | async-start | bytes 32768 | tf_op jit(solution)/shard_map/all_to_all | solution.py:570
  45.3 17.4 %collective-permute-start.5 = (f32[3,18,128]{2,1,0:T(8,128)S(1)}, f32[3,18,128]{2,1,0:T(8,128)S(1)}, u32[]{:S(2)}, u32[]{:S(2)}) collective-permute-start(f32[3,18,128]{2,1,0:T(8,128)S(1)} %get-tuple-element.86), channel_id=1, source_target_pairs={{16,32},{32,16},{48,64},{64,48},{80,96},{96,80},{112,128},{128,112... | collective-permute-start | bytes 82952 | tf_op jit(solution)/shard_map/ppermute | solution.py:541
  48.7 14.0 %collective-permute-start.4 = (f32[3,18,128]{2,1,0:T(8,128)S(1)}, f32[3,18,128]{2,1,0:T(8,128)S(1)}, u32[]{:S(2)}, u32[]{:S(2)}) collective-permute-start(f32[3,18,128]{2,1,0:T(8,128)S(1)} %get-tuple-element.85), channel_id=1, source_target_pairs={{0,16},{16,0},{32,48},{48,32},{64,80},{80,64},{96,112},{112,96},{1... | collective-permute-start | bytes 82952 | tf_op jit(solution)/shard_map/ppermute | solution.py:541
  51.6 19.0 %all-to-all-start.1 = ((f32[16,1,128]{2,1,0:T(1,128)}), f32[16,1,128]{2,1,0:T(1,128)S(1)}, u32[]{:S(2)}, u32[]{:S(2)}) async-start(f32[16,1,128]{2,1,0:T(1,128)} %broadcast_in_dim.2), calls=%async_computation.1 | async-start | bytes 16384 | tf_op jit(solution)/shard_map/all_to_all | solution.py:575
  62.9 7.7 %collective-permute-start.6 = (f32[3,4,128]{2,1,0:T(4,128)S(1)}, f32[3,4,128]{2,1,0:T(4,128)S(1)}, u32[]{:S(2)}, u32[]{:S(2)}) collective-permute-start(f32[3,4,128]{2,1,0:T(4,128)S(1)} %get-tuple-element.115), channel_id=1, source_target_pairs={{0,1},{1,0},{2,3},{3,2},{4,5},{5,4},{6,7},{7,6},{8,9},{9,8},{10,11... | collective-permute-start | bytes 18440 | tf_op jit(solution)/shard_map/ppermute | solution.py:541
  65.7 8.5 %collective-permute-start.7 = (f32[3,4,128]{2,1,0:T(4,128)S(1)}, f32[3,4,128]{2,1,0:T(4,128)S(1)}, u32[]{:S(2)}, u32[]{:S(2)}) collective-permute-start(f32[3,4,128]{2,1,0:T(4,128)S(1)} %get-tuple-element.114), channel_id=1, source_target_pairs={{1,2},{2,1},{3,4},{4,3},{5,6},{6,5},{7,8},{8,7},{9,10},{10,9},{11,... | collective-permute-start | bytes 18440 | tf_op jit(solution)/shard_map/ppermute | solution.py:541

commit v6 on v5

--- a/solution.py
+++ b/solution.py
@@ -133,7 +133,7 @@
         vt[rows_at(c + 1, PTS), :] = sv[rows_at(c, step), :].T.astype(bf16)
         return carry
 
-    lax.fori_loop(0, COLS, turn, 0, unroll=8)
+    lax.fori_loop(0, COLS, turn, 0, unroll=16)
 
 
 def inside_body(links, su, vt, src, info, totals, block, weights):
@@ -203,10 +203,9 @@
     totals[...] = inside[...]
     for c in range(EXT_COLS):
         for h in range(2):
-            sv[pl.ds(c * PTS + h * PIECES + 16, 8), :] = other_const
-            sv[pl.ds(c * PTS + h * PIECES + 24, 8), :] = zero8
+            sv[pl.ds((2 * c + h) * PIECES + 16, 8), :] = other_const
+            sv[pl.ds((2 * c + h) * PIECES + 24, 8), :] = zero8
             src[pl.ds(((h * LAST) * EXT_COLS + c) * 8, 8), :] = ones
-        sv[pl.ds(c * PTS + 64, 64), :] = jnp.zeros((64, PTS), f32)
     for r in range(ROWS):
         for h in range(2):
             sides[pl.ds((h * ROWS + r) * PIECES + 16, 8), :] = other_const
@@ -221,7 +220,7 @@
         xyz = [halo(x) for x in range(3)]
         a, norm = scaled(xyz, centre)
         far = jnp.maximum(far, jnp.where(there, norm, 0.0))
-        put_other(sv, a, norm, lambda k: pl.ds(PTS + h * PIECES + k, COLS, stride=PTS))
+        put_other(sv, a, norm, lambda k: pl.ds((2 + h) * PIECES + k, COLS, stride=2 * PIECES))
         first = (h * LAST * EXT_COLS + 1) * 8
         for x in range(3):
             raw[pl.ds(first + x, COLS, stride=8), :] = xyz[x]
@@ -239,7 +238,7 @@
         col = h * (EXT_COLS - 1)
         for e in range(2):
             one = slice(e * LAST, e * LAST + 1)
-            put_other(sv, [v[one] for v in a], norm[one], lambda k: pl.ds(col * PTS + e * PIECES + k, 1))
+            put_other(sv, [v[one] for v in a], norm[one], lambda k: pl.ds((2 * col + e) * PIECES + k, 1))
         for x in range(3):
             raw[pl.ds(col * 8 + x, EXT_ROWS, stride=EXT_COLS * 8), :] = xyz[x]
         for l in range(LAYERS):
@@ -253,7 +252,7 @@
     @pl.when(near)
     def _():
         def turn(c, carry):
-            vt[rows_at(c, PTS), :] = sv[rows_at(c, PTS), :].T.astype(bf16)
+            vt[rows_at(c, PTS), :] = sv[rows_at(c, 2 * PIECES), :].T.astype(bf16)
             return carry
 
         lax.fori_loop(0, EXT_COLS, turn, 0, unroll=18)
@@ -271,8 +270,7 @@
             for h in range(2):
                 own = su[rows_at(c * ROWS + h * (ROWS - 1), PIECES), :].astype(bf16)
                 block[rows_at(2 * c + h, PIECES), pl.ds(h * PTS, PTS)] = own
-            here = block[rows_at(c, 2 * PIECES), :]
-            own = jnp.concatenate([here, jnp.zeros((64, 2 * PTS), bf16)], axis=0)
+            own = block[rows_at(c, 2 * PIECES), :]
             weights[rows_at(c, 3 * PTS), :] = bell_weights(vt[rows_at(c, PTS, 3 * PTS), :], own)
             return carry
 
@@ -492,9 +490,9 @@
         ("stiff", "links", "inside", "su", "info", "x_first", "x_second", "y_first", "y_second"),
         [((LAYERS, ROWS, COLS, PTS), f32), ((ROWS, COLS, PTS), f32), ((peers, PTS), f32)],
         [
-            ((EXT_COLS * PTS, PTS), f32),
+            ((EXT_COLS * 2 * PIECES, PTS), f32),
             ((2 * PTS, PTS), f32),
-            ((EXT_COLS * PTS, PTS), bf16),
+            ((EXT_COLS * PTS, 2 * PIECES), bf16),
             ((PTS, 2 * PTS), bf16),
             ((COLS * 2 * PIECES, 2 * PTS), bf16),
             ((2 * PTS, 2 * len(INSIDE) * PTS), bf16),

time: 75.4 us -> 75.4 us (level)
  transfers between devices with their start and end apart: 10 -> 10, of which waited for: 3 -> 3; matrix products, arithmetic and copies ran while one was open for 1% -> 1% of each run, Pallas kernels for 19% -> 18%
where the time goes in v6:
time: 75.4 us; the launch traced here: 74.9 us
  starting transfers between devices  46.9 us (62%)
  Pallas kernels  18.7 us (25%)
  waiting for transfers between devices  6.45 us (9%)
  local copies, waits for them, and re-layouts  1.78 us (2%)
  between operations  0.96 us (1%)
    all_to_all x1, starting transfers between devices, local(): peaks = lax.all_to_all(peak, 'gx', 0, 0, tiled=True)  13.1 us
    ppermute x4, starting transfers between devices, swap(): lax.ppermute(second, axis, with_second)  12.9 us
    all_to_all x1, starting transfers between devices, local(): peaks = lax.all_to_all(peaks, 'gy', 0, 0, tiled=True)  11 us
    ppermute x4, starting transfers between devices, swap(): lax.ppermute(first, axis, with_first)  9.86 us
    pallas_call x1, Pallas kernels, local(): totals = inside(neighbours, *pieces)[0]  7.47 us
    pallas_call x1, Pallas kernels, local(): force(displacement, strength, corners, *x_halos, *y_halos)  4.7 us
    pallas_call x1, Pallas kernels, local(): rim(stiffness, neighbours, totals, own_pieces, info, *x_halos, *y_halos)  4.11 us
    ppermute x4, waiting for transfers between devices, swap(): lax.ppermute(second, axis, with_second)  3.57 us
  transfers between devices with their start and end apart: 10, of which 3 were waited for; matrix products, arithmetic and copies ran while one was open for 1% of the time, Pallas kernels for 18%

profile of v6, /device:TPU:6, one launch (start us, length us, event | category | flops | bytes accessed | tf_op | source)
XLA Modules:
  0.0 74.9 jit_solution(4638526693989067285)
XLA Ops:
  0.6 0.0 copy-start.2
  0.6 0.0 copy-start.1
  0.7 0.9 %dynamic-slice_bitcast_fusion = (f32[5,16,128]{2,1,0:T(8,128)S(1)}, f32[5,16,128]{2,1,0:T(8,128)S(1)}) fusion(f32[5,4,16,128]{3,2,1,0:T(8,128)} %strain.1, s32[]{:T(128)S(6)} %select_n.83, s32[]{:T(128)S(6)} %select_n.82), kind=kLoop, calls=%fused_computation.6 | loop fusion | bytes 163848 | tf_op jit(solution)/shard_map/jit(dynamic_index_in_dim)/squeeze | solution.py:548
  1.5 0.0 copy-done.2
  1.5 0.0 copy-done.1
  1.6 0.0 copy-start
  1.6 2.1 %collective-permute-start = (f32[11,16,128]{2,1,0:T(8,128)S(1)}, f32[11,16,128]{2,1,0:T(8,128)S(1)}, u32[]{:S(2)}, u32[]{:S(2)}) collective-permute-start(f32[11,16,128]{2,1,0:T(8,128)S(1)} %pad_maximum_fusion), channel_id=1, source_target_pairs={{0,16},{16,0},{32,48},{48,32},{64,80},{80,64},{96,112},{112,96},{1... | collective-permute-start | bytes 270344 | tf_op jit(solution)/shard_map/ppermute | solution.py:539
  3.7 0.7 collective-permute-start.1
  4.4 0.0 copy-done
  4.4 1.6 %split_block.1 = (f32[2048,128]{1,0:T(8,128)S(1)}, bf16[2304,128]{1,0:T(8,128)(2,1)S(1)}, f32[576,128]{1,0:T(8,128)S(1)}, f32[8,128]{1,0:T(8,128)S(1)}) custom-call(f32[5,4,16,128]{3,2,1,0:T(8,128)S(1)} %copy-done, f32[3,4,16,128]{3,2,1,0:T(8,128)S(1)} %copy-done.1), custom_call_target="tpu_custom_call" | custom-call | flops 3000000000 | bytes 1048576 | tf_op jit(solution)/shard_map/split_block/pallas_call | solution.py:555
  6.1 0.0 collective-permute-done.x_first
  6.1 0.0 collective-permute-done.1.x_second
  6.2 2.7 %collective-permute-start.2 = (f32[11,6,128]{2,1,0:T(8,128)S(1)}, f32[11,6,128]{2,1,0:T(8,128)S(1)}, u32[]{:S(2)}, u32[]{:S(2)}) collective-permute-start(f32[11,6,128]{2,1,0:T(8,128)S(1)} %pad_maximum_fusion.2), channel_id=1, source_target_pairs={{0,1},{1,0},{2,3},{3,2},{4,5},{5,4},{6,7},{7,6},{8,9},{9,8},{10,11... | collective-permute-start | bytes 101384 | tf_op jit(solution)/shard_map/ppermute | solution.py:539
  9.0 0.0 copy-start.5
  9.0 0.0 copy-start.4
  9.0 6.7 %collective-permute-start.3 = (f32[11,6,128]{2,1,0:T(8,128)S(1)}, f32[11,6,128]{2,1,0:T(8,128)S(1)}, u32[]{:S(2)}, u32[]{:S(2)}) collective-permute-start(f32[11,6,128]{2,1,0:T(8,128)S(1)} %pad_maximum_fusion.3), channel_id=1, source_target_pairs={{1,2},{2,1},{3,4},{4,3},{5,6},{6,5},{7,8},{8,7},{9,10},{10,9},{11,... | collective-permute-start | bytes 101384 | tf_op jit(solution)/shard_map/ppermute | solution.py:539
  15.7 0.0 copy-done.5
  15.7 7.5 %inside_links.1.inside = f32[512,128]{1,0:T(8,128)S(1)} custom-call(s32[9,4,16]{2,1,0:T(4,128)S(1)} %copy-done.5, f32[2048,128]{1,0:T(8,128)S(1)} %get-tuple-element.74.su, bf16[2304,128]{1,0:T(8,128)(2,1)S(1)} %get-tuple-element.75.vt, f32[576,128]{1,0:T(8,128)S(1)} %get-tuple-element.76.src, f32[8,128]{1,0:T(8,128)S(1)} %get-tuple-element.77.info), custom_call_target="tpu_custom_call" | custom-call | flops 6000000000 | bytes 1048576 | tf_op jit(solution)/shard_map/inside_links/pallas_call | solution.py:566
  23.2 0.0 copy-start.3
  23.2 0.0 collective-permute-done.2.y_first
  23.2 0.0 collective-permute-done.3.y_second
  23.2 0.0 copy-done.4
  23.2 4.1 %rim_links.1 = (f32[5,4,16,128]{3,2,1,0:T(8,128)}, f32[4,16,128]{2,1,0:T(8,128)S(1)}, f32[32,128]{1,0:T(8,128)}) custom-call(f32[1,4,16,128]{3,2,1,0:T(8,128)S(1)} %copy-done.4, s32[9,4,16]{2,1,0:T(4,128)S(1)} %copy-done.5, f32[512,128]{1,0:T(8,128)S(1)} %inside_links.1.inside, f32[2048,128]{1,0:T(8,128)S(1)} %get-tuple-element.74.su, ...), custom_call_target="tpu_custom_call" | custom-call | flops 4000000000 | bytes 1048576 | tf_op jit(solution)/shard_map/rim_links/pallas_call | solution.py:567
  27.4 13.1 %all-to-all-start = ((f32[32,1,128]{2,1,0:T(1,128)}), f32[32,1,128]{2,1,0:T(1,128)S(1)}, u32[]{:S(2)}, u32[]{:S(2)}) async-start(f32[32,1,128]{2,1,0:T(1,128)} %bitcast.13), calls=%async_computation | async-start | bytes 32768 | tf_op jit(solution)/shard_map/all_to_all | solution.py:568
  40.5 0.0 copy-done.3
  40.5 4.7 %node_forces.1 = (f32[3,4,16,128]{3,2,1,0:T(8,128)S(1)}, f32[3,18,128]{2,1,0:T(8,128)S(1)}, f32[3,18,128]{2,1,0:T(8,128)S(1)}, f32[3,4,128]{2,1,0:T(4,128)S(1)}, f32[3,4,128]{2,1,0:T(4,128)S(1)}) custom-call(f32[3,4,16,128]{3,2,1,0:T(8,128)S(1)} %copy-done.2, f32[4,16,128]{2,1,0:T(8,128)S(1)} %get-tuple-element.81.strength, s32[4,4,16,128]{3,2,1,0:T(8,128)S(1)} %copy-done.3, ...), custom_call_target="tpu_custom_call" | custom-call | flops 8000000000 | bytes 1048576 | tf_op jit(solution)/shard_map/node_forces/pallas_call | solution.py:569
  45.2 0.7 collective-permute-start.5
  45.9 2.8 %all-to-all-done = f32[32,1,128]{2,1,0:T(1,128)S(1)} async-done(((f32[32,1,128]{2,1,0:T(1,128)}), f32[32,1,128]{2,1,0:T(1,128)S(1)}, u32[]{:S(2)}, u32[]{:S(2)}) %all-to-all-start) | async-done | bytes 16416 | tf_op jit(solution)/shard_map/all_to_all | solution.py:568
  48.7 2.3 %collective-permute-start.4 = (f32[3,18,128]{2,1,0:T(8,128)S(1)}, f32[3,18,128]{2,1,0:T(8,128)S(1)}, u32[]{:S(2)}, u32[]{:S(2)}) collective-permute-start(f32[3,18,128]{2,1,0:T(8,128)S(1)} %get-tuple-element.85), channel_id=1, source_target_pairs={{0,16},{16,0},{32,48},{48,32},{64,80},{80,64},{96,112},{112,96},{1... | collective-permute-start | bytes 82952 | tf_op jit(solution)/shard_map/ppermute | solution.py:539
  51.0 0.6 broadcast_in_dim.2
  51.6 11.0 %all-to-all-start.1 = ((f32[16,1,128]{2,1,0:T(1,128)}), f32[16,1,128]{2,1,0:T(1,128)S(1)}, u32[]{:S(2)}, u32[]{:S(2)}) async-start(f32[16,1,128]{2,1,0:T(1,128)} %broadcast_in_dim.2), calls=%async_computation.1 | async-start | bytes 16384 | tf_op jit(solution)/shard_map/all_to_all | solution.py:573
  62.6 0.0 collective-permute-done.5.x_second
  62.6 0.0 collective-permute-done.4.x_first
  62.8 2.8 %collective-permute-start.6 = (f32[3,4,128]{2,1,0:T(4,128)S(1)}, f32[3,4,128]{2,1,0:T(4,128)S(1)}, u32[]{:S(2)}, u32[]{:S(2)}) collective-permute-start(f32[3,4,128]{2,1,0:T(4,128)S(1)} %get-tuple-element.115), channel_id=1, source_target_pairs={{0,1},{1,0},{2,3},{3,2},{4,5},{5,4},{6,7},{7,6},{8,9},{9,8},{10,11... | collective-permute-start | bytes 18440 | tf_op jit(solution)/shard_map/ppermute | solution.py:539
  65.6 4.9 %collective-permute-start.7 = (f32[3,4,128]{2,1,0:T(4,128)S(1)}, f32[3,4,128]{2,1,0:T(4,128)S(1)}, u32[]{:S(2)}, u32[]{:S(2)}) collective-permute-start(f32[3,4,128]{2,1,0:T(4,128)S(1)} %get-tuple-element.114), channel_id=1, source_target_pairs={{1,2},{2,1},{3,4},{4,3},{5,6},{6,5},{7,8},{8,7},{9,10},{10,9},{11,... | collective-permute-start | bytes 18440 | tf_op jit(solution)/shard_map/ppermute | solution.py:539
  70.5 0.1 all-to-all-done.1
  70.6 0.0 collective-permute-done.6.y_first
  70.6 3.6 %collective-permute-done.7.y_second = f32[3,4,128]{2,1,0:T(4,128)S(1)} collective-permute-done((f32[3,4,128]{2,1,0:T(4,128)S(1)}, f32[3,4,128]{2,1,0:T(4,128)S(1)}, u32[]{:S(2)}, u32[]{:S(2)}) %collective-permute-start.7) | collective-permute-done | bytes 6176 | tf_op jit(solution)/shard_map/ppermute | solution.py:539
  74.2 0.8 %finish.1 = f32[3,4,16,128]{3,2,1,0:T(8,128)} custom-call(f32[3,4,16,128]{3,2,1,0:T(8,128)S(1)} %get-tuple-element.82.inner, f32[3,18,128]{2,1,0:T(8,128)S(1)} %collective-permute-done.4.x_first, f32[3,18,128]{2,1,0:T(8,128)S(1)} %collective-permute-done.5.x_second, f32[3,4,128]{2,1,0:T(4,128)S(1)} %collective-permute-done.6.y_first, ...), custom_call_target="tpu_custom_call" | custom-call | flops 1000000 | bytes 1048576 | tf_op jit(solution)/shard_map/finish/pallas_call | solution.py:582
  (19 shorter events, 0.4 us)
Async XLA Ops:
  0.6 0.9 %copy-start.2 = (f32[3,4,16,128]{3,2,1,0:T(8,128)S(1)}, f32[3,4,16,128]{3,2,1,0:T(8,128)}, u32[]{:S(2)}) copy-start(f32[3,4,16,128]{3,2,1,0:T(8,128)} %disp.1) | copy-start | bytes 294916
  0.6 0.9 %copy-start.1 = (f32[3,4,16,128]{3,2,1,0:T(8,128)S(1)}, f32[3,4,16,128]{3,2,1,0:T(8,128)}, u32[]{:S(2)}) copy-start(f32[3,4,16,128]{3,2,1,0:T(8,128)} %coords.1) | copy-start | bytes 294916
  1.6 2.8 %copy-start = (f32[5,4,16,128]{3,2,1,0:T(8,128)S(1)}, f32[5,4,16,128]{3,2,1,0:T(8,128)}, u32[]{:S(2)}) copy-start(f32[5,4,16,128]{3,2,1,0:T(8,128)} %strain.1) | copy-start | bytes 491524
  1.6 4.5 %collective-permute-start = (f32[11,16,128]{2,1,0:T(8,128)S(1)}, f32[11,16,128]{2,1,0:T(8,128)S(1)}, u32[]{:S(2)}, u32[]{:S(2)}) collective-permute-start(f32[11,16,128]{2,1,0:T(8,128)S(1)} %pad_maximum_fusion), channel_id=1, source_target_pairs={{0,16},{16,0},{32,48},{48,32},{64,80},{80,64},{96,112},{112,96},{1... | collective-permute-start | bytes 270344 | tf_op jit(solution)/shard_map/ppermute | solution.py:539
  3.7 2.4 %collective-permute-start.1 = (f32[11,16,128]{2,1,0:T(8,128)S(1)}, f32[11,16,128]{2,1,0:T(8,128)S(1)}, u32[]{:S(2)}, u32[]{:S(2)}) collective-permute-start(f32[11,16,128]{2,1,0:T(8,128)S(1)} %pad_maximum_fusion.1), channel_id=1, source_target_pairs={{16,32},{32,16},{48,64},{64,48},{80,96},{96,80},{112,128},{128,112... | collective-permute-start | bytes 270344 | tf_op jit(solution)/shard_map/ppermute | solution.py:539
  6.2 17.0 %collective-permute-start.2 = (f32[11,6,128]{2,1,0:T(8,128)S(1)}, f32[11,6,128]{2,1,0:T(8,128)S(1)}, u32[]{:S(2)}, u32[]{:S(2)}) collective-permute-start(f32[11,6,128]{2,1,0:T(8,128)S(1)} %pad_maximum_fusion.2), channel_id=1, source_target_pairs={{0,1},{1,0},{2,3},{3,2},{4,5},{5,4},{6,7},{7,6},{8,9},{9,8},{10,11... | collective-permute-start | bytes 101384 | tf_op jit(solution)/shard_map/ppermute | solution.py:539
  9.0 6.7 %copy-start.5 = (s32[9,4,16]{2,1,0:T(4,128)S(1)}, s32[9,4,16]{2,1,0:T(4,128)}, u32[]{:S(2)}) copy-start(s32[9,4,16]{2,1,0:T(4,128)} %links.3) | copy-start | bytes 6916
  9.0 14.2 %copy-start.4 = (f32[1,4,16,128]{3,2,1,0:T(8,128)S(1)}, f32[1,4,16,128]{3,2,1,0:T(8,128)}, u32[]{:S(2)}) copy-start(f32[1,4,16,128]{3,2,1,0:T(8,128)} %stiff.1) | copy-start | bytes 98308
  9.0 14.2 %collective-permute-start.3 = (f32[11,6,128]{2,1,0:T(8,128)S(1)}, f32[11,6,128]{2,1,0:T(8,128)S(1)}, u32[]{:S(2)}, u32[]{:S(2)}) collective-permute-start(f32[11,6,128]{2,1,0:T(8,128)S(1)} %pad_maximum_fusion.3), channel_id=1, source_target_pairs={{1,2},{2,1},{3,4},{4,3},{5,6},{6,5},{7,8},{8,7},{9,10},{10,9},{11,... | collective-permute-start | bytes 101384 | tf_op jit(solution)/shard_map/ppermute | solution.py:539
  23.2 17.3 %copy-start.3 = (s32[4,4,16,128]{3,2,1,0:T(8,128)S(1)}, s32[4,4,16,128]{3,2,1,0:T(8,128)}, u32[]{:S(2)}) copy-start(s32[4,4,16,128]{3,2,1,0:T(8,128)} %corners.1) | copy-start | bytes 393220
  27.4 21.3 %all-to-all-start = ((f32[32,1,128]{2,1,0:T(1,128)}), f32[32,1,128]{2,1,0:T(1,128)S(1)}, u32[]{:S(2)}, u32[]{:S(2)}) async-start(f32[32,1,128]{2,1,0:T(1,128)} %bitcast.13), calls=%async_computation | async-start | bytes 32768 | tf_op jit(solution)/shard_map/all_to_all | solution.py:568
  45.2 17.4 %collective-permute-start.5 = (f32[3,18,128]{2,1,0:T(8,128)S(1)}, f32[3,18,128]{2,1,0:T(8,128)S(1)}, u32[]{:S(2)}, u32[]{:S(2)}) collective-permute-start(f32[3,18,128]{2,1,0:T(8,128)S(1)} %get-tuple-element.86), channel_id=1, source_target_pairs={{16,32},{32,16},{48,64},{64,48},{80,96},{96,80},{112,128},{128,112... | collective-permute-start | bytes 82952 | tf_op jit(solution)/shard_map/ppermute | solution.py:539
  48.7 14.0 %collective-permute-start.4 = (f32[3,18,128]{2,1,0:T(8,128)S(1)}, f32[3,18,128]{2,1,0:T(8,128)S(1)}, u32[]{:S(2)}, u32[]{:S(2)}) collective-permute-start(f32[3,18,128]{2,1,0:T(8,128)S(1)} %get-tuple-element.85), channel_id=1, source_target_pairs={{0,16},{16,0},{32,48},{48,32},{64,80},{80,64},{96,112},{112,96},{1... | collective-permute-start | bytes 82952 | tf_op jit(solution)/shard_map/ppermute | solution.py:539
  51.6 19.0 %all-to-all-start.1 = ((f32[16,1,128]{2,1,0:T(1,128)}), f32[16,1,128]{2,1,0:T(1,128)S(1)}, u32[]{:S(2)}, u32[]{:S(2)}) async-start(f32[16,1,128]{2,1,0:T(1,128)} %broadcast_in_dim.2), calls=%async_computation.1 | async-start | bytes 16384 | tf_op jit(solution)/shard_map/all_to_all | solution.py:573
  62.8 7.7 %collective-permute-start.6 = (f32[3,4,128]{2,1,0:T(4,128)S(1)}, f32[3,4,128]{2,1,0:T(4,128)S(1)}, u32[]{:S(2)}, u32[]{:S(2)}) collective-permute-start(f32[3,4,128]{2,1,0:T(4,128)S(1)} %get-tuple-element.115), channel_id=1, source_target_pairs={{0,1},{1,0},{2,3},{3,2},{4,5},{5,4},{6,7},{7,6},{8,9},{9,8},{10,11... | collective-permute-start | bytes 18440 | tf_op jit(solution)/shard_map/ppermute | solution.py:539
  65.6 8.5 %collective-permute-start.7 = (f32[3,4,128]{2,1,0:T(4,128)S(1)}, f32[3,4,128]{2,1,0:T(4,128)S(1)}, u32[]{:S(2)}, u32[]{:S(2)}) collective-permute-start(f32[3,4,128]{2,1,0:T(4,128)S(1)} %get-tuple-element.114), channel_id=1, source_target_pairs={{1,2},{2,1},{3,4},{4,3},{5,6},{6,5},{7,8},{8,7},{9,10},{10,9},{11,... | collective-permute-start | bytes 18440 | tf_op jit(solution)/shard_map/ppermute | solution.py:539
